TPU v7x, 512 devices: a whole 4x8x8 slice. The times are simulated.
512 devices in a mesh: gx: 8 (over y), gy: 8 (over z_hi, core), gz: 8 (over x, z_lo).
Axes of the slice: x: 4, y: 8, z: 8 (z_hi: 4, z_lo: 2; z = z_hi * 2 + z_lo), core: 2. Of those that a mesh axis runs over, the one named last changes fastest.
Arguments:
- features: bfloat16 [8, 8, 8, 32, 49, 128], P('gx', 'gy', 'gz'), may hold values from -6 to 6
- border_atoms: int32 [8, 8, 8, 4], P('gx', 'gy', 'gz'), may hold values from 0 to 31, as said below
- inner_source: int32 [8, 8, 8, 128], P('gx', 'gy', 'gz'), may hold values from 0 to 31
- inner_target: int32 [8, 8, 8, 128], P('gx', 'gy', 'gz'), may hold values from 0 to 31
- inner_rotation: int32 [8, 8, 8, 128], P('gx', 'gy', 'gz'), may hold values from 0 to 255
- inner_count: int32 [8, 8, 8], P('gx', 'gy', 'gz'), may hold values from 64 to 128, as said below
- cross_source: int32 [8, 8, 8, 128], P('gx', 'gy', 'gz'), may hold values from 0 to 107, as said below
- cross_target: int32 [8, 8, 8, 128], P('gx', 'gy', 'gz'), may hold values from 0 to 31
- cross_rotation: int32 [8, 8, 8, 2, 128], P('gx', 'gy', 'gz'), may hold values from 0 to 255
- cross_count: int32 [8, 8, 8], P('gx', 'gy', 'gz'), may hold values from 64 to 128, as said below
- rotations: bfloat16 [49, 49, 256], replicated, as said below
- order_zero: bfloat16 [896, 896], P(('gy', 'gz')), may hold values from -0.1875 to 0.1875
- order_one: bfloat16 [2, 768, 768], P(None, ('gy', 'gz')), may hold values from -0.15625 to 0.15625
- order_two: bfloat16 [2, 640, 640], P(None, ('gy', 'gz')), may hold values from -0.15625 to 0.15625
Outputs:
- updated: bfloat16 [8, 8, 8, 32, 49, 128], P('gx', 'gy', 'gz')
Inputs may be any that keep to these rules, and one draw needn't show every extreme that they name: `border_atoms`: 4 different atoms of the cell. `inner_count`: edges at positions below the count are live; some cell has all 128 live. `cross_count`: edges at positions below the count are live; some cell has all 128 live. `cross_source`: a row s * 4 + t of around with s never 13, the cell itself. An entry rotations[i, j, r] is zero unless i and j have the same degree.
All inputs are finite; a program needn't handle non-finite values.
Results may differ from a plain program's by a relative error of at most 0.006.
Values may be sent and summed in bfloat16 or wider, within the bound.
No kernel may reach another device: no remote copies, remote signals or barrier semaphores. Data moves between devices by JAX's collectives and lax.ppermute only.
A program may use at most 128 MiB of HBM per device.

v0:
```python
import math

import jax
import jax.numpy as jnp
import numpy as np
from jax import lax
from jax.sharding import PartitionSpec as P

LMAX = 6


def extended(block, sides, width):
    for axis, dim in sides:
        count = lax.axis_size(axis)
        forward = [(i, i + 1) for i in range(count - 1)]
        forward.append((count - 1, 0))
        backward = [(target, source) for source, target in forward]
        low = lax.ppermute(
            lax.slice_in_dim(block, block.shape[dim] - width, None, axis=dim), axis, forward
        )
        high = lax.ppermute(lax.slice_in_dim(block, 0, width, axis=dim), axis, backward)
        block = jnp.concatenate([low, block, high], axis=dim)
    return block


def kept_rows(top_degree):
    listing = [d * d + d for d in range(top_degree + 1)]
    for shift in (1, -1, 2, -2):
        listing = listing + [d * d + d + shift for d in range(abs(shift), top_degree + 1)]
    return np.array(listing, dtype=np.int32)


def conv_messages(sources, chosen, full_zero, full_one, full_two):
    row_total = sources.shape[0]
    channels = sources.shape[2]
    size_zero = LMAX + 1
    size_one = LMAX
    size_two = LMAX - 1
    turned = jnp.einsum("nrj,njc->nrc", chosen, sources, preferred_element_type=jnp.float32).astype(
        jnp.bfloat16
    )
    zero_part = turned[:, :size_zero].reshape(row_total, size_zero * channels)
    plus_one = turned[:, size_zero : size_zero + size_one].reshape(row_total, size_one * channels)
    minus_one = turned[:, size_zero + size_one : size_zero + 2 * size_one].reshape(
        row_total, size_one * channels
    )
    two_start = size_zero + 2 * size_one
    plus_two = turned[:, two_start : two_start + size_two].reshape(row_total, size_two * channels)
    minus_two = turned[:, two_start + size_two : two_start + 2 * size_two].reshape(
        row_total, size_two * channels
    )
    out_zero = jnp.dot(zero_part, full_zero, preferred_element_type=jnp.float32)
    out_plus1 = jnp.dot(plus_one, full_one[0], preferred_element_type=jnp.float32) - jnp.dot(
        minus_one, full_one[1], preferred_element_type=jnp.float32
    )
    out_minus1 = jnp.dot(minus_one, full_one[0], preferred_element_type=jnp.float32) + jnp.dot(
        plus_one, full_one[1], preferred_element_type=jnp.float32
    )
    out_plus2 = jnp.dot(plus_two, full_two[0], preferred_element_type=jnp.float32) - jnp.dot(
        minus_two, full_two[1], preferred_element_type=jnp.float32
    )
    out_minus2 = jnp.dot(minus_two, full_two[0], preferred_element_type=jnp.float32) + jnp.dot(
        plus_two, full_two[1], preferred_element_type=jnp.float32
    )
    pieces = [out_zero, out_plus1, out_minus1, out_plus2, out_minus2]
    mixed = jnp.concatenate(
        [piece.reshape(row_total, -1, channels) for piece in pieces], axis=1
    ).astype(jnp.bfloat16)
    return jnp.einsum("nrj,nrc->njc", chosen, mixed, preferred_element_type=jnp.float32)


def collect(total, source_table, sources, targets, picked, live, trimmed, weights):
    edge_total = sources.shape[0]
    block_size = math.gcd(128, edge_total)

    def advance(running, position):
        first_edge = position * block_size
        live_mask = (first_edge + jnp.arange(block_size, dtype=jnp.int32) < live).astype(
            jnp.float32
        )
        chosen = jnp.transpose(trimmed[:, :, picked], (2, 0, 1))
        result = conv_messages(source_table[sources], chosen, weights[0], weights[1], weights[2])
        result = result * live_mask[:, None, None]
        running = running.at[targets].add(result.reshape(block_size, -1))
        return (running, None)

    total, _ = lax.scan(advance, total, jnp.arange(edge_total // block_size, dtype=jnp.int32))
    return total


def fold_sides(padded, axis_dim):
    lower = lax.slice_in_dim(padded, 0, 1, axis=axis_dim)
    middle = lax.slice_in_dim(padded, 2, 3, axis=axis_dim)
    upper = lax.slice_in_dim(padded, 4, 5, axis=axis_dim)
    return lower + middle + upper


def fold_x(partial_value):
    padded = extended(partial_value.astype(jnp.bfloat16), (("gx", 0),), 1).astype(
        partial_value.dtype
    )
    return fold_sides(padded, 0)


def fold_y(partial_value):
    padded = extended(partial_value.astype(jnp.bfloat16), (("gy", 1),), 1).astype(
        partial_value.dtype
    )
    return fold_sides(padded, 1)


def fold_z(partial_value):
    padded = extended(partial_value.astype(jnp.bfloat16), (("gz", 2),), 1).astype(
        partial_value.dtype
    )
    return fold_sides(padded, 2)


def shards(
    features,
    border_atoms,
    inner_source,
    inner_target,
    inner_rotation,
    inner_count,
    cross_source,
    cross_target,
    cross_rotation,
    cross_count,
    rotations,
    order_zero,
    order_one,
    order_two,
):
    full_zero, full_one, full_two = (
        lax.all_gather(order_zero, ("gy", "gz"), axis=0, tiled=True),
        lax.all_gather(order_one, ("gy", "gz"), axis=1, tiled=True),
        lax.all_gather(order_two, ("gy", "gz"), axis=1, tiled=True),
    )
    weights = (full_zero, full_one, full_two)
    local_atoms = features[0, 0, 0]
    atom_total = local_atoms.shape[0]
    harmonics = local_atoms.shape[1]
    channels = local_atoms.shape[2]
    border_rows = border_atoms[0, 0, 0]
    border_total = border_rows.shape[0]
    border = local_atoms[border_rows].reshape(1, 1, 1, border_total, harmonics, channels)
    beside_all = extended(border, (("gx", 0), ("gy", 1), ("gz", 2)), 1)
    beside_all = beside_all.reshape(27 * border_total, harmonics, channels)
    trimmed = rotations[jnp.asarray(kept_rows(LMAX)), :, :]
    gathered = jnp.zeros((atom_total, harmonics * channels), jnp.float32)
    gathered = collect(
        gathered,
        local_atoms,
        inner_source[0, 0, 0],
        inner_target[0, 0, 0],
        inner_rotation[0, 0, 0],
        inner_count[0, 0, 0],
        trimmed,
        weights,
    )
    gathered = collect(
        gathered,
        beside_all,
        cross_source[0, 0, 0],
        cross_target[0, 0, 0],
        cross_rotation[0, 0, 0, 0],
        cross_count[0, 0, 0],
        trimmed,
        weights,
    )
    returned = jnp.zeros((27 * border_total, harmonics * channels), jnp.float32)
    returned = collect(
        returned,
        local_atoms,
        cross_target[0, 0, 0],
        cross_source[0, 0, 0],
        cross_rotation[0, 0, 0, 1],
        cross_count[0, 0, 0],
        trimmed,
        weights,
    )
    returned = returned.reshape(3, 3, 3, border_total, harmonics * channels)
    returned = fold_z(fold_y(fold_x(returned)))
    gathered = gathered.at[border_rows].add(returned.reshape(border_total, -1))
    updated = local_atoms.astype(jnp.float32) + 0.25 * gathered.reshape(
        atom_total, harmonics, channels
    )
    return updated.astype(jnp.bfloat16).reshape(features.shape)


def solution(mesh):
    in_specs = (
        P("gx", "gy", "gz", None, None, None),
        P("gx", "gy", "gz", None),
        P("gx", "gy", "gz", None),
        P("gx", "gy", "gz", None),
        P("gx", "gy", "gz", None),
        P("gx", "gy", "gz"),
        P("gx", "gy", "gz", None),
        P("gx", "gy", "gz", None),
        P("gx", "gy", "gz", None, None),
        P("gx", "gy", "gz"),
        P(),
        P(("gy", "gz"), None),
        P(None, ("gy", "gz"), None),
        P(None, ("gy", "gz"), None),
    )
    out_specs = P("gx", "gy", "gz", None, None, None)
    return jax.shard_map(shards, mesh=mesh, in_specs=in_specs, out_specs=out_specs, check_vma=False)
```

profile of v0, /device:TPU:129, one launch (start us, length us, event | category | flops | bytes accessed | tf_op | source)
XLA Modules:
  0.0 741.7 jit_solution(9208425399380260902)
XLA Ops:
  11.1 5.1 collective-permute-start.1
  21.5 4.1 copy.200
  30.1 2.5 convolution_convert_fusion
  43.1 2.9 collective-permute-start.3
  45.9 6.9 collective-permute-start.2
  57.1 6.1 collective-permute-start.5
  63.2 2.4 collective-permute-start.4
  79.2 7.2 collective-permute-done.4
  95.7 105.9 %all-gather.9.cloned.1.call-done = bf16[64,14,896]{2,1,0:T(8,128)(2,1)} async-done(((bf16[1,14,896]{2,1,0:T(8,128)(2,1)}), bf16[64,14,896]{2,1,0:T(8,128)(2,1)}) %all-gather.9.cloned.1.call-update) | async-done | bytes 1605648 | tf_op jit(solution)/shard_map/all_gather | solution.py:136
  201.6 3.7 reshape.612
  205.3 2.9 copy.203
  212.2 184.6 %all-gather.7.cloned.1.call-done = bf16[2,640,640]{2,0,1:T(2,128)(2,1)} async-done(((bf16[2,10,640]{2,0,1:T(2,128)(2,1)}), bf16[2,640,640]{2,0,1:T(2,128)(2,1)}) %all-gather.7.cloned.1.call-update) | async-done | bytes 1638416 | tf_op jit(solution)/shard_map/all_gather | solution.py:138
  396.7 4.8 fusion.53
  411.9 177.2 %all-gather.5.cloned.1.call-done = bf16[2,768,768]{2,0,1:T(2,128)(2,1)} async-done(((bf16[2,12,768]{2,0,1:T(2,128)(2,1)}), bf16[2,768,768]{2,0,1:T(2,128)(2,1)}) %all-gather.5.cloned.1.call-update) | async-done | bytes 2359312 | tf_op jit(solution)/shard_map/all_gather | solution.py:137
  589.1 6.4 fusion.52
  606.6 4.6 convolution_multiply_fusion
  611.2 4.7 copy.260
  615.9 4.9 copy.261
  620.8 7.5 %scatter_custom_fusion.2 = f32[108,6272]{1,0:T(8,128)} fusion(s32[128]{0:T(128)S(1)} %fusion.50, f32[128,6272]{1,0:T(8,128)} %copy.261, f32[]{:T(128)} %constant.37.clone.1), kind=kCustom, calls=%fused_computation.19 | custom fusion | flops 802816 | bytes 2710016 | tf_op jit(solution)/shard_map/while/body/eval_jaxpr/scatter-add | solution.py:84
  632.3 3.5 convert_element_type.88
  650.7 4.6 collective-permute-start.7
  661.8 4.4 convolution_multiply_fusion.1
  667.9 11.9 %collective-permute-start.8 = (bf16[1,1,3,4,6272]{4,3,2,1,0:T(4,128)(2,1)S(1)}, bf16[1,1,3,4,6272]{4,3,2,1,0:T(4,128)(2,1)S(1)}, u32[]{:S(2)}, u32[]{:S(2)}) collective-permute-start(bf16[1,1,3,4,6272]{4,3,2,1,0:T(4,128)(2,1)S(1)} %get-tuple-element.98), channel_id=1, source_target_pairs={{0,8},{8,16},{16,24},{24,32},{32,40},{40,48},{48,56},{56,0},{1,9},... | collective-permute-start | bytes 451592 | tf_op jit(solution)/shard_map/ppermute | solution.py:18
  682.4 7.7 %collective-permute-done.9 = bf16[1,1,3,4,6272]{4,3,2,1,0:T(4,128)(2,1)S(1)} collective-permute-done((bf16[1,1,3,4,6272]{4,3,2,1,0:T(4,128)(2,1)S(1)}, bf16[1,1,3,4,6272]{4,3,2,1,0:T(4,128)(2,1)S(1)}, u32[]{:S(2)}, u32[]{:S(2)}) %collective-permute-start.9) | collective-permute-done | bytes 150560 | tf_op jit(solution)/shard_map/ppermute | solution.py:21
  692.3 5.5 collective-permute-start.11
  697.8 3.2 convolution_multiply_fusion.2
  701.0 4.5 copy.222
  705.5 4.9 copy.223
  710.3 4.5 copy.242
  714.8 4.9 copy.243
  719.7 6.0 scatter_custom_fusion
  725.7 6.3 scatter_fusion
  (223 shorter events, 110.1 us)
Async XLA Ops:
  6.5 14.4 %copy-start = (bf16[49,49,256]{2,1,0:T(8,128)(2,1)S(1)}, bf16[49,49,256]{2,1,0:T(8,128)(2,1)}, u32[]{:S(2)}) copy-start(bf16[49,49,256]{2,1,0:T(8,128)(2,1)} %param.25) | copy-start | bytes 3687940
  6.5 195.1 %all-gather.9.cloned.1.call-start = ((), (), s32[]{:S(2)}) async-start(), calls=%async_computation.2 | async-start | bytes 1863680 | tf_op jit(solution)/shard_map/all_gather | solution.py:136
  7.3 389.5 %all-gather.7.cloned.1.call-start = ((), (), s32[]{:S(2)}) async-start(), calls=%async_computation.1 | async-start | bytes 1664000 | tf_op jit(solution)/shard_map/all_gather | solution.py:138
  8.0 581.1 %all-gather.5.cloned.1.call-start = ((), (), s32[]{:S(2)}) async-start(), calls=%async_computation | async-start | bytes 2396160 | tf_op jit(solution)/shard_map/all_gather | solution.py:137
  11.1 31.9 %collective-permute-start.1 = (bf16[1,1,1,4,49,128]{5,4,3,2,1,0:T(8,128)(2,1)S(1)}, bf16[1,1,1,4,49,128]{5,4,3,2,1,0:T(8,128)(2,1)S(1)}, u32[]{:S(2)}, u32[]{:S(2)}) collective-permute-start(bf16[1,1,1,4,49,128]{5,4,3,2,1,0:T(8,128)(2,1)S(1)} %bitcast.192), channel_id=1, source_target_pairs={{64,0},{128,64},{192,128},{256,192},{320,256},{384,320},{448,384},... | collective-permute-start | bytes 150536 | tf_op jit(solution)/shard_map/ppermute | solution.py:21
  16.2 26.8 %collective-permute-start = (bf16[1,1,1,4,49,128]{5,4,3,2,1,0:T(8,128)(2,1)S(1)}, bf16[1,1,1,4,49,128]{5,4,3,2,1,0:T(8,128)(2,1)S(1)}, u32[]{:S(2)}, u32[]{:S(2)}) collective-permute-start(bf16[1,1,1,4,49,128]{5,4,3,2,1,0:T(8,128)(2,1)S(1)} %bitcast.193), channel_id=1, source_target_pairs={{0,64},{64,128},{128,192},{192,256},{256,320},{320,384},{384,448},... | collective-permute-start | bytes 150536 | tf_op jit(solution)/shard_map/ppermute | solution.py:18
  41.0 24.7 %copy-start.9 = (bf16[128,29,128]{2,1,0:T(8,128)(2,1)}, bf16[128,29,128]{2,1,0:T(8,128)(2,1)S(1)}, u32[]{:S(2)}) copy-start(bf16[128,29,128]{2,1,0:T(8,128)(2,1)S(1)} %convolution_convert_fusion.2) | copy-start | bytes 2850820
  41.1 11.8 %copy-start.35 = (s32[1,1,1,128]{3,2,1,0:T(1,128)S(1)}, s32[1,1,1,128]{3,2,1,0:T(1,128)}, u32[]{:S(2)}) copy-start(s32[1,1,1,128]{3,2,1,0:T(1,128)} %param.21) | copy-start | bytes 1540
  43.0 22.6 %copy-start.33 = (bf16[1,1,1,4,49,128]{5,4,3,2,1,0:T(8,128)(2,1)}, bf16[1,1,1,4,49,128]{5,4,3,2,1,0:T(8,128)(2,1)S(1)}, u32[]{:S(2)}) copy-start(bf16[1,1,1,4,49,128]{5,4,3,2,1,0:T(8,128)(2,1)S(1)} %collective-permute-done.1) | copy-start | bytes 150532
  43.0 22.6 %copy-start.34 = (bf16[1,1,1,4,49,128]{5,4,3,2,1,0:T(8,128)(2,1)}, bf16[1,1,1,4,49,128]{5,4,3,2,1,0:T(8,128)(2,1)S(1)}, u32[]{:S(2)}) copy-start(bf16[1,1,1,4,49,128]{5,4,3,2,1,0:T(8,128)(2,1)S(1)} %collective-permute-done) | copy-start | bytes 150532
  43.1 12.0 %collective-permute-start.3 = (bf16[3,1,1,4,49,128]{5,4,3,2,1,0:T(8,128)(2,1)S(1)}, bf16[3,1,1,4,49,128]{5,4,3,2,1,0:T(8,128)(2,1)S(1)}, u32[]{:S(2)}, u32[]{:S(2)}) collective-permute-start(bf16[3,1,1,4,49,128]{5,4,3,2,1,0:T(8,128)(2,1)S(1)} %pad_maximum_fusion.4), channel_id=1, source_target_pairs={{8,0},{16,8},{24,16},{32,24},{40,32},{48,40},{56,48},{0,56},{9,1},... | collective-permute-start | bytes 451592 | tf_op jit(solution)/shard_map/ppermute | solution.py:21
  45.9 10.3 %collective-permute-start.2 = (bf16[3,1,1,4,49,128]{5,4,3,2,1,0:T(8,128)(2,1)S(1)}, bf16[3,1,1,4,49,128]{5,4,3,2,1,0:T(8,128)(2,1)S(1)}, u32[]{:S(2)}, u32[]{:S(2)}) collective-permute-start(bf16[3,1,1,4,49,128]{5,4,3,2,1,0:T(8,128)(2,1)S(1)} %pad_maximum_fusion.4), channel_id=1, source_target_pairs={{0,8},{8,16},{16,24},{24,32},{32,40},{40,48},{48,56},{56,0},{1,9},... | collective-permute-start | bytes 451592 | tf_op jit(solution)/shard_map/ppermute | solution.py:18
  55.1 12.0 %copy-start.27 = (bf16[3,1,1,4,49,128]{5,4,3,2,1,0:T(8,128)(2,1)}, bf16[3,1,1,4,49,128]{5,4,3,2,1,0:T(8,128)(2,1)S(1)}, u32[]{:S(2)}) copy-start(bf16[3,1,1,4,49,128]{5,4,3,2,1,0:T(8,128)(2,1)S(1)} %collective-permute-done.3) | copy-start | bytes 451588
  56.2 9.5 %copy-start.28 = (bf16[3,1,1,4,49,128]{5,4,3,2,1,0:T(8,128)(2,1)}, bf16[3,1,1,4,49,128]{5,4,3,2,1,0:T(8,128)(2,1)S(1)}, u32[]{:S(2)}) copy-start(bf16[3,1,1,4,49,128]{5,4,3,2,1,0:T(8,128)(2,1)S(1)} %collective-permute-done.2) | copy-start | bytes 451588
  57.1 22.1 %collective-permute-start.5 = (bf16[3,3,1,4,49,128]{5,4,3,2,1,0:T(8,128)(2,1)}, bf16[3,3,1,4,49,128]{5,4,3,2,1,0:T(8,128)(2,1)}, u32[]{:S(2)}, u32[]{:S(2)}) collective-permute-start(bf16[3,3,1,4,49,128]{5,4,3,2,1,0:T(8,128)(2,1)} %pad_maximum_fusion.1), channel_id=1, source_target_pairs={{1,0},{2,1},{3,2},{4,3},{5,4},{6,5},{7,6},{0,7},{9,8},{10,9},{11,1... | collective-permute-start | bytes 1354760 | tf_op jit(solution)/shard_map/ppermute | solution.py:21
  63.2 23.2 %collective-permute-start.4 = (bf16[3,3,1,4,49,128]{5,4,3,2,1,0:T(8,128)(2,1)}, bf16[3,3,1,4,49,128]{5,4,3,2,1,0:T(8,128)(2,1)}, u32[]{:S(2)}, u32[]{:S(2)}) collective-permute-start(bf16[3,3,1,4,49,128]{5,4,3,2,1,0:T(8,128)(2,1)} %pad_maximum_fusion.1), channel_id=1, source_target_pairs={{0,1},{1,2},{2,3},{3,4},{4,5},{5,6},{6,7},{7,0},{8,9},{9,10},{10,1... | collective-permute-start | bytes 1354760 | tf_op jit(solution)/shard_map/ppermute | solution.py:18
  65.7 10.3 %slice-start = ((bf16[128,29,128]{2,1,0:T(8,128)(2,1)}), bf16[128,7,128]{2,1,0:T(8,128)(2,1)S(1)}, s32[]{:S(2)}) async-start(bf16[128,29,128]{2,1,0:T(8,128)(2,1)} %copy-done.9), calls=%async_computation.3 | async-start | bytes 524288 | tf_op jit(solution)/shard_map/while/body/eval_jaxpr/slice | solution.py:42
  67.1 9.9 %copy-start.22 = (bf16[128,5,128]{2,1,0:T(8,128)(2,1)S(1)}, bf16[128,5,128]{2,1,0:T(8,128)(2,1)}, u32[]{:S(2)}) copy-start(bf16[128,5,128]{2,1,0:T(8,128)(2,1)} %get-tuple-element.94) | copy-start | bytes 491524
  69.5 20.6 %copy-start.5 = (bf16[128,29,49]{2,1,0:T(8,128)(2,1)}, bf16[128,29,49]{2,1,0:T(8,128)(2,1)S(1)}, u32[]{:S(2)}) copy-start(bf16[128,29,49]{2,1,0:T(8,128)(2,1)S(1)} %gather_fusion.3) | copy-start | bytes 1091332
  649.2 9.9 %copy-start.32 = (bf16[128,5,128]{2,0,1:T(8,128)(2,1)S(1)}, bf16[128,5,128]{2,0,1:T(8,128)(2,1)}, u32[]{:S(2)}) copy-start(bf16[128,5,128]{2,0,1:T(8,128)(2,1)} %copy.239) | copy-start | bytes 491524
  650.4 10.7 %copy-start.30 = (bf16[128,5,128]{2,0,1:T(8,128)(2,1)S(1)}, bf16[128,5,128]{2,0,1:T(8,128)(2,1)}, u32[]{:S(2)}) copy-start(bf16[128,5,128]{2,0,1:T(8,128)(2,1)} %copy.240) | copy-start | bytes 491524
  650.4 11.4 %copy-start.6 = (bf16[128,29,49]{2,1,0:T(8,128)(2,1)S(1)}, bf16[128,29,49]{2,1,0:T(8,128)(2,1)}, u32[]{:S(2)}) copy-start(bf16[128,29,49]{2,1,0:T(8,128)(2,1)} %copy-done.5) | copy-start | bytes 1091332
  650.7 15.4 %collective-permute-start.7 = (bf16[1,3,3,4,6272]{4,3,2,1,0:T(4,128)(2,1)S(1)}, bf16[1,3,3,4,6272]{4,3,2,1,0:T(4,128)(2,1)S(1)}, u32[]{:S(2)}, u32[]{:S(2)}) collective-permute-start(bf16[1,3,3,4,6272]{4,3,2,1,0:T(4,128)(2,1)S(1)} %slice.185), channel_id=1, source_target_pairs={{64,0},{128,64},{192,128},{256,192},{320,256},{384,320},{448,384},... | collective-permute-start | bytes 1354760 | tf_op jit(solution)/shard_map/ppermute | solution.py:21
  655.3 11.6 %collective-permute-start.6 = (bf16[1,3,3,4,6272]{4,3,2,1,0:T(4,128)(2,1)}, bf16[1,3,3,4,6272]{4,3,2,1,0:T(4,128)(2,1)S(1)}, u32[]{:S(2)}, u32[]{:S(2)}) collective-permute-start(bf16[1,3,3,4,6272]{4,3,2,1,0:T(4,128)(2,1)} %slice.183), channel_id=1, source_target_pairs={{0,64},{64,128},{128,192},{192,256},{256,320},{320,384},{384,448},... | collective-permute-start | bytes 1354760 | tf_op jit(solution)/shard_map/ppermute | solution.py:18
  666.2 15.6 %copy-start.14 = (bf16[128,29,128]{2,0,1:T(8,128)(2,1)S(1)}, bf16[128,29,128]{2,0,1:T(8,128)(2,1)}, u32[]{:S(2)}) copy-start(bf16[128,29,128]{2,0,1:T(8,128)(2,1)} %constant_dynamic-update-slice_fusion.2) | copy-start | bytes 2850820
  666.2 15.7 %copy-start.31 = (bf16[128,5,128]{2,0,1:T(8,128)(2,1)S(1)}, bf16[128,5,128]{2,0,1:T(8,128)(2,1)}, u32[]{:S(2)}) copy-start(bf16[128,5,128]{2,0,1:T(8,128)(2,1)} %copy.219) | copy-start | bytes 491524
  666.2 15.7 %copy-start.29 = (bf16[128,5,128]{2,0,1:T(8,128)(2,1)S(1)}, bf16[128,5,128]{2,0,1:T(8,128)(2,1)}, u32[]{:S(2)}) copy-start(bf16[128,5,128]{2,0,1:T(8,128)(2,1)} %copy.220) | copy-start | bytes 491524
  667.8 30.0 %copy-start.4 = (bf16[128,29,49]{2,1,0:T(8,128)(2,1)S(1)}, bf16[128,29,49]{2,1,0:T(8,128)(2,1)}, u32[]{:S(2)}) copy-start(bf16[128,29,49]{2,1,0:T(8,128)(2,1)} %copy-done.3) | copy-start | bytes 1091332
  667.9 14.4 %collective-permute-start.8 = (bf16[1,1,3,4,6272]{4,3,2,1,0:T(4,128)(2,1)S(1)}, bf16[1,1,3,4,6272]{4,3,2,1,0:T(4,128)(2,1)S(1)}, u32[]{:S(2)}, u32[]{:S(2)}) collective-permute-start(bf16[1,1,3,4,6272]{4,3,2,1,0:T(4,128)(2,1)S(1)} %get-tuple-element.98), channel_id=1, source_target_pairs={{0,8},{8,16},{16,24},{24,32},{32,40},{40,48},{48,56},{56,0},{1,9},... | collective-permute-start | bytes 451592 | tf_op jit(solution)/shard_map/ppermute | solution.py:18
  679.9 10.2 %collective-permute-start.9 = (bf16[1,1,3,4,6272]{4,3,2,1,0:T(4,128)(2,1)S(1)}, bf16[1,1,3,4,6272]{4,3,2,1,0:T(4,128)(2,1)S(1)}, u32[]{:S(2)}, u32[]{:S(2)}) collective-permute-start(bf16[1,1,3,4,6272]{4,3,2,1,0:T(4,128)(2,1)S(1)} %get-tuple-element.110), channel_id=1, source_target_pairs={{8,0},{16,8},{24,16},{32,24},{40,32},{48,40},{56,48},{0,56},{9,1},... | collective-permute-start | bytes 451592 | tf_op jit(solution)/shard_map/ppermute | solution.py:21
  690.4 41.5 %collective-permute-start.10 = (bf16[1,1,1,4,6272]{4,3,2,1,0:T(4,128)(2,1)S(1)}, bf16[1,1,1,4,6272]{4,3,2,1,0:T(4,128)(2,1)S(1)}, u32[]{:S(2)}, u32[]{:S(2)}) collective-permute-start(bf16[1,1,1,4,6272]{4,3,2,1,0:T(4,128)(2,1)S(1)} %get-tuple-element.111), channel_id=1, source_target_pairs={{0,1},{1,2},{2,3},{3,4},{4,5},{5,6},{6,7},{7,0},{8,9},{9,10},{10,1... | collective-permute-start | bytes 150536 | tf_op jit(solution)/shard_map/ppermute | solution.py:18
  692.3 39.6 %collective-permute-start.11 = (bf16[1,1,1,4,6272]{4,3,2,1,0:T(4,128)(2,1)S(1)}, bf16[1,1,1,4,6272]{4,3,2,1,0:T(4,128)(2,1)S(1)}, u32[]{:S(2)}, u32[]{:S(2)}) collective-permute-start(bf16[1,1,1,4,6272]{4,3,2,1,0:T(4,128)(2,1)S(1)} %get-tuple-element.112), channel_id=1, source_target_pairs={{1,0},{2,1},{3,2},{4,3},{5,4},{6,5},{7,6},{0,7},{9,8},{10,9},{11,1... | collective-permute-start | bytes 150536 | tf_op jit(solution)/shard_map/ppermute | solution.py:21
  (21 other events, 65.0 us)
Sparse Core Ops, SparseCore 0:
  9.5 192.0 all-gather.8
  203.7 193.0 all-gather.6
  398.9 190.2 all-gather.4
where the time goes:
time: 748 us; the launch traced here: 742 us
  waiting for transfers between devices  489 us (65%)
  local copies, waits for them, and re-layouts  116 us (16%)
  starting transfers between devices  53.6 us (7%)
  matrix products  36.7 us (5%)
  other arithmetic  31.6 us (4%)
  between operations  15.5 us (2%)
    all_gather x1, waiting for transfers between devices, shards(): lax.all_gather(order_two, ('gy', 'gz'), axis=1, tiled=True)  185 us
    all_gather x1, waiting for transfers between devices, shards(): lax.all_gather(order_one, ('gy', 'gz'), axis=1, tiled=True)  177 us
    all_gather x1, waiting for transfers between devices, shards(): lax.all_gather(order_zero, ('gy', 'gz'), axis=0, tiled=True)  106 us
    ppermute x6, starting transfers between devices, extended(): lax.ppermute(lax.slice_in_dim(block, block.shape[dim] - width, None, axis...  27.5 us
    ppermute x6, starting transfers between devices, extended(): lax.ppermute(lax.slice_in_dim(block, 0, width, axis=dim), axis, backward)  26 us
    scatter-add x3, other arithmetic, advance(): running = running.at[targets].add(result.reshape(block_size, -1))  19.8 us
  transfers between devices with their start and end apart: 15, of which 9 were waited for; matrix products, arithmetic and copies ran while one was open for 16% of the time, Pallas kernels for 0%

commit v1 on v0

v1 whole, which is shorter than its diff:
```python
import functools

import jax
import jax.numpy as jnp
import numpy as np
from jax import lax
from jax.experimental import pallas as pl
from jax.experimental.pallas import tpu as pltpu
from jax.sharding import Mesh
from jax.sharding import PartitionSpec as P

LMAX = 6
HARM = (LMAX + 1) ** 2
JP = 56
KEPT = 29
KP = 32
EDGES = 128
ROTS = 256
ATOMS = 32
BOUND = 4
AROUND = 27 * BOUND
STEP = 32
PITCH = EDGES + 1
LANES = 128
BF16 = jnp.bfloat16
F32 = jnp.float32

SMEM = pl.BlockSpec(memory_space=pltpu.SMEM)
VMEM = pl.BlockSpec(memory_space=pltpu.VMEM)
HBM = pl.BlockSpec(memory_space=pl.ANY)
PARAMS = pltpu.CompilerParams(vmem_limit_bytes=56 * 2**20)

ROWS0, BLK0 = 16, 7
ROWS1, BLK1 = 24, 6
ROWS2, BLK2 = 24, 5
G0 = 4 * ROWS0 * BLK0
G1 = 4 * ROWS1 * BLK1
G2 = 4 * ROWS2 * BLK2
GROWS = G0 + G1 + G2


def kept_rows():
    listing = [d * d + d for d in range(LMAX + 1)]
    for shift in (1, -1, 2, -2):
        listing += [d * d + d + shift for d in range(abs(shift), LMAX + 1)]
    return listing


def slot_order():
    order = []
    for zh in range(4):
        for zl in range(2):
            for core in range(2):
                for x in range(4):
                    order.append(((zh * 2 + core) * 4 + x) * 2 + zl)
    return order


def spreads():
    order = slot_order()
    zero = np.zeros((2, 512, 512), np.float32)
    one = np.zeros((768, 768), np.float32)
    two = np.zeros((2, 768, 768), np.float32)
    for slot, shard in enumerate(order):
        half, local = divmod(slot, 32)
        for r in range(14):
            zero[half, shard * 14 + r - 384 * half, local * ROWS0 + r] = 1
        for r in range(12):
            if half == 0:
                one[shard * 12 + r, local * ROWS1 + r] = 1
                one[384 + shard * 12 + r, local * ROWS1 + 12 + r] = 1
        for r in range(10):
            two[half, shard * 10 + r - 256 * half, local * ROWS2 + r] = 1
            two[half, 384 + shard * 10 + r - 256 * half, local * ROWS2 + 10 + r] = 1
    return [jnp.asarray(m, BF16) for m in (zero, one, two)]


def tables_kernel(border_atoms, feats, x_out, border_out, tmp):
    for j in range(HARM):
        tmp[pl.ds(j * 33, ATOMS), :] = feats[j].astype(F32)
    tail = jnp.zeros((JP - HARM, LANES), F32)
    for a in range(ATOMS):
        rows = tmp[pl.ds(a, HARM, stride=33), :]
        x_out[a] = jnp.concatenate([rows, tail], axis=0).astype(BF16)
    for t in range(BOUND):
        border_out[t] = x_out[border_atoms[t]]


def blocks_of(count):
    return (count + (STEP - 1)) // STEP


def forward_kernel(count, sources, picked, x_ref, rot_ref, sp0, sp1, sp2, t0, t1, t2, tmp):
    def step(s, carry):
        for u in range(STEP):
            e = s * STEP + u
            rows = jnp.dot(rot_ref[picked[e]], x_ref[sources[e]], preferred_element_type=F32)
            tmp[pl.ds(e, KP, stride=PITCH), :] = rows
        return carry

    lax.fori_loop(0, blocks_of(count[0]), step, 0)

    def plane(i):
        return tmp[pl.ds(i * PITCH, EDGES), :].astype(BF16)

    def spread(planes, matrix):
        return jnp.dot(jnp.concatenate(planes, axis=1), matrix, preferred_element_type=F32).astype(BF16)

    zero = [plane(i) for i in range(7)]
    t0[:, 0:512] = spread(zero[0:4], sp0[0])
    t0[:, 512:1024] = spread(zero[3:7], sp0[1])
    plus = [plane(7 + i) for i in range(6)]
    minus = [plane(13 + i) for i in range(6)]
    for h in range(2):
        p, q = plus[3 * h : 3 * h + 3], minus[3 * h : 3 * h + 3]
        t1[0, :, 768 * h : 768 * (h + 1)] = spread(p + [-m for m in q], sp1[...])
        t1[1, :, 768 * h : 768 * (h + 1)] = spread(q + p, sp1[...])
    plus = [plane(19 + i) for i in range(5)]
    minus = [plane(24 + i) for i in range(5)]
    for h in range(2):
        p, q = plus[2 * h : 2 * h + 3], minus[2 * h : 2 * h + 3]
        t2[0, :, 768 * h : 768 * (h + 1)] = spread(p + [-m for m in q], sp2[h])
        t2[1, :, 768 * h : 768 * (h + 1)] = spread(q + p, sp2[h])


def forward(count, sources, picked, x, table, sp):
    return pl.pallas_call(
        forward_kernel,
        out_shape=(
            jax.ShapeDtypeStruct((EDGES, 1024), BF16),
            jax.ShapeDtypeStruct((2, EDGES, 1536), BF16),
            jax.ShapeDtypeStruct((2, EDGES, 1536), BF16),
        ),
        in_specs=[SMEM, SMEM, SMEM, VMEM, VMEM, VMEM, VMEM, VMEM],
        out_specs=(VMEM, VMEM, VMEM),
        scratch_shapes=[pltpu.VMEM((KP * PITCH, LANES), F32)],
        compiler_params=PARAMS,
    )(count, sources, picked, x, table, *sp)


def back_kernel(sets, trash, finish, *refs):
    counts, picked, targets = refs[0:sets], refs[sets : 2 * sets], refs[2 * sets : 3 * sets]
    refs = refs[3 * sets :]
    turned = [refs[3 * i : 3 * i + 3] for i in range(sets)]
    rot_ref, gathered = refs[3 * sets : 3 * sets + 2]
    refs = refs[3 * sets + 2 :]
    outs, (w0, w1, w2, tmp, acc, sems) = refs[:-6], refs[-6:]
    copies = []
    start = 0
    for n, (ref, size) in enumerate(((w0, G0), (w1, G1), (w2, G2))):
        copies.append(pltpu.make_async_copy(gathered.at[:, pl.ds(start, size), :], ref, sems.at[n]))
        copies[-1].start()
        start += size
    acc[...] = jnp.zeros_like(acc)
    for i in range(sets):
        tmp[i, pl.ds(KEPT * PITCH, (KP - KEPT) * PITCH), :] = jnp.zeros(((KP - KEPT) * PITCH, LANES), F32)

    def mix(lhs, ref, rows, blocks, places):
        for b in range(0, blocks, 2):
            width = min(2, blocks - b)
            weight = [
                ref[:, (b + i) * rows : (b + i + 1) * rows, :].reshape(16 * rows, LANES) for i in range(width)
            ]
            weight = jnp.concatenate(weight, axis=1) if width == 2 else weight[0]
            result = jnp.dot(lhs, weight, preferred_element_type=F32)
            for n, (i, first) in enumerate(places):
                for w in range(width):
                    tmp[i, pl.ds((first + b + w) * PITCH, EDGES), :] = result[
                        n * EDGES : (n + 1) * EDGES, w * LANES : (w + 1) * LANES
                    ]

    copies[0].wait()
    mix(
        jnp.concatenate([turned[i][0][...] for i in range(sets)], axis=0),
        w0, 4 * ROWS0, BLK0, [(i, 0) for i in range(sets)],
    )
    for n, (ref, rows, blocks, first) in enumerate(((w1, ROWS1, BLK1, 7), (w2, ROWS2, BLK2, 19))):
        copies[n + 1].wait()
        mix(
            jnp.concatenate([turned[i][n + 1][sign] for i in range(sets) for sign in range(2)], axis=0),
            ref, 4 * rows, blocks, [(i, first + sign * blocks) for i in range(sets) for sign in range(2)],
        )

    for i in range(sets):
        count = counts[i][0]

        def step(s, carry, i=i, count=count):
            for u in range(STEP):
                e = s * STEP + u
                rows = tmp[i, pl.ds(e, KP, stride=PITCH), :].astype(BF16)
                part = lax.dot_general(
                    rot_ref[picked[i][e]], rows, (((0,), (0,)), ((), ())), preferred_element_type=F32
                )
                acc[jnp.where(e < count, targets[i][e], trash)] += part
            return carry

        lax.fori_loop(0, blocks_of(count), step, 0)
    finish(acc, *outs)


def store_returned(acc, low, middle, high):
    low[...] = acc[0:36].astype(BF16)
    middle[...] = acc[36:72]
    high[...] = acc[72:108].astype(BF16)


def store_gathered(acc, out):
    out[...] = acc[0:ATOMS]


def back(counts, picked, targets, turned, table, gathered, rows, trash, finish, out_shape):
    sets = len(counts)
    return pl.pallas_call(
        functools.partial(back_kernel, sets, trash, finish),
        out_shape=out_shape,
        in_specs=[SMEM] * (3 * sets) + [VMEM] * (3 * sets + 1) + [HBM],
        out_specs=jax.tree.map(lambda _: VMEM, out_shape),
        scratch_shapes=[
            pltpu.VMEM((16, G0, LANES), BF16),
            pltpu.VMEM((16, G1, LANES), BF16),
            pltpu.VMEM((16, G2, LANES), BF16),
            pltpu.VMEM((sets, KP * PITCH, LANES), F32),
            pltpu.VMEM((rows, JP, LANES), F32),
            pltpu.SemaphoreType.DMA((3,)),
        ],
        compiler_params=PARAMS,
    )(*counts, *picked, *targets, *[t for one in turned for t in one], table, gathered)


def final_kernel(border_atoms, feats, gathered, returned, out, acc):
    for a in range(ATOMS):
        acc[pl.ds(a * 57, JP), :] = gathered[a]
    for t in range(BOUND):
        acc[pl.ds(border_atoms[t] * 57, JP), :] += returned[t]
    for j in range(HARM):
        total = acc[pl.ds(j, ATOMS, stride=57), :]
        out[j] = (feats[j].astype(F32) + 0.25 * total).astype(BF16)


def ring(axis, block, shift):
    count = lax.axis_size(axis)
    return lax.ppermute(block, axis, [(i, (i + shift) % count) for i in range(count)])


GX, GY, GZ = "gx", ("zh", "core"), ("x", "zl")


def shards(
    features,
    border_atoms,
    inner_source,
    inner_target,
    inner_rotation,
    inner_count,
    cross_source,
    cross_target,
    cross_rotation,
    cross_count,
    rotations,
    order_zero,
    order_one,
    order_two,
):
    share0 = jnp.pad(order_zero.reshape(14, BLK0, LANES).transpose(1, 0, 2), ((0, 0), (0, 2), (0, 0)))
    share1 = order_one.reshape(2, 12, BLK1, LANES).transpose(2, 0, 1, 3).reshape(BLK1, ROWS1, LANES)
    share2 = order_two.reshape(2, 10, BLK2, LANES).transpose(2, 0, 1, 3).reshape(BLK2, 20, LANES)
    share2 = jnp.pad(share2, ((0, 0), (0, ROWS2 - 20), (0, 0)))
    share = jnp.concatenate([s.reshape(-1, LANES) for s in (share0, share1, share2)], axis=0)
    four = lax.all_gather(share, "x", axis=0, tiled=False)
    pieces = []
    start = 0
    for rows, blocks in ((ROWS0, BLK0), (ROWS1, BLK1), (ROWS2, BLK2)):
        piece = four[:, start : start + rows * blocks].reshape(4, blocks, rows, LANES)
        pieces.append(piece.transpose(1, 0, 2, 3).reshape(blocks * 4 * rows, LANES))
        start += rows * blocks
    gathered_weights = lax.all_gather(jnp.concatenate(pieces, axis=0), ("zh", "zl", "core"), axis=0, tiled=False)

    feats = features[0, 0, 0].transpose(1, 0, 2)
    border_rows = border_atoms[0, 0, 0]
    x, border = pl.pallas_call(
        tables_kernel,
        out_shape=(
            jax.ShapeDtypeStruct((ATOMS, JP, LANES), BF16),
            jax.ShapeDtypeStruct((BOUND, JP, LANES), BF16),
        ),
        in_specs=[SMEM, VMEM],
        out_specs=(VMEM, VMEM),
        scratch_shapes=[pltpu.VMEM((HARM * 33, LANES), F32)],
        compiler_params=PARAMS,
    )(border_rows, feats)

    near = border
    for axis in (GX, GY, GZ):
        low = ring(axis, near, 1)
        high = ring(axis, near, -1)
        near = jnp.concatenate([low, near, high], axis=0)
    slot, atom = cross_source[0, 0, 0] // BOUND, cross_source[0, 0, 0] % BOUND
    far_rows = (((slot % 3) * 3 + (slot // 3) % 3) * 3 + slot // 9) * BOUND + atom

    select = np.zeros((KP, HARM), np.float32)
    select[np.arange(KEPT), kept_rows()] = 1
    table = jnp.einsum("ki,ijr->rkj", jnp.asarray(select, BF16), rotations, preferred_element_type=F32)
    table = jnp.pad(table.astype(BF16), ((0, 0), (0, 0), (0, JP - HARM)))

    sp = spreads()
    count_in, count_x = inner_count.reshape(1), cross_count.reshape(1)
    source_in, target_in, rot_in = inner_source[0, 0, 0], inner_target[0, 0, 0], inner_rotation[0, 0, 0]
    source_x, target_x = cross_source[0, 0, 0], cross_target[0, 0, 0]
    rot_inward, rot_outward = cross_rotation[0, 0, 0, 0], cross_rotation[0, 0, 0, 1]
    turned_out = forward(count_x, target_x, rot_outward, x, table, sp)
    turned_in = forward(count_in, source_in, rot_in, x, table, sp)
    turned_x = forward(count_x, far_rows, rot_inward, near, table, sp)

    face = (36, JP, LANES)
    low, middle, high = back(
        [count_x], [rot_outward], [source_x], [turned_out], table, gathered_weights, 112, AROUND, store_returned,
        (jax.ShapeDtypeStruct(face, BF16), jax.ShapeDtypeStruct(face, F32), jax.ShapeDtypeStruct(face, BF16)),
    )
    returned = middle + ring(GX, low, -1).astype(F32) + ring(GX, high, 1).astype(F32)
    for axis in (GY, GZ):
        third = returned.shape[0] // 3
        low = ring(axis, returned[:third].astype(BF16), -1).astype(F32)
        high = ring(axis, returned[2 * third :].astype(BF16), 1).astype(F32)
        returned = returned[third : 2 * third] + low + high

    gathered = back(
        [count_in, count_x], [rot_in, rot_inward], [target_in, target_x], [turned_in, turned_x], table,
        gathered_weights, 40, ATOMS, store_gathered, jax.ShapeDtypeStruct((ATOMS, JP, LANES), F32),
    )

    updated = pl.pallas_call(
        final_kernel,
        out_shape=jax.ShapeDtypeStruct((HARM, ATOMS, LANES), BF16),
        in_specs=[SMEM, VMEM, VMEM, VMEM],
        out_specs=VMEM,
        scratch_shapes=[pltpu.VMEM((ATOMS * 57, LANES), F32)],
        compiler_params=PARAMS,
    )(border_rows, feats, gathered, returned)
    return updated.transpose(1, 0, 2).reshape(features.shape)


def solution(mesh):
    fine = Mesh(mesh.devices.reshape(8, 4, 2, 4, 2), ("gx", "zh", "core", "x", "zl"))
    cell = ("gx", GY, GZ)
    plane = GY + GZ
    in_specs = (
        P(*cell, None, None, None),
        P(*cell, None),
        P(*cell, None),
        P(*cell, None),
        P(*cell, None),
        P(*cell),
        P(*cell, None),
        P(*cell, None),
        P(*cell, None, None),
        P(*cell),
        P(),
        P(plane, None),
        P(None, plane, None),
        P(None, plane, None),
    )
    out_specs = P(*cell, None, None, None)
    return jax.shard_map(shards, mesh=fine, in_specs=in_specs, out_specs=out_specs, check_vma=False)
```

time: 748 us -> 174 us (0.23)
  the two profiles are of different devices: /device:TPU:129 before, /device:TPU:24 now
where the time goes in v1:
time: 174 us; the launch traced here: 173 us
  starting transfers between devices  47 us (27%)
  Pallas kernels  44.9 us (26%)
  waiting for transfers between devices  31.7 us (18%)
  local copies, waits for them, and re-layouts  17.6 us (10%)
  between operations  15.2 us (9%)
  blocking collectives  12.9 us (7%)
  other arithmetic  2.31 us (1%)
    ppermute x12, starting transfers between devices, ring(): lax.ppermute(block, axis, [(i, (i + shift) % count) for i in range(count)])  47 us
    pallas_call x2, Pallas kernels, back(): pl.pallas_call(functools.partial(back_kernel, sets, trash, finish), out_s...  20.9 us
    pallas_call x3, Pallas kernels, forward(): pl.pallas_call(forward_kernel, out_shape=(jax.ShapeDtypeStruct((EDGES, 10...  19.8 us
    ppermute x12, waiting for transfers between devices, ring(): lax.ppermute(block, axis, [(i, (i + shift) % count) for i in range(count)])  18.4 us
    all_gather x1, waiting for transfers between devices, shards(): lax.all_gather(jnp.concatenate(pieces, axis=0), ('zh', 'zl', 'core'), axi...  13.3 us
    all_gather x1, blocking collectives, shards(): four = lax.all_gather(share, 'x', axis=0, tiled=False)  12.9 us
    unnamed x43, local copies, waits for them, and re-layouts  7.37 us
    convert_element_type x1, local copies, waits for them, and re-layouts, shards(): table = jnp.pad(table.astype(BF16), ((0, 0), (0, 0), (0, JP - HARM)))  4.34 us
  transfers between devices with their start and end apart: 13, of which 6 were waited for; matrix products, arithmetic and copies ran while one was open for 9% of the time, Pallas kernels for 25%

profile of v1, /device:TPU:24, one launch (start us, length us, event | category | flops | bytes accessed | tf_op | source)
XLA Modules:
  0.0 172.8 jit_solution(2241904635118539074)
XLA Ops:
  6.5 0.9 reshape.50
  9.2 12.9 %all-gather = bf16[1504,128]{1,0:T(8,128)(2,1)S(1)} all-gather(bf16[376,128]{1,0:T(8,128)(2,1)S(1)} %pad_maximum_fusion.1), channel_id=2, replica_groups=mesh['gx'=8,'zh'=4,'core'=2,'x'=4,'zl'=2] {'x'}, dimensions={0}, use_global_device_ids=true | all-gather | bytes 481280 | tf_op jit(solution)/shard_map/all_gather | solution.py:269
  23.0 1.9 %shard_map.172 = (bf16[32,56,128]{2,1,0:T(8,128)(2,1)}, bf16[4,56,128]{2,1,0:T(8,128)(2,1)}) custom-call(s32[4]{0:T(128)} %bitcast.74, bf16[49,32,128]{2,1,0:T(8,128)(2,1)} %bitcast.54), custom_call_target="tpu_custom_call" | custom-call | tf_op jit(solution)/shard_map/pallas_call | solution.py:280
  24.9 4.7 %collective-permute-start = (bf16[4,56,128]{2,1,0:T(8,128)(2,1)}, bf16[4,56,128]{2,1,0:T(8,128)(2,1)S(1)}, u32[]{:S(2)}, u32[]{:S(2)}) collective-permute-start(bf16[4,56,128]{2,1,0:T(8,128)(2,1)} %get-tuple-element.23), channel_id=1, source_target_pairs={{0,64},{64,128},{128,192},{192,256},{256,320},{320,384},{384,448},... | collective-permute-start | bytes 172040 | tf_op jit(solution)/shard_map/ppermute | solution.py:242
  29.6 1.9 %collective-permute-start.1 = (bf16[4,56,128]{2,1,0:T(8,128)(2,1)}, bf16[4,56,128]{2,1,0:T(8,128)(2,1)S(1)}, u32[]{:S(2)}, u32[]{:S(2)}) collective-permute-start(bf16[4,56,128]{2,1,0:T(8,128)(2,1)} %get-tuple-element.23), channel_id=1, source_target_pairs={{0,448},{64,0},{128,64},{192,128},{256,192},{320,256},{384,320},{4... | collective-permute-start | bytes 172040 | tf_op jit(solution)/shard_map/ppermute | solution.py:242
  32.6 4.5 %collective-permute-done.1 = bf16[4,56,128]{2,1,0:T(8,128)(2,1)S(1)} collective-permute-done((bf16[4,56,128]{2,1,0:T(8,128)(2,1)}, bf16[4,56,128]{2,1,0:T(8,128)(2,1)S(1)}, u32[]{:S(2)}, u32[]{:S(2)}) %collective-permute-start.1) | collective-permute-done | bytes 57376 | tf_op jit(solution)/shard_map/ppermute | solution.py:242
  37.1 1.9 %collective-permute-start.2 = (bf16[12,56,128]{2,1,0:T(8,128)(2,1)S(1)}, bf16[12,56,128]{2,1,0:T(8,128)(2,1)S(1)}, u32[]{:S(2)}, u32[]{:S(2)}) collective-permute-start(bf16[12,56,128]{2,1,0:T(8,128)(2,1)S(1)} %constant_dynamic-update-slice_fusion), channel_id=1, source_target_pairs={{0,8},{8,16},{16,24},{24,32},{32,40},{40,48},{48,56},{56,0},{1,9},... | collective-permute-start | bytes 516104 | tf_op jit(solution)/shard_map/ppermute | solution.py:242
  39.0 7.0 %collective-permute-start.3 = (bf16[12,56,128]{2,1,0:T(8,128)(2,1)S(1)}, bf16[12,56,128]{2,1,0:T(8,128)(2,1)S(1)}, u32[]{:S(2)}, u32[]{:S(2)}) collective-permute-start(bf16[12,56,128]{2,1,0:T(8,128)(2,1)S(1)} %constant_dynamic-update-slice_fusion), channel_id=1, source_target_pairs={{0,56},{8,0},{16,8},{24,16},{32,24},{40,32},{48,40},{56,48},{1,57}... | collective-permute-start | bytes 516104 | tf_op jit(solution)/shard_map/ppermute | solution.py:242
  46.1 2.9 %collective-permute-done.2 = bf16[12,56,128]{2,1,0:T(8,128)(2,1)S(1)} collective-permute-done((bf16[12,56,128]{2,1,0:T(8,128)(2,1)S(1)}, bf16[12,56,128]{2,1,0:T(8,128)(2,1)S(1)}, u32[]{:S(2)}, u32[]{:S(2)}) %collective-permute-start.2) | collective-permute-done | bytes 172064 | tf_op jit(solution)/shard_map/ppermute | solution.py:242
  50.3 1.5 constant_dynamic-update-slice_fusion.5
  53.8 7.1 %collective-permute-start.4 = (bf16[36,56,128]{2,1,0:T(8,128)(2,1)}, bf16[36,56,128]{2,1,0:T(8,128)(2,1)}, u32[]{:S(2)}, u32[]{:S(2)}) collective-permute-start(bf16[36,56,128]{2,1,0:T(8,128)(2,1)} %constant_dynamic-update-slice_fusion.3), channel_id=1, source_target_pairs={{0,1},{1,2},{2,3},{3,4},{4,5},{5,6},{6,7},{7,0},{8,9},{9,10},{10,1... | collective-permute-start | bytes 1548296 | tf_op jit(solution)/shard_map/ppermute | solution.py:242
  60.9 1.4 convolution_convert_fusion
  62.2 4.3 %copy.34 = bf16[32,49,256]{1,0,2:T(8,128)(2,1)S(1)} copy(bf16[32,49,256]{2,0,1:T(8,128)(2,1)} %convolution_convert_fusion) | data formatting | bytes 1605632 | tf_op jit(solution)/shard_map/convert_element_type | solution.py:303
  66.6 1.8 %pad.12.rot_ref.refs_12_.refs_6_ = bf16[256,32,56]{2,1,0:T(8,128)(2,1)} pad(bf16[256,32,49]{2,1,0:T(8,128)(2,1)S(1)} %bitcast.53, bf16[]{:T(256)} %constant.53.clone.1), padding=0_0x0_0x0_7 | pad | bytes 1720322 | tf_op jit(solution)/shard_map/jit(_pad)/pad | solution.py:303
  69.7 6.4 %shard_map.176 = (bf16[128,1024]{1,0:T(8,128)(2,1)}, bf16[2,128,1536]{2,1,0:T(8,128)(2,1)}, bf16[2,128,1536]{2,1,0:T(8,128)(2,1)}) custom-call(s32[1]{0:T(128)} %bitcast.49.count, s32[128]{0:T(128)} %bitcast.72, s32[128]{0:T(128)} %get-tuple-element.41.picked.refs_1_, bf16[32,56,128]{2,1,0:T(8,128)(2,1)} %get-tuple-element.19.x_ref, ...), custom_call_target="tpu_custom_call" | custom-call | tf_op jit(solution)/shard_map/pallas_call | solution.py:127
  76.1 13.3 %all-gather.4.cloned.1.call-done = bf16[24064,128]{1,0:T(8,128)(2,1)} async-done(((bf16[1504,128]{1,0:T(8,128)(2,1)}), bf16[24064,128]{1,0:T(8,128)(2,1)}) %all-gather.4.cloned.1.call-update) | async-done | bytes 6160400 | tf_op jit(solution)/shard_map/all_gather | solution.py:276
  89.4 9.0 %shard_map.177 = (bf16[36,56,128]{2,1,0:T(8,128)(2,1)}, f32[36,56,128]{2,1,0:T(8,128)}, bf16[36,56,128]{2,1,0:T(8,128)(2,1)}) custom-call(s32[1]{0:T(128)} %bitcast.50.refs_0_, s32[128]{0:T(128)} %get-tuple-element.41.picked.refs_1_, s32[128]{0:T(128)} %bitcast.76, bf16[128,1024]{1,0:T(8,128)(2,1)} %get-tuple-element.27.refs_3_, ...), custom_call_target="tpu_custom_call" | custom-call | tf_op jit(solution)/shard_map/pallas_call | solution.py:213
  98.4 3.3 %collective-permute-start.6 = (bf16[36,56,128]{2,1,0:T(8,128)(2,1)}, bf16[36,56,128]{2,1,0:T(8,128)(2,1)S(1)}, u32[]{:S(2)}, u32[]{:S(2)}) collective-permute-start(bf16[36,56,128]{2,1,0:T(8,128)(2,1)} %get-tuple-element.31), channel_id=1, source_target_pairs={{0,448},{64,0},{128,64},{192,128},{256,192},{320,256},{384,320},{4... | collective-permute-start | bytes 1548296 | tf_op jit(solution)/shard_map/ppermute | solution.py:242
  101.7 4.3 %collective-permute-start.7 = (bf16[36,56,128]{2,1,0:T(8,128)(2,1)}, bf16[36,56,128]{2,1,0:T(8,128)(2,1)S(1)}, u32[]{:S(2)}, u32[]{:S(2)}) collective-permute-start(bf16[36,56,128]{2,1,0:T(8,128)(2,1)} %get-tuple-element.32), channel_id=1, source_target_pairs={{0,64},{64,128},{128,192},{192,256},{256,320},{320,384},{384,448},... | collective-permute-start | bytes 1548296 | tf_op jit(solution)/shard_map/ppermute | solution.py:242
  107.3 6.4 %shard_map.173 = (bf16[128,1024]{1,0:T(8,128)(2,1)}, bf16[2,128,1536]{2,1,0:T(8,128)(2,1)}, bf16[2,128,1536]{2,1,0:T(8,128)(2,1)}) custom-call(s32[1]{0:T(128)} %bitcast.45.count, s32[128]{0:T(128)} %bitcast.77, s32[128]{0:T(128)} %bitcast.70, bf16[32,56,128]{2,1,0:T(8,128)(2,1)} %get-tuple-element.19.x_ref, ...), custom_call_target="tpu_custom_call" | custom-call | tf_op jit(solution)/shard_map/pallas_call | solution.py:127
  113.7 5.1 %collective-permute-start.5 = (bf16[36,56,128]{2,1,0:T(8,128)(2,1)}, bf16[36,56,128]{2,1,0:T(8,128)(2,1)S(1)}, u32[]{:S(2)}, u32[]{:S(2)}) collective-permute-start(bf16[36,56,128]{2,1,0:T(8,128)(2,1)} %constant_dynamic-update-slice_fusion.3), channel_id=1, source_target_pairs={{0,7},{1,0},{2,1},{3,2},{4,3},{5,4},{6,5},{7,6},{8,15},{9,8},{10,9... | collective-permute-start | bytes 1548296 | tf_op jit(solution)/shard_map/ppermute | solution.py:242
  118.8 1.1 constant_dynamic-update-slice_fusion.14
  120.3 3.9 %collective-permute-start.8 = (bf16[12,56,128]{2,1,0:T(8,128)(2,1)S(1)}, bf16[12,56,128]{2,1,0:T(8,128)(2,1)S(1)}, u32[]{:S(2)}, u32[]{:S(2)}) collective-permute-start(bf16[12,56,128]{2,1,0:T(8,128)(2,1)S(1)} %get-tuple-element.37), channel_id=1, source_target_pairs={{0,56},{8,0},{16,8},{24,16},{32,24},{40,32},{48,40},{56,48},{1,57}... | collective-permute-start | bytes 516104 | tf_op jit(solution)/shard_map/ppermute | solution.py:242
  124.2 1.9 %collective-permute-start.9 = (bf16[12,56,128]{2,1,0:T(8,128)(2,1)S(1)}, bf16[12,56,128]{2,1,0:T(8,128)(2,1)S(1)}, u32[]{:S(2)}, u32[]{:S(2)}) collective-permute-start(bf16[12,56,128]{2,1,0:T(8,128)(2,1)S(1)} %get-tuple-element.38), channel_id=1, source_target_pairs={{0,8},{8,16},{16,24},{24,32},{32,40},{40,48},{48,56},{56,0},{1,9},... | collective-permute-start | bytes 516104 | tf_op jit(solution)/shard_map/ppermute | solution.py:242
  126.2 0.9 collective-permute-done.8
  127.1 9.9 %collective-permute-done.9 = bf16[12,56,128]{2,1,0:T(8,128)(2,1)S(1)} collective-permute-done((bf16[12,56,128]{2,1,0:T(8,128)(2,1)S(1)}, bf16[12,56,128]{2,1,0:T(8,128)(2,1)S(1)}, u32[]{:S(2)}, u32[]{:S(2)}) %collective-permute-start.9) | collective-permute-done | bytes 172064 | tf_op jit(solution)/shard_map/ppermute | solution.py:242
  137.0 1.9 %collective-permute-start.10 = (bf16[4,56,128]{2,1,0:T(8,128)(2,1)S(1)}, bf16[4,56,128]{2,1,0:T(8,128)(2,1)S(1)}, u32[]{:S(2)}, u32[]{:S(2)}) collective-permute-start(bf16[4,56,128]{2,1,0:T(8,128)(2,1)S(1)} %get-tuple-element.39), channel_id=1, source_target_pairs={{0,7},{1,0},{2,1},{3,2},{4,3},{5,4},{6,5},{7,6},{8,15},{9,8},{10,9... | collective-permute-start | bytes 172040 | tf_op jit(solution)/shard_map/ppermute | solution.py:242
  139.0 3.9 %collective-permute-start.11 = (bf16[4,56,128]{2,1,0:T(8,128)(2,1)S(1)}, bf16[4,56,128]{2,1,0:T(8,128)(2,1)S(1)}, u32[]{:S(2)}, u32[]{:S(2)}) collective-permute-start(bf16[4,56,128]{2,1,0:T(8,128)(2,1)S(1)} %get-tuple-element.40), channel_id=1, source_target_pairs={{0,1},{1,2},{2,3},{3,4},{4,5},{5,6},{6,7},{7,0},{8,9},{9,10},{10,1... | collective-permute-start | bytes 172040 | tf_op jit(solution)/shard_map/ppermute | solution.py:242
  143.0 1.2 copy-done.1
  144.2 6.9 %shard_map.174 = (bf16[128,1024]{1,0:T(8,128)(2,1)}, bf16[2,128,1536]{2,1,0:T(8,128)(2,1)}, bf16[2,128,1536]{2,1,0:T(8,128)(2,1)}) custom-call(s32[1]{0:T(128)} %bitcast.47.count, s32[128]{0:T(128)} %fusion.4.sources, s32[128]{0:T(128)} %get-tuple-element.42.picked.refs_3_, bf16[108,56,128]{2,1,0:T(8,128)(2,1)} %copy-done.1, ...), custom_call_target="tpu_custom_call" | custom-call | tf_op jit(solution)/shard_map/pallas_call | solution.py:127
  151.1 12.0 %shard_map.175.gathered = f32[32,56,128]{2,1,0:T(8,128)} custom-call(s32[1]{0:T(128)} %bitcast.46.refs_0_, s32[1]{0:T(128)} %bitcast.48.refs_1_, s32[128]{0:T(128)} %bitcast.71, s32[128]{0:T(128)} %get-tuple-element.42.picked.refs_3_, s32[128]{0:T(128)} %bitcast.78, s32[128]{0:T(128)} %bitcast.73, bf16[128,1024]{1,0:T(8,128)(2,1)} %get-tuple-element.20.refs_6_, ...), custom_call_target="tpu_custom_call" | custom-call | tf_op jit(solution)/shard_map/pallas_call | solution.py:213
  163.8 2.2 %shard_map.178 = bf16[49,32,128]{2,1,0:T(8,128)(2,1)} custom-call(s32[4]{0:T(128)} %bitcast.75, bf16[49,32,128]{2,1,0:T(8,128)(2,1)} %bitcast.55, f32[32,56,128]{2,1,0:T(8,128)} %shard_map.175.gathered, f32[4,56,128]{2,1,0:T(8,128)} %fusion.2.returned), custom_call_target="tpu_custom_call" | custom-call | tf_op jit(solution)/shard_map/pallas_call | solution.py:331
  (76 shorter events, 9.4 us)
Async XLA Ops:
  6.5 54.3 %copy-start = (bf16[49,49,256]{2,1,0:T(8,128)(2,1)S(1)}, bf16[49,49,256]{2,1,0:T(8,128)(2,1)}, u32[]{:S(2)}) copy-start(bf16[49,49,256]{2,1,0:T(8,128)(2,1)} %param.28) | copy-start | bytes 3687940
  6.5 82.9 %all-gather.4.cloned.1.call-start = ((), (), s32[]{:S(2)}) async-start(), calls=%async_computation | async-start | bytes 6545408 | tf_op jit(solution)/shard_map/all_gather | solution.py:276
  22.2 38.7 %copy-start.12 = (bf16[32,49,1]{1,0,2:T(8,128)(2,1)S(1)}, bf16[32,49,1]{1,0,2:T(8,128)(2,1)}, u32[]{:S(2)}) copy-start(bf16[32,49,1]{1,0,2:T(8,128)(2,1)} %constant.84) | copy-start | bytes 9412
  24.9 6.8 %collective-permute-start = (bf16[4,56,128]{2,1,0:T(8,128)(2,1)}, bf16[4,56,128]{2,1,0:T(8,128)(2,1)S(1)}, u32[]{:S(2)}, u32[]{:S(2)}) collective-permute-start(bf16[4,56,128]{2,1,0:T(8,128)(2,1)} %get-tuple-element.23), channel_id=1, source_target_pairs={{0,64},{64,128},{128,192},{192,256},{256,320},{320,384},{384,448},... | collective-permute-start | bytes 172040 | tf_op jit(solution)/shard_map/ppermute | solution.py:242
  29.6 7.5 %collective-permute-start.1 = (bf16[4,56,128]{2,1,0:T(8,128)(2,1)}, bf16[4,56,128]{2,1,0:T(8,128)(2,1)S(1)}, u32[]{:S(2)}, u32[]{:S(2)}) collective-permute-start(bf16[4,56,128]{2,1,0:T(8,128)(2,1)} %get-tuple-element.23), channel_id=1, source_target_pairs={{0,448},{64,0},{128,64},{192,128},{256,192},{320,256},{384,320},{4... | collective-permute-start | bytes 172040 | tf_op jit(solution)/shard_map/ppermute | solution.py:242
  31.7 22.0 %copy-start.10 = (bf16[4,56,128]{2,1,0:T(8,128)(2,1)}, bf16[4,56,128]{2,1,0:T(8,128)(2,1)S(1)}, u32[]{:S(2)}) copy-start(bf16[4,56,128]{2,1,0:T(8,128)(2,1)S(1)} %collective-permute-done) | copy-start | bytes 172036
  37.1 16.7 %copy-start.7 = (bf16[4,56,128]{2,1,0:T(8,128)(2,1)}, bf16[4,56,128]{2,1,0:T(8,128)(2,1)S(1)}, u32[]{:S(2)}) copy-start(bf16[4,56,128]{2,1,0:T(8,128)(2,1)S(1)} %collective-permute-done.1) | copy-start | bytes 172036
  37.1 11.9 %collective-permute-start.2 = (bf16[12,56,128]{2,1,0:T(8,128)(2,1)S(1)}, bf16[12,56,128]{2,1,0:T(8,128)(2,1)S(1)}, u32[]{:S(2)}, u32[]{:S(2)}) collective-permute-start(bf16[12,56,128]{2,1,0:T(8,128)(2,1)S(1)} %constant_dynamic-update-slice_fusion), channel_id=1, source_target_pairs={{0,8},{8,16},{16,24},{24,32},{32,40},{40,48},{48,56},{56,0},{1,9},... | collective-permute-start | bytes 516104 | tf_op jit(solution)/shard_map/ppermute | solution.py:242
  39.0 13.4 %collective-permute-start.3 = (bf16[12,56,128]{2,1,0:T(8,128)(2,1)S(1)}, bf16[12,56,128]{2,1,0:T(8,128)(2,1)S(1)}, u32[]{:S(2)}, u32[]{:S(2)}) collective-permute-start(bf16[12,56,128]{2,1,0:T(8,128)(2,1)S(1)} %constant_dynamic-update-slice_fusion), channel_id=1, source_target_pairs={{0,56},{8,0},{16,8},{24,16},{32,24},{40,32},{48,40},{56,48},{1,57}... | collective-permute-start | bytes 516104 | tf_op jit(solution)/shard_map/ppermute | solution.py:242
  49.0 4.8 %copy-start.5 = (bf16[12,56,128]{2,1,0:T(8,128)(2,1)}, bf16[12,56,128]{2,1,0:T(8,128)(2,1)S(1)}, u32[]{:S(2)}) copy-start(bf16[12,56,128]{2,1,0:T(8,128)(2,1)S(1)} %collective-permute-done.2) | copy-start | bytes 516100
  52.4 0.7 copy-start.3
  53.8 65.1 %collective-permute-start.4 = (bf16[36,56,128]{2,1,0:T(8,128)(2,1)}, bf16[36,56,128]{2,1,0:T(8,128)(2,1)}, u32[]{:S(2)}, u32[]{:S(2)}) collective-permute-start(bf16[36,56,128]{2,1,0:T(8,128)(2,1)} %constant_dynamic-update-slice_fusion.3), channel_id=1, source_target_pairs={{0,1},{1,2},{2,3},{3,4},{4,5},{5,6},{6,7},{7,0},{8,9},{9,10},{10,1... | collective-permute-start | bytes 1548296 | tf_op jit(solution)/shard_map/ppermute | solution.py:242
  66.6 2.5 %copy-start.13 = (s32[1,1,1,2,128]{4,3,2,1,0:T(2,128)S(1)}, s32[1,1,1,2,128]{4,3,2,1,0:T(2,128)}, u32[]{:S(2)}) copy-start(s32[1,1,1,2,128]{4,3,2,1,0:T(2,128)} %param.26) | copy-start | bytes 3076
  89.4 16.6 %copy-start.14 = (s32[1,1,1,128]{3,2,1,0:T(1,128)S(1)}, s32[1,1,1,128]{3,2,1,0:T(1,128)}, u32[]{:S(2)}) copy-start(s32[1,1,1,128]{3,2,1,0:T(1,128)} %param.24) | copy-start | bytes 1540
  98.4 21.6 %collective-permute-start.6 = (bf16[36,56,128]{2,1,0:T(8,128)(2,1)}, bf16[36,56,128]{2,1,0:T(8,128)(2,1)S(1)}, u32[]{:S(2)}, u32[]{:S(2)}) collective-permute-start(bf16[36,56,128]{2,1,0:T(8,128)(2,1)} %get-tuple-element.31), channel_id=1, source_target_pairs={{0,448},{64,0},{128,64},{192,128},{256,192},{320,256},{384,320},{4... | collective-permute-start | bytes 1548296 | tf_op jit(solution)/shard_map/ppermute | solution.py:242
  101.7 18.3 %collective-permute-start.7 = (bf16[36,56,128]{2,1,0:T(8,128)(2,1)}, bf16[36,56,128]{2,1,0:T(8,128)(2,1)S(1)}, u32[]{:S(2)}, u32[]{:S(2)}) collective-permute-start(bf16[36,56,128]{2,1,0:T(8,128)(2,1)} %get-tuple-element.32), channel_id=1, source_target_pairs={{0,64},{64,128},{128,192},{192,256},{256,320},{320,384},{384,448},... | collective-permute-start | bytes 1548296 | tf_op jit(solution)/shard_map/ppermute | solution.py:242
  107.3 12.6 %copy-start.6 = (bf16[12,56,128]{2,1,0:T(8,128)(2,1)S(1)}, bf16[12,56,128]{2,1,0:T(8,128)(2,1)}, u32[]{:S(2)}) copy-start(bf16[12,56,128]{2,1,0:T(8,128)(2,1)} %copy-done.5) | copy-start | bytes 516100
  107.3 12.6 %copy-start.11 = (bf16[4,56,128]{2,1,0:T(8,128)(2,1)S(1)}, bf16[4,56,128]{2,1,0:T(8,128)(2,1)}, u32[]{:S(2)}) copy-start(bf16[4,56,128]{2,1,0:T(8,128)(2,1)} %copy-done.10) | copy-start | bytes 172036
  107.3 12.6 %copy-start.9 = (bf16[4,56,128]{2,1,0:T(8,128)(2,1)S(1)}, bf16[4,56,128]{2,1,0:T(8,128)(2,1)}, u32[]{:S(2)}) copy-start(bf16[4,56,128]{2,1,0:T(8,128)(2,1)} %get-tuple-element.23) | copy-start | bytes 172036
  113.7 6.3 %copy-start.2 = (f32[36,56,128]{2,1,0:T(8,128)S(1)}, f32[36,56,128]{2,1,0:T(8,128)}, u32[]{:S(2)}) copy-start(f32[36,56,128]{2,1,0:T(8,128)} %get-tuple-element.30) | copy-start | bytes 3096580
  113.7 29.2 %collective-permute-start.5 = (bf16[36,56,128]{2,1,0:T(8,128)(2,1)}, bf16[36,56,128]{2,1,0:T(8,128)(2,1)S(1)}, u32[]{:S(2)}, u32[]{:S(2)}) collective-permute-start(bf16[36,56,128]{2,1,0:T(8,128)(2,1)} %constant_dynamic-update-slice_fusion.3), channel_id=1, source_target_pairs={{0,7},{1,0},{2,1},{3,2},{4,3},{5,4},{6,5},{7,6},{8,15},{9,8},{10,9... | collective-permute-start | bytes 1548296 | tf_op jit(solution)/shard_map/ppermute | solution.py:242
  120.0 6.1 %copy-start.8 = (bf16[4,56,128]{2,1,0:T(8,128)(2,1)S(1)}, bf16[4,56,128]{2,1,0:T(8,128)(2,1)}, u32[]{:S(2)}) copy-start(bf16[4,56,128]{2,1,0:T(8,128)(2,1)} %copy-done.7) | copy-start | bytes 172036
  120.0 6.1 %copy-start.4 = (bf16[12,56,128]{2,1,0:T(8,128)(2,1)S(1)}, bf16[12,56,128]{2,1,0:T(8,128)(2,1)}, u32[]{:S(2)}) copy-start(bf16[12,56,128]{2,1,0:T(8,128)(2,1)} %copy-done.3) | copy-start | bytes 516100
  120.3 6.8 %collective-permute-start.8 = (bf16[12,56,128]{2,1,0:T(8,128)(2,1)S(1)}, bf16[12,56,128]{2,1,0:T(8,128)(2,1)S(1)}, u32[]{:S(2)}, u32[]{:S(2)}) collective-permute-start(bf16[12,56,128]{2,1,0:T(8,128)(2,1)S(1)} %get-tuple-element.37), channel_id=1, source_target_pairs={{0,56},{8,0},{16,8},{24,16},{32,24},{40,32},{48,40},{56,48},{1,57}... | collective-permute-start | bytes 516104 | tf_op jit(solution)/shard_map/ppermute | solution.py:242
  124.2 12.8 %collective-permute-start.9 = (bf16[12,56,128]{2,1,0:T(8,128)(2,1)S(1)}, bf16[12,56,128]{2,1,0:T(8,128)(2,1)S(1)}, u32[]{:S(2)}, u32[]{:S(2)}) collective-permute-start(bf16[12,56,128]{2,1,0:T(8,128)(2,1)S(1)} %get-tuple-element.38), channel_id=1, source_target_pairs={{0,8},{8,16},{16,24},{24,32},{32,40},{40,48},{48,56},{56,0},{1,9},... | collective-permute-start | bytes 516104 | tf_op jit(solution)/shard_map/ppermute | solution.py:242
  137.0 26.0 %collective-permute-start.10 = (bf16[4,56,128]{2,1,0:T(8,128)(2,1)S(1)}, bf16[4,56,128]{2,1,0:T(8,128)(2,1)S(1)}, u32[]{:S(2)}, u32[]{:S(2)}) collective-permute-start(bf16[4,56,128]{2,1,0:T(8,128)(2,1)S(1)} %get-tuple-element.39), channel_id=1, source_target_pairs={{0,7},{1,0},{2,1},{3,2},{4,3},{5,4},{6,5},{7,6},{8,15},{9,8},{10,9... | collective-permute-start | bytes 172040 | tf_op jit(solution)/shard_map/ppermute | solution.py:242
  139.0 24.1 %collective-permute-start.11 = (bf16[4,56,128]{2,1,0:T(8,128)(2,1)S(1)}, bf16[4,56,128]{2,1,0:T(8,128)(2,1)S(1)}, u32[]{:S(2)}, u32[]{:S(2)}) collective-permute-start(bf16[4,56,128]{2,1,0:T(8,128)(2,1)S(1)} %get-tuple-element.40), channel_id=1, source_target_pairs={{0,1},{1,2},{2,3},{3,4},{4,5},{5,6},{6,7},{7,0},{8,9},{9,10},{10,1... | collective-permute-start | bytes 172040 | tf_op jit(solution)/shard_map/ppermute | solution.py:242
  143.0 1.2 copy-start.1
Sparse Core Ops, SparseCore 0:
  23.1 66.2 all-gather.3

commit v2 on v1

v2 whole, which is shorter than its diff:
```python
import functools

import jax
import jax.numpy as jnp
import numpy as np
from jax import lax
from jax.experimental import pallas as pl
from jax.experimental.pallas import tpu as pltpu
from jax.sharding import Mesh
from jax.sharding import PartitionSpec as P

LMAX = 6
HARM = (LMAX + 1) ** 2
JP = 56
KEPT = 29
KP = 32
EDGES = 128
ROTS = 256
ATOMS = 32
BOUND = 4
AROUND = 27 * BOUND
STEP = 32
PITCH = EDGES + 1
LANES = 128
BF16 = jnp.bfloat16
F32 = jnp.float32

SMEM = pl.BlockSpec(memory_space=pltpu.SMEM)
VMEM = pl.BlockSpec(memory_space=pltpu.VMEM)
HBM = pl.BlockSpec(memory_space=pltpu.HBM)
ANY = pl.BlockSpec(memory_space=pl.ANY)
PARAMS = pltpu.CompilerParams(vmem_limit_bytes=24 * 2**20)
WIDE = pltpu.CompilerParams(vmem_limit_bytes=58 * 2**20)

ROWS0, BLK0 = 16, 7
ROWS1, BLK1 = 24, 6
ROWS2, BLK2 = 20, 5
G0 = 4 * ROWS0 * BLK0
G1 = 4 * ROWS1 * BLK1
G2 = 4 * ROWS2 * BLK2
GROWS = G0 + G1 + G2


def kept_rows():
    listing = [d * d + d for d in range(LMAX + 1)]
    for shift in (1, -1, 2, -2):
        listing += [d * d + d + shift for d in range(abs(shift), LMAX + 1)]
    return listing


def slot_order():
    order = []
    for zh in range(4):
        for zl in range(2):
            for core in range(2):
                for x in range(4):
                    order.append(((zh * 2 + core) * 4 + x) * 2 + zl)
    return order


def spreads():
    order = slot_order()
    zero = np.zeros((2, 512, 512), np.float32)
    one = np.zeros((768, 768), np.float32)
    two = np.zeros((2, 768, 640), np.float32)
    for slot, shard in enumerate(order):
        half, local = divmod(slot, 32)
        for r in range(14):
            zero[half, shard * 14 + r - 384 * half, local * ROWS0 + r] = 1
        for r in range(12):
            if half == 0:
                one[shard * 12 + r, local * ROWS1 + r] = 1
                one[384 + shard * 12 + r, local * ROWS1 + 12 + r] = 1
        for r in range(10):
            two[half, shard * 10 + r - 256 * half, local * ROWS2 + r] = 1
            two[half, 384 + shard * 10 + r - 256 * half, local * ROWS2 + 10 + r] = 1
    return [jnp.asarray(m, BF16) for m in (zero, one, two)]


def tables_kernel(border_atoms, feats, x_out, border_out, tmp):
    for j in range(HARM):
        tmp[pl.ds(j * 33, ATOMS), :] = feats[j].astype(F32)
    tail = jnp.zeros((JP - HARM, LANES), F32)
    for a in range(ATOMS):
        rows = tmp[pl.ds(a, HARM, stride=33), :]
        x_out[a] = jnp.concatenate([rows, tail], axis=0).astype(BF16)
    for t in range(BOUND):
        border_out[t] = x_out[border_atoms[t]]


def rotations_kernel(rotations, out, tmp):
    blank = jnp.zeros((LANES - HARM, ROTS), F32)
    for n, i in enumerate(kept_rows()):
        rows = jnp.concatenate([rotations[i].astype(F32), blank], axis=0)
        tmp[pl.ds(n, ROTS, stride=KP + 1), :] = rows.T
    for n in range(KEPT, KP):
        tmp[pl.ds(n, ROTS, stride=KP + 1), :] = jnp.zeros((ROTS, LANES), F32)
    for r in range(ROTS):
        out[r] = tmp[pl.ds(r * (KP + 1), KP), 0:JP].astype(BF16)


def blocks_of(count):
    return (count + (STEP - 1)) // STEP


def forward_kernel(sets, *refs):
    counts, sources, picked = refs[0:sets], refs[sets : 2 * sets], refs[2 * sets : 3 * sets]
    x_ref, rot_ref = refs[3 * sets : 3 * sets + 2]
    spread_refs = refs[3 * sets + 2 : 3 * sets + 5]
    outs, (tmp, sp0, sp1, sp2, sems) = refs[3 * sets + 6 : -5], refs[-5:]
    copies = [
        pltpu.make_async_copy(source, target, sems.at[n])
        for n, (source, target) in enumerate(zip(spread_refs, (sp0, sp1, sp2), strict=True))
    ]
    for copy in copies:
        copy.start()

    def spread(planes, matrix):
        return jnp.dot(jnp.concatenate(planes, axis=1), matrix, preferred_element_type=F32).astype(BF16)

    for i in range(sets):
        t0, t1, t2 = outs[3 * i : 3 * i + 3]

        def step(s, carry, i=i):
            for u in range(STEP):
                e = s * STEP + u
                rows = jnp.dot(rot_ref[picked[i][e]], x_ref[sources[i][e]], preferred_element_type=F32)
                tmp[i, pl.ds(e, KP, stride=PITCH), :] = rows
            return carry

        lax.fori_loop(0, blocks_of(counts[i][0]), step, 0)

        def plane(n, i=i):
            return tmp[i, pl.ds(n * PITCH, EDGES), :].astype(BF16)

        if i == 0:
            for copy in copies:
                copy.wait()
        zero = [plane(n) for n in range(7)]
        t0[:, 0:512] = spread(zero[0:4], sp0[0])
        t0[:, 512:1024] = spread(zero[3:7], sp0[1])
        plus = [plane(7 + n) for n in range(6)]
        minus = [plane(13 + n) for n in range(6)]
        for h in range(2):
            p, q = plus[3 * h : 3 * h + 3], minus[3 * h : 3 * h + 3]
            t1[0, :, 768 * h : 768 * (h + 1)] = spread(p + [-m for m in q], sp1[...])
            t1[1, :, 768 * h : 768 * (h + 1)] = spread(q + p, sp1[...])
        plus = [plane(19 + n) for n in range(5)]
        minus = [plane(24 + n) for n in range(5)]
        for h in range(2):
            p, q = plus[2 * h : 2 * h + 3], minus[2 * h : 2 * h + 3]
            t2[0, :, 640 * h : 640 * (h + 1)] = spread(p + [-m for m in q], sp2[h])
            t2[1, :, 640 * h : 640 * (h + 1)] = spread(q + p, sp2[h])


def forward(counts, sources, picked, x, table, sp, after):
    sets = len(counts)
    one = (
        jax.ShapeDtypeStruct((EDGES, 64 * ROWS0), BF16),
        jax.ShapeDtypeStruct((2, EDGES, 64 * ROWS1), BF16),
        jax.ShapeDtypeStruct((2, EDGES, 64 * ROWS2), BF16),
    )
    outs = pl.pallas_call(
        functools.partial(forward_kernel, sets),
        out_shape=one * sets,
        in_specs=[SMEM] * (3 * sets) + [VMEM] * 2 + [HBM] * 3 + [ANY],
        out_specs=(VMEM,) * (3 * sets),
        scratch_shapes=[pltpu.VMEM((sets, KP * PITCH, LANES), F32)]
        + [pltpu.VMEM(m.shape, BF16) for m in sp]
        + [pltpu.SemaphoreType.DMA((3,))],
        compiler_params=WIDE,
    )(*counts, *sources, *picked, x, table, *sp, after)
    return [outs[3 * i : 3 * i + 3] for i in range(sets)]


def back_kernel(sets, trash, finish, *refs):
    counts, picked, targets = refs[0:sets], refs[sets : 2 * sets], refs[2 * sets : 3 * sets]
    refs = refs[3 * sets :]
    sources = [refs[3 * i : 3 * i + 3] for i in range(sets)]
    table, gathered, _ = refs[3 * sets : 3 * sets + 3]
    refs = refs[3 * sets + 3 :]
    outs, (w0, w1, w2, t0, t1, t2, rot_ref, tmp, acc, sems) = refs[:-10], refs[-10:]
    moves = []
    start = 0
    for n, (weight, turned, size) in enumerate(((w0, t0, G0), (w1, t1, G1), (w2, t2, G2))):
        moves.append([(sources[i][n], turned.at[i]) for i in range(sets)])
        moves[-1].append((gathered.at[:, pl.ds(start, size), :], weight))
        start += size
    moves.append([(table, rot_ref)])
    copies = []
    for n, group in enumerate(moves):
        copies.append(
            [pltpu.make_async_copy(src, dst, sems.at[n, m]) for m, (src, dst) in enumerate(group)]
        )
        for copy in copies[-1]:
            copy.start()

    def arrived(n):
        for copy in copies[n]:
            copy.wait()

    acc[...] = jnp.zeros_like(acc)
    for i in range(sets):
        tmp[i, pl.ds(KEPT * PITCH, (KP - KEPT) * PITCH), :] = jnp.zeros(((KP - KEPT) * PITCH, LANES), F32)

    def mix(lhs, ref, rows, blocks, places):
        for b in range(0, blocks, 2):
            width = min(2, blocks - b)
            weight = [
                ref[:, (b + i) * rows : (b + i + 1) * rows, :].reshape(16 * rows, LANES) for i in range(width)
            ]
            weight = jnp.concatenate(weight, axis=1) if width == 2 else weight[0]
            result = jnp.dot(lhs, weight, preferred_element_type=F32)
            for n, (i, first) in enumerate(places):
                for w in range(width):
                    tmp[i, pl.ds((first + b + w) * PITCH, EDGES), :] = result[
                        n * EDGES : (n + 1) * EDGES, w * LANES : (w + 1) * LANES
                    ]

    arrived(0)
    mix(t0[...].reshape(sets * EDGES, 64 * ROWS0), w0, 4 * ROWS0, BLK0, [(i, 0) for i in range(sets)])
    for n, (lhs, ref, rows, blocks, first) in enumerate(((t1, w1, ROWS1, BLK1, 7), (t2, w2, ROWS2, BLK2, 19))):
        arrived(n + 1)
        mix(
            lhs[...].reshape(sets * 2 * EDGES, 64 * rows), ref, 4 * rows, blocks,
            [(i, first + sign * blocks) for i in range(sets) for sign in range(2)],
        )
    arrived(3)

    for i in range(sets):
        count = counts[i][0]

        def step(s, carry, i=i, count=count):
            for u in range(STEP):
                e = s * STEP + u
                rows = tmp[i, pl.ds(e, KP, stride=PITCH), :].astype(BF16)
                part = lax.dot_general(
                    rot_ref[picked[i][e]], rows, (((0,), (0,)), ((), ())), preferred_element_type=F32
                )
                acc[jnp.where(e < count, targets[i][e], trash)] += part
            return carry

        lax.fori_loop(0, blocks_of(count), step, 0)
    finish(acc, *outs)


def store_returned(acc, low, middle, high):
    low[...] = acc[0:36].astype(BF16)
    middle[...] = acc[36:72]
    high[...] = acc[72:108].astype(BF16)


def store_gathered(acc, out):
    out[...] = acc[0:ATOMS]


def back(counts, picked, targets, turned, table, gathered, after, rows, trash, finish, out_shape):
    sets = len(counts)
    return pl.pallas_call(
        functools.partial(back_kernel, sets, trash, finish),
        out_shape=out_shape,
        in_specs=[SMEM] * (3 * sets) + [HBM] * (3 * sets + 2) + [ANY],
        out_specs=jax.tree.map(lambda _: VMEM, out_shape),
        scratch_shapes=[
            pltpu.VMEM((16, G0, LANES), BF16),
            pltpu.VMEM((16, G1, LANES), BF16),
            pltpu.VMEM((16, G2, LANES), BF16),
            pltpu.VMEM((sets, EDGES, 64 * ROWS0), BF16),
            pltpu.VMEM((sets, 2, EDGES, 64 * ROWS1), BF16),
            pltpu.VMEM((sets, 2, EDGES, 64 * ROWS2), BF16),
            pltpu.VMEM((ROTS, KP, JP), BF16),
            pltpu.VMEM((sets, KP * PITCH, LANES), F32),
            pltpu.VMEM((rows, JP, LANES), F32),
            pltpu.SemaphoreType.DMA((4, sets + 1)),
        ],
        compiler_params=WIDE,
    )(*counts, *picked, *targets, *[t for one in turned for t in one], table, gathered, after)


def final_kernel(border_atoms, feats, gathered_in, gathered_x, returned, out, acc):
    for a in range(ATOMS):
        acc[pl.ds(a * 57, JP), :] = gathered_in[a] + gathered_x[a]
    for t in range(BOUND):
        acc[pl.ds(border_atoms[t] * 57, JP), :] += returned[t]
    for j in range(HARM):
        total = acc[pl.ds(j, ATOMS, stride=57), :]
        out[j] = (feats[j].astype(F32) + 0.25 * total).astype(BF16)


def ring(axis, block, shift):
    count = lax.axis_size(axis)
    return lax.ppermute(block, axis, [(i, (i + shift) % count) for i in range(count)])


GX, GY, GZ = "gx", ("zh", "core"), ("x", "zl")


def shards(
    features,
    border_atoms,
    inner_source,
    inner_target,
    inner_rotation,
    inner_count,
    cross_source,
    cross_target,
    cross_rotation,
    cross_count,
    rotations,
    order_zero,
    order_one,
    order_two,
):
    share0 = jnp.pad(order_zero.reshape(14, BLK0, LANES).transpose(1, 0, 2), ((0, 0), (0, 2), (0, 0)))
    share1 = order_one.reshape(2, 12, BLK1, LANES).transpose(2, 0, 1, 3).reshape(BLK1, ROWS1, LANES)
    share2 = order_two.reshape(2, 10, BLK2, LANES).transpose(2, 0, 1, 3).reshape(BLK2, 20, LANES)
    share = jnp.concatenate([s.reshape(-1, LANES) for s in (share0, share1, share2)], axis=0)
    four = lax.all_gather(share, "x", axis=0, tiled=False)
    pieces = []
    start = 0
    for rows, blocks in ((ROWS0, BLK0), (ROWS1, BLK1), (ROWS2, BLK2)):
        piece = four[:, start : start + rows * blocks].reshape(4, blocks, rows, LANES)
        pieces.append(piece.transpose(1, 0, 2, 3).reshape(blocks * 4 * rows, LANES))
        start += rows * blocks
    gathered_weights = lax.all_gather(jnp.concatenate(pieces, axis=0), ("zh", "zl", "core"), axis=0, tiled=False)

    feats = features[0, 0, 0].transpose(1, 0, 2)
    border_rows = border_atoms[0, 0, 0]
    x, border = pl.pallas_call(
        tables_kernel,
        out_shape=(
            jax.ShapeDtypeStruct((ATOMS, JP, LANES), BF16),
            jax.ShapeDtypeStruct((BOUND, JP, LANES), BF16),
        ),
        in_specs=[SMEM, VMEM],
        out_specs=(VMEM, VMEM),
        scratch_shapes=[pltpu.VMEM((HARM * 33, LANES), F32)],
        compiler_params=PARAMS,
    )(border_rows, feats)

    table = pl.pallas_call(
        rotations_kernel,
        out_shape=jax.ShapeDtypeStruct((ROTS, KP, JP), BF16),
        in_specs=[VMEM],
        out_specs=VMEM,
        scratch_shapes=[pltpu.VMEM((ROTS * (KP + 1), LANES), F32)],
        compiler_params=pltpu.CompilerParams(vmem_limit_bytes=12 * 2**20),
    )(rotations)

    sp = spreads()
    count_in, count_x = inner_count.reshape(1), cross_count.reshape(1)
    source_in, target_in, rot_in = inner_source[0, 0, 0], inner_target[0, 0, 0], inner_rotation[0, 0, 0]
    far_rows, target_x = cross_source[0, 0, 0], cross_target[0, 0, 0]
    rot_inward, rot_outward = cross_rotation[0, 0, 0, 0], cross_rotation[0, 0, 0, 1]

    def widen(axis, block):
        return jnp.concatenate([ring(axis, block, 1), block, ring(axis, block, -1)], axis=0)

    near = widen(GZ, border)
    turned_out, turned_in = forward(
        [count_x, count_in], [target_x, source_in], [rot_outward, rot_in], x, table, sp, near
    )
    near = widen(GY, near)
    near, turned_in = lax.optimization_barrier((near, turned_in))
    near = widen(GX, near)

    face = (36, JP, LANES)
    inside = (ATOMS, JP, LANES)
    low, middle, high = back(
        [count_x], [rot_outward], [far_rows], [turned_out], table, gathered_weights, near, 112, AROUND,
        store_returned,
        (jax.ShapeDtypeStruct(face, BF16), jax.ShapeDtypeStruct(face, F32), jax.ShapeDtypeStruct(face, BF16)),
    )

    def fold(axis, low, middle, high):
        return middle + ring(axis, low, -1).astype(F32) + ring(axis, high, 1).astype(F32)

    def thirds(block):
        third = block.shape[0] // 3
        return block[:third].astype(BF16), block[third : 2 * third], block[2 * third :].astype(BF16)

    gathered_in = back(
        [count_in], [rot_in], [target_in], [turned_in], table, gathered_weights, low, 40, ATOMS, store_gathered,
        jax.ShapeDtypeStruct(inside, F32),
    )
    [turned_x] = forward([count_x], [far_rows], [rot_inward], near, table, sp, gathered_in)
    returned = fold(GX, low, middle, high)
    returned, turned_x = lax.optimization_barrier((returned, turned_x))
    gathered_x = back(
        [count_x], [rot_inward], [target_x], [turned_x], table, gathered_weights, returned, 40, ATOMS,
        store_gathered, jax.ShapeDtypeStruct(inside, F32),
    )
    returned = fold(GY, *thirds(returned))
    returned, gathered_x = lax.optimization_barrier((returned, gathered_x))
    returned = fold(GZ, *thirds(returned))

    updated = pl.pallas_call(
        final_kernel,
        out_shape=jax.ShapeDtypeStruct((HARM, ATOMS, LANES), BF16),
        in_specs=[SMEM] + [VMEM] * 4,
        out_specs=VMEM,
        scratch_shapes=[pltpu.VMEM((ATOMS * 57, LANES), F32)],
        compiler_params=PARAMS,
    )(border_rows, feats, gathered_in, gathered_x, returned)
    return updated.transpose(1, 0, 2).reshape(features.shape)


def solution(mesh):
    fine = Mesh(mesh.devices.reshape(8, 4, 2, 4, 2), ("gx", "zh", "core", "x", "zl"))
    cell = ("gx", GY, GZ)
    plane = GY + GZ
    in_specs = (
        P(*cell, None, None, None),
        P(*cell, None),
        P(*cell, None),
        P(*cell, None),
        P(*cell, None),
        P(*cell),
        P(*cell, None),
        P(*cell, None),
        P(*cell, None, None),
        P(*cell),
        P(),
        P(plane, None),
        P(None, plane, None),
        P(None, plane, None),
    )
    out_specs = P(*cell, None, None, None)
    return jax.shard_map(shards, mesh=fine, in_specs=in_specs, out_specs=out_specs, check_vma=False)
```

time: 174 us -> 144 us (0.83)
  the two profiles are of different devices: /device:TPU:24 before, /device:TPU:70 now
where the time goes in v2:
time: 144 us; the launch traced here: 143 us
  starting transfers between devices  43.8 us (30%)
  Pallas kernels  41.8 us (29%)
  waiting for transfers between devices  22.7 us (16%)
  between operations  15.3 us (11%)
  blocking collectives  12.8 us (9%)
  local copies, waits for them, and re-layouts  4.91 us (3%)
  other arithmetic  2.22 us (2%)
    ppermute x12, starting transfers between devices, ring(): lax.ppermute(block, axis, [(i, (i + shift) % count) for i in range(count)])  43.8 us
    pallas_call x3, Pallas kernels, back(): pl.pallas_call(functools.partial(back_kernel, sets, trash, finish), out_s...  23.1 us
    pallas_call x2, Pallas kernels, forward(): pl.pallas_call(functools.partial(forward_kernel, sets), out_shape=one * s...  15.7 us
    ppermute x12, waiting for transfers between devices, ring(): lax.ppermute(block, axis, [(i, (i + shift) % count) for i in range(count)])  15.5 us
    all_gather x1, blocking collectives, shards(): four = lax.all_gather(share, 'x', axis=0, tiled=False)  12.8 us
    all_gather x1, waiting for transfers between devices, shards(): lax.all_gather(jnp.concatenate(pieces, axis=0), ('zh', 'zl', 'core'), axi...  7.18 us
  transfers between devices with their start and end apart: 13, of which 6 were waited for; matrix products, arithmetic and copies ran while one was open for 1% of the time, Pallas kernels for 22%

profile of v2, /device:TPU:70, one launch (start us, length us, event | category | flops | bytes accessed | tf_op | source)
XLA Modules:
  0.0 143.4 jit_solution(4553635288111534816)
XLA Ops:
  6.5 0.8 reshape.44
  7.4 0.8 reshape.43
  8.2 0.8 reshape.41
  9.1 12.8 %all-gather.2 = bf16[4,356,128]{2,1,0:T(8,128)(2,1)S(1)} all-gather(bf16[1,356,128]{2,1,0:T(8,128)(2,1)S(1)} %maximum_bitcast_fusion), channel_id=2, replica_groups=mesh['gx'=8,'zh'=4,'core'=2,'x'=4,'zl'=2] {'x'}, dimensions={0}, use_global_device_ids=true | all-gather | bytes 455680 | tf_op jit(solution)/shard_map/all_gather | solution.py:318
  22.1 0.8 pad_maximum_fusion
  22.9 0.7 shard_map.163
  23.5 6.6 %collective-permute-start = (bf16[4,56,128]{2,1,0:T(8,128)(2,1)S(1)}, bf16[4,56,128]{2,1,0:T(8,128)(2,1)S(1)}, u32[]{:S(2)}, u32[]{:S(2)}) collective-permute-start(bf16[4,56,128]{2,1,0:T(8,128)(2,1)S(1)} %get-tuple-element.29), channel_id=1, source_target_pairs={{0,1},{1,2},{2,3},{3,4},{4,5},{5,6},{6,7},{7,0},{8,9},{9,10},{10,1... | collective-permute-start | bytes 172040 | tf_op jit(solution)/shard_map/ppermute | solution.py:292
  30.1 1.9 %collective-permute-start.1 = (bf16[4,56,128]{2,1,0:T(8,128)(2,1)S(1)}, bf16[4,56,128]{2,1,0:T(8,128)(2,1)S(1)}, u32[]{:S(2)}, u32[]{:S(2)}) collective-permute-start(bf16[4,56,128]{2,1,0:T(8,128)(2,1)S(1)} %get-tuple-element.29), channel_id=1, source_target_pairs={{0,7},{1,0},{2,1},{3,2},{4,3},{5,4},{6,5},{7,6},{8,15},{9,8},{10,9... | collective-permute-start | bytes 172040 | tf_op jit(solution)/shard_map/ppermute | solution.py:292
  33.4 0.8 shard_map.164.refs_7_.refs_6_.refs_4_
  34.2 1.3 copy-done
  35.6 2.7 %collective-permute-done.1 = bf16[4,56,128]{2,1,0:T(8,128)(2,1)S(1)} collective-permute-done((bf16[4,56,128]{2,1,0:T(8,128)(2,1)S(1)}, bf16[4,56,128]{2,1,0:T(8,128)(2,1)S(1)}, u32[]{:S(2)}, u32[]{:S(2)}) %collective-permute-start.1) | collective-permute-done | bytes 57376 | tf_op jit(solution)/shard_map/ppermute | solution.py:292
  38.3 1.9 %collective-permute-start.2 = (bf16[12,56,128]{2,1,0:T(8,128)(2,1)S(1)}, bf16[12,56,128]{2,1,0:T(8,128)(2,1)S(1)}, u32[]{:S(2)}, u32[]{:S(2)}) collective-permute-start(bf16[12,56,128]{2,1,0:T(8,128)(2,1)S(1)} %constant_dynamic-update-slice_fusion.refs_11_), channel_id=1, source_target_pairs={{0,8},{8,16},{16,24},{24,32},{32,40},{40,48},{48,56},{56,0},{1,9},... | collective-permute-start | bytes 516104 | tf_op jit(solution)/shard_map/ppermute | solution.py:292
  40.8 5.7 %collective-permute-start.3 = (bf16[12,56,128]{2,1,0:T(8,128)(2,1)S(1)}, bf16[12,56,128]{2,1,0:T(8,128)(2,1)S(1)}, u32[]{:S(2)}, u32[]{:S(2)}) collective-permute-start(bf16[12,56,128]{2,1,0:T(8,128)(2,1)S(1)} %constant_dynamic-update-slice_fusion.refs_11_), channel_id=1, source_target_pairs={{0,56},{8,0},{16,8},{24,16},{32,24},{40,32},{48,40},{56,48},{1,57}... | collective-permute-start | bytes 516104 | tf_op jit(solution)/shard_map/ppermute | solution.py:292
  46.6 8.8 %shard_map.165 = (bf16[128,1024]{1,0:T(8,128)(2,1)}, bf16[2,128,1536]{2,1,0:T(8,128)(2,1)}, bf16[2,128,1280]{2,1,0:T(8,128)(2,1)}, bf16[128,1024]{1,0:T(8,128)(2...) custom-call(s32[1]{0:T(128)} %bitcast.42.refs_0_, s32[1]{0:T(128)} %bitcast.40.refs_1_, s32[128]{0:T(128)} %bitcast.66, ...), custom_call_target="tpu_custom_call" | custom-call | tf_op jit(solution)/shard_map/pallas_call | solution.py:163
  55.6 1.9 %collective-permute-start.4 = (bf16[36,56,128]{2,1,0:T(8,128)(2,1)S(1)}, bf16[36,56,128]{2,1,0:T(8,128)(2,1)S(1)}, u32[]{:S(2)}, u32[]{:S(2)}) collective-permute-start(bf16[36,56,128]{2,1,0:T(8,128)(2,1)S(1)} %constant_dynamic-update-slice_fusion.3), channel_id=1, source_target_pairs={{0,64},{64,128},{128,192},{192,256},{256,320},{320,384},{384,448},... | collective-permute-start | bytes 1548296 | tf_op jit(solution)/shard_map/ppermute | solution.py:292
  57.5 5.1 %collective-permute-start.5 = (bf16[36,56,128]{2,1,0:T(8,128)(2,1)S(1)}, bf16[36,56,128]{2,1,0:T(8,128)(2,1)S(1)}, u32[]{:S(2)}, u32[]{:S(2)}) collective-permute-start(bf16[36,56,128]{2,1,0:T(8,128)(2,1)S(1)} %constant_dynamic-update-slice_fusion.3), channel_id=1, source_target_pairs={{0,448},{64,0},{128,64},{192,128},{256,192},{320,256},{384,320},{4... | collective-permute-start | bytes 1548296 | tf_op jit(solution)/shard_map/ppermute | solution.py:292
  62.6 6.4 %collective-permute-done.4 = bf16[36,56,128]{2,1,0:T(8,128)(2,1)S(1)} collective-permute-done((bf16[36,56,128]{2,1,0:T(8,128)(2,1)S(1)}, bf16[36,56,128]{2,1,0:T(8,128)(2,1)S(1)}, u32[]{:S(2)}, u32[]{:S(2)}) %collective-permute-start.4) | collective-permute-done | bytes 516128 | tf_op jit(solution)/shard_map/ppermute | solution.py:292
  69.2 1.2 collective-permute-done.5
  70.4 7.2 %all-gather.5.cloned.1.call-done = bf16[22784,128]{1,0:T(8,128)(2,1)} async-done(((bf16[1424,128]{1,0:T(8,128)(2,1)}), bf16[22784,128]{1,0:T(8,128)(2,1)}) %all-gather.5.cloned.1.call-update) | async-done | bytes 5832720 | tf_op jit(solution)/shard_map/all_gather | solution.py:325
  77.6 8.1 %shard_map.166 = (bf16[36,56,128]{2,1,0:T(8,128)(2,1)}, f32[36,56,128]{2,1,0:T(8,128)}, bf16[36,56,128]{2,1,0:T(8,128)(2,1)}) custom-call(s32[1]{0:T(128)} %bitcast.43.refs_0_, s32[128]{0:T(128)} %get-tuple-element.58.refs_4_.refs_1_, s32[128]{0:T(128)} %bitcast.64, bf16[128,1024]{1,0:T(8,128)(2,1)} %get-tuple-element.37.refs_3_, ...), custom_call_target="tpu_custom_call" | custom-call | tf_op jit(solution)/shard_map/pallas_call | solution.py:259
  85.7 3.4 %collective-permute-start.7 = (bf16[36,56,128]{2,1,0:T(8,128)(2,1)}, bf16[36,56,128]{2,1,0:T(8,128)(2,1)S(1)}, u32[]{:S(2)}, u32[]{:S(2)}) collective-permute-start(bf16[36,56,128]{2,1,0:T(8,128)(2,1)} %get-tuple-element.43), channel_id=1, source_target_pairs={{0,64},{64,128},{128,192},{192,256},{256,320},{320,384},{384,448},... | collective-permute-start | bytes 1548296 | tf_op jit(solution)/shard_map/ppermute | solution.py:292
  89.0 3.7 %collective-permute-start.6 = (bf16[36,56,128]{2,1,0:T(8,128)(2,1)}, bf16[36,56,128]{2,1,0:T(8,128)(2,1)S(1)}, u32[]{:S(2)}, u32[]{:S(2)}) collective-permute-start(bf16[36,56,128]{2,1,0:T(8,128)(2,1)} %get-tuple-element.41.refs_8_), channel_id=1, source_target_pairs={{0,448},{64,0},{128,64},{192,128},{256,192},{320,256},{384,320},{4... | collective-permute-start | bytes 1548296 | tf_op jit(solution)/shard_map/ppermute | solution.py:292
  92.7 7.3 %shard_map.167.refs_8_.gathered_in = f32[32,56,128]{2,1,0:T(8,128)} custom-call(s32[1]{0:T(128)} %bitcast.41.refs_0_, s32[128]{0:T(128)} %bitcast.63, s32[128]{0:T(128)} %bitcast.69, bf16[128,1024]{1,0:T(8,128)(2,1)} %get-tuple-element.34.refs_3_, bf16[2,128,1536]{2,1,0:T(8,128)(2,1)} %get-tuple-element.35.refs_4_, ...), custom_call_target="tpu_custom_call" | custom-call | tf_op jit(solution)/shard_map/pallas_call | solution.py:259
  100.1 6.8 %shard_map.168 = (bf16[128,1024]{1,0:T(8,128)(2,1)}, bf16[2,128,1536]{2,1,0:T(8,128)(2,1)}, bf16[2,128,1280]{2,1,0:T(8,128)(2,1)}) custom-call(s32[1]{0:T(128)} %bitcast.44.refs_0_, s32[128]{0:T(128)} %bitcast.65, s32[128]{0:T(128)} %get-tuple-element.57.refs_2_.refs_1_, bf16[108,56,128]{2,1,0:T(8,128)(2,1)} %copy-done.8, bf16[256,32,56]{2,1,0:T(8,128)(2,1)} %copy-done, ...), custom_call_target="tpu_custom_call" | custom-call | tf_op jit(solution)/shard_map/pallas_call | solution.py:163
  107.3 1.9 %collective-permute-start.9 = (bf16[12,56,128]{2,1,0:T(8,128)(2,1)S(1)}, bf16[12,56,128]{2,1,0:T(8,128)(2,1)S(1)}, u32[]{:S(2)}, u32[]{:S(2)}) collective-permute-start(bf16[12,56,128]{2,1,0:T(8,128)(2,1)S(1)} %get-tuple-element.54), channel_id=1, source_target_pairs={{0,8},{8,16},{16,24},{24,32},{32,40},{40,48},{48,56},{56,0},{1,9},... | collective-permute-start | bytes 516104 | tf_op jit(solution)/shard_map/ppermute | solution.py:292
  109.2 5.8 %collective-permute-start.8 = (bf16[12,56,128]{2,1,0:T(8,128)(2,1)S(1)}, bf16[12,56,128]{2,1,0:T(8,128)(2,1)S(1)}, u32[]{:S(2)}, u32[]{:S(2)}) collective-permute-start(bf16[12,56,128]{2,1,0:T(8,128)(2,1)S(1)} %get-tuple-element.53), channel_id=1, source_target_pairs={{0,56},{8,0},{16,8},{24,16},{32,24},{40,32},{48,40},{56,48},{1,57}... | collective-permute-start | bytes 516104 | tf_op jit(solution)/shard_map/ppermute | solution.py:292
  115.0 7.7 %shard_map.169.gathered_x = f32[32,56,128]{2,1,0:T(8,128)} custom-call(s32[1]{0:T(128)} %bitcast.45.refs_0_, s32[128]{0:T(128)} %get-tuple-element.57.refs_2_.refs_1_, s32[128]{0:T(128)} %bitcast.67, bf16[128,1024]{1,0:T(8,128)(2,1)} %get-tuple-element.48.refs_3_, bf16[2,128,1536]{2,1,0:T(8,128)(2,1)} %get-tuple-element.49.refs_4_, ...), custom_call_target="tpu_custom_call" | custom-call | tf_op jit(solution)/shard_map/pallas_call | solution.py:259
  122.7 1.2 convert_add_fusion.1
  123.9 2.8 %collective-permute-start.11 = (bf16[4,56,128]{2,1,0:T(8,128)(2,1)S(1)}, bf16[4,56,128]{2,1,0:T(8,128)(2,1)S(1)}, u32[]{:S(2)}, u32[]{:S(2)}) collective-permute-start(bf16[4,56,128]{2,1,0:T(8,128)(2,1)S(1)} %get-tuple-element.56), channel_id=1, source_target_pairs={{0,1},{1,2},{2,3},{3,4},{4,5},{5,6},{6,7},{7,0},{8,9},{9,10},{10,1... | collective-permute-start | bytes 172040 | tf_op jit(solution)/shard_map/ppermute | solution.py:292
  126.8 3.0 %collective-permute-start.10 = (bf16[4,56,128]{2,1,0:T(8,128)(2,1)S(1)}, bf16[4,56,128]{2,1,0:T(8,128)(2,1)S(1)}, u32[]{:S(2)}, u32[]{:S(2)}) collective-permute-start(bf16[4,56,128]{2,1,0:T(8,128)(2,1)S(1)} %get-tuple-element.55), channel_id=1, source_target_pairs={{0,7},{1,0},{2,1},{3,2},{4,3},{5,4},{6,5},{7,6},{8,15},{9,8},{10,9... | collective-permute-start | bytes 172040 | tf_op jit(solution)/shard_map/ppermute | solution.py:292
  130.1 4.9 %collective-permute-done.10 = bf16[4,56,128]{2,1,0:T(8,128)(2,1)S(1)} collective-permute-done((bf16[4,56,128]{2,1,0:T(8,128)(2,1)S(1)}, bf16[4,56,128]{2,1,0:T(8,128)(2,1)S(1)}, u32[]{:S(2)}, u32[]{:S(2)}) %collective-permute-start.10) | collective-permute-done | bytes 57376 | tf_op jit(solution)/shard_map/ppermute | solution.py:292
  135.0 1.5 %shard_map.170 = bf16[49,32,128]{2,1,0:T(8,128)(2,1)} custom-call(s32[4]{0:T(128)S(1)} %bitcast.49, bf16[49,32,128]{2,1,0:T(8,128)(2,1)S(1)} %bitcast.47, f32[32,56,128]{2,1,0:T(8,128)S(1)} %copy-done.1, f32[32,56,128]{2,1,0:T(8,128)S(1)} %copy-done.2, f32[4,56,128]{2,1,0:T(8,128)S(1)} %convert_add_fusion.2.returned), custom_call_target="tpu_custom_call" | custom-call | tf_op jit(solution)/shard_map/pallas_call | solution.py:397
  (66 shorter events, 1.8 us)
Async XLA Ops:
  6.5 71.1 %all-gather.5.cloned.1.call-start = ((), (), s32[]{:S(2)}) async-start(), calls=%async_computation | async-start | bytes 6197248 | tf_op jit(solution)/shard_map/all_gather | solution.py:325
  21.8 1.0 copy-start.3
  21.8 1.0 copy-start.6
  21.9 11.5 %copy-start.4 = (bf16[49,49,256]{2,1,0:T(8,128)(2,1)S(1)}, bf16[49,49,256]{2,1,0:T(8,128)(2,1)}, u32[]{:S(2)}) copy-start(bf16[49,49,256]{2,1,0:T(8,128)(2,1)} %rotations.1) | copy-start | bytes 3687940
  23.5 10.7 %copy-start.5 = (bf16[32,56,128]{2,1,0:T(8,128)(2,1)}, bf16[32,56,128]{2,1,0:T(8,128)(2,1)S(1)}, u32[]{:S(2)}) copy-start(bf16[32,56,128]{2,1,0:T(8,128)(2,1)S(1)} %get-tuple-element.30.refs_6_) | copy-start | bytes 1376260
  23.5 12.0 %collective-permute-start = (bf16[4,56,128]{2,1,0:T(8,128)(2,1)S(1)}, bf16[4,56,128]{2,1,0:T(8,128)(2,1)S(1)}, u32[]{:S(2)}, u32[]{:S(2)}) collective-permute-start(bf16[4,56,128]{2,1,0:T(8,128)(2,1)S(1)} %get-tuple-element.29), channel_id=1, source_target_pairs={{0,1},{1,2},{2,3},{3,4},{4,5},{5,6},{6,7},{7,0},{8,9},{9,10},{10,1... | collective-permute-start | bytes 172040 | tf_op jit(solution)/shard_map/ppermute | solution.py:292
  30.1 8.2 %collective-permute-start.1 = (bf16[4,56,128]{2,1,0:T(8,128)(2,1)S(1)}, bf16[4,56,128]{2,1,0:T(8,128)(2,1)S(1)}, u32[]{:S(2)}, u32[]{:S(2)}) collective-permute-start(bf16[4,56,128]{2,1,0:T(8,128)(2,1)S(1)} %get-tuple-element.29), channel_id=1, source_target_pairs={{0,7},{1,0},{2,1},{3,2},{4,3},{5,4},{6,5},{7,6},{8,15},{9,8},{10,9... | collective-permute-start | bytes 172040 | tf_op jit(solution)/shard_map/ppermute | solution.py:292
  33.4 6.9 %copy-start.11 = (s32[1,1,1,2,128]{4,3,2,1,0:T(2,128)S(1)}, s32[1,1,1,2,128]{4,3,2,1,0:T(2,128)}, u32[]{:S(2)}) copy-start(s32[1,1,1,2,128]{4,3,2,1,0:T(2,128)} %param.25) | copy-start | bytes 3076
  34.2 1.4 copy-start
  38.3 8.2 %copy-start.10 = (bf16[12,56,128]{2,1,0:T(8,128)(2,1)}, bf16[12,56,128]{2,1,0:T(8,128)(2,1)S(1)}, u32[]{:S(2)}) copy-start(bf16[12,56,128]{2,1,0:T(8,128)(2,1)S(1)} %constant_dynamic-update-slice_fusion.refs_11_) | copy-start | bytes 516100
  38.3 17.1 %collective-permute-start.2 = (bf16[12,56,128]{2,1,0:T(8,128)(2,1)S(1)}, bf16[12,56,128]{2,1,0:T(8,128)(2,1)S(1)}, u32[]{:S(2)}, u32[]{:S(2)}) collective-permute-start(bf16[12,56,128]{2,1,0:T(8,128)(2,1)S(1)} %constant_dynamic-update-slice_fusion.refs_11_), channel_id=1, source_target_pairs={{0,8},{8,16},{16,24},{24,32},{32,40},{40,48},{48,56},{56,0},{1,9},... | collective-permute-start | bytes 516104 | tf_op jit(solution)/shard_map/ppermute | solution.py:292
  40.8 14.7 %collective-permute-start.3 = (bf16[12,56,128]{2,1,0:T(8,128)(2,1)S(1)}, bf16[12,56,128]{2,1,0:T(8,128)(2,1)S(1)}, u32[]{:S(2)}, u32[]{:S(2)}) collective-permute-start(bf16[12,56,128]{2,1,0:T(8,128)(2,1)S(1)} %constant_dynamic-update-slice_fusion.refs_11_), channel_id=1, source_target_pairs={{0,56},{8,0},{16,8},{24,16},{32,24},{40,32},{48,40},{56,48},{1,57}... | collective-permute-start | bytes 516104 | tf_op jit(solution)/shard_map/ppermute | solution.py:292
  55.6 13.5 %collective-permute-start.4 = (bf16[36,56,128]{2,1,0:T(8,128)(2,1)S(1)}, bf16[36,56,128]{2,1,0:T(8,128)(2,1)S(1)}, u32[]{:S(2)}, u32[]{:S(2)}) collective-permute-start(bf16[36,56,128]{2,1,0:T(8,128)(2,1)S(1)} %constant_dynamic-update-slice_fusion.3), channel_id=1, source_target_pairs={{0,64},{64,128},{128,192},{192,256},{256,320},{320,384},{384,448},... | collective-permute-start | bytes 1548296 | tf_op jit(solution)/shard_map/ppermute | solution.py:292
  57.5 12.8 %collective-permute-start.5 = (bf16[36,56,128]{2,1,0:T(8,128)(2,1)S(1)}, bf16[36,56,128]{2,1,0:T(8,128)(2,1)S(1)}, u32[]{:S(2)}, u32[]{:S(2)}) collective-permute-start(bf16[36,56,128]{2,1,0:T(8,128)(2,1)S(1)} %constant_dynamic-update-slice_fusion.3), channel_id=1, source_target_pairs={{0,448},{64,0},{128,64},{192,128},{256,192},{320,256},{384,320},{4... | collective-permute-start | bytes 1548296 | tf_op jit(solution)/shard_map/ppermute | solution.py:292
  70.4 7.2 %copy-start.8 = (bf16[108,56,128]{2,1,0:T(8,128)(2,1)}, bf16[108,56,128]{2,1,0:T(8,128)(2,1)S(1)}, u32[]{:S(2)}) copy-start(bf16[108,56,128]{2,1,0:T(8,128)(2,1)S(1)} %constant_dynamic-update-slice_fusion.8.refs_8_.refs_3_) | copy-start | bytes 4644868
  85.7 21.3 %collective-permute-start.7 = (bf16[36,56,128]{2,1,0:T(8,128)(2,1)}, bf16[36,56,128]{2,1,0:T(8,128)(2,1)S(1)}, u32[]{:S(2)}, u32[]{:S(2)}) collective-permute-start(bf16[36,56,128]{2,1,0:T(8,128)(2,1)} %get-tuple-element.43), channel_id=1, source_target_pairs={{0,64},{64,128},{128,192},{192,256},{256,320},{320,384},{384,448},... | collective-permute-start | bytes 1548296 | tf_op jit(solution)/shard_map/ppermute | solution.py:292
  89.0 17.9 %collective-permute-start.6 = (bf16[36,56,128]{2,1,0:T(8,128)(2,1)}, bf16[36,56,128]{2,1,0:T(8,128)(2,1)S(1)}, u32[]{:S(2)}, u32[]{:S(2)}) collective-permute-start(bf16[36,56,128]{2,1,0:T(8,128)(2,1)} %get-tuple-element.41.refs_8_), channel_id=1, source_target_pairs={{0,448},{64,0},{128,64},{192,128},{256,192},{320,256},{384,320},{4... | collective-permute-start | bytes 1548296 | tf_op jit(solution)/shard_map/ppermute | solution.py:292
  100.1 6.9 %copy-start.9 = (f32[36,56,128]{2,1,0:T(8,128)S(1)}, f32[36,56,128]{2,1,0:T(8,128)}, u32[]{:S(2)}) copy-start(f32[36,56,128]{2,1,0:T(8,128)} %get-tuple-element.42) | copy-start | bytes 3096580
  107.1 7.8 %copy-start.7 = (f32[36,56,128]{2,1,0:T(8,128)}, f32[36,56,128]{2,1,0:T(8,128)S(1)}, u32[]{:S(2)}) copy-start(f32[36,56,128]{2,1,0:T(8,128)S(1)} %convert_add_fusion.refs_8_) | copy-start | bytes 3096580
  107.3 15.4 %collective-permute-start.9 = (bf16[12,56,128]{2,1,0:T(8,128)(2,1)S(1)}, bf16[12,56,128]{2,1,0:T(8,128)(2,1)S(1)}, u32[]{:S(2)}, u32[]{:S(2)}) collective-permute-start(bf16[12,56,128]{2,1,0:T(8,128)(2,1)S(1)} %get-tuple-element.54), channel_id=1, source_target_pairs={{0,8},{8,16},{16,24},{24,32},{32,40},{40,48},{48,56},{56,0},{1,9},... | collective-permute-start | bytes 516104 | tf_op jit(solution)/shard_map/ppermute | solution.py:292
  109.2 13.5 %collective-permute-start.8 = (bf16[12,56,128]{2,1,0:T(8,128)(2,1)S(1)}, bf16[12,56,128]{2,1,0:T(8,128)(2,1)S(1)}, u32[]{:S(2)}, u32[]{:S(2)}) collective-permute-start(bf16[12,56,128]{2,1,0:T(8,128)(2,1)S(1)} %get-tuple-element.53), channel_id=1, source_target_pairs={{0,56},{8,0},{16,8},{24,16},{32,24},{40,32},{48,40},{56,48},{1,57}... | collective-permute-start | bytes 516104 | tf_op jit(solution)/shard_map/ppermute | solution.py:292
  122.7 12.3 %copy-start.1 = (f32[32,56,128]{2,1,0:T(8,128)S(1)}, f32[32,56,128]{2,1,0:T(8,128)}, u32[]{:S(2)}) copy-start(f32[32,56,128]{2,1,0:T(8,128)} %shard_map.167.refs_8_.gathered_in) | copy-start | bytes 2752516
  122.7 12.3 %copy-start.2 = (f32[32,56,128]{2,1,0:T(8,128)S(1)}, f32[32,56,128]{2,1,0:T(8,128)}, u32[]{:S(2)}) copy-start(f32[32,56,128]{2,1,0:T(8,128)} %shard_map.169.gathered_x) | copy-start | bytes 2752516
  123.9 6.2 %collective-permute-start.11 = (bf16[4,56,128]{2,1,0:T(8,128)(2,1)S(1)}, bf16[4,56,128]{2,1,0:T(8,128)(2,1)S(1)}, u32[]{:S(2)}, u32[]{:S(2)}) collective-permute-start(bf16[4,56,128]{2,1,0:T(8,128)(2,1)S(1)} %get-tuple-element.56), channel_id=1, source_target_pairs={{0,1},{1,2},{2,3},{3,4},{4,5},{5,6},{6,7},{7,0},{8,9},{9,10},{10,1... | collective-permute-start | bytes 172040 | tf_op jit(solution)/shard_map/ppermute | solution.py:292
  126.8 8.2 %collective-permute-start.10 = (bf16[4,56,128]{2,1,0:T(8,128)(2,1)S(1)}, bf16[4,56,128]{2,1,0:T(8,128)(2,1)S(1)}, u32[]{:S(2)}, u32[]{:S(2)}) collective-permute-start(bf16[4,56,128]{2,1,0:T(8,128)(2,1)S(1)} %get-tuple-element.55), channel_id=1, source_target_pairs={{0,7},{1,0},{2,1},{3,2},{4,3},{5,4},{6,5},{7,6},{8,15},{9,8},{10,9... | collective-permute-start | bytes 172040 | tf_op jit(solution)/shard_map/ppermute | solution.py:292
Sparse Core Ops, SparseCore 0:
  23.0 54.5 all-gather.4

commit v3 on v2

--- a/solution.py
+++ b/solution.py
@@ -103,17 +103,19 @@
     return (count + (STEP - 1)) // STEP
 
 
-def forward_kernel(sets, *refs):
+def forward_kernel(sets, parts, *refs):
     counts, sources, picked = refs[0:sets], refs[sets : 2 * sets], refs[2 * sets : 3 * sets]
-    x_ref, rot_ref = refs[3 * sets : 3 * sets + 2]
-    spread_refs = refs[3 * sets + 2 : 3 * sets + 5]
-    outs, (tmp, sp0, sp1, sp2, sems) = refs[3 * sets + 6 : -5], refs[-5:]
-    copies = [
-        pltpu.make_async_copy(source, target, sems.at[n])
-        for n, (source, target) in enumerate(zip(spread_refs, (sp0, sp1, sp2), strict=True))
-    ]
+    refs = refs[3 * sets :]
+    part_refs, table, spread_refs = refs[0:parts], refs[parts], refs[parts + 1 : parts + 4]
+    outs, (tmp, x_ref, rot_ref, sp0, sp1, sp2, sems) = refs[parts + 5 : -7], refs[-7:]
+    rows = x_ref.shape[0] // parts
+    moves = [(part, x_ref.at[pl.ds(n * rows, rows)]) for n, part in enumerate(part_refs)]
+    moves += [(table, rot_ref), *zip(spread_refs, (sp0, sp1, sp2), strict=True)]
+    copies = [pltpu.make_async_copy(src, dst, sems.at[n]) for n, (src, dst) in enumerate(moves)]
     for copy in copies:
         copy.start()
+    for copy in copies[:-3]:
+        copy.wait()
 
     def spread(planes, matrix):
         return jnp.dot(jnp.concatenate(planes, axis=1), matrix, preferred_element_type=F32).astype(BF16)
@@ -134,7 +136,7 @@
             return tmp[i, pl.ds(n * PITCH, EDGES), :].astype(BF16)
 
         if i == 0:
-            for copy in copies:
+            for copy in copies[-3:]:
                 copy.wait()
         zero = [plane(n) for n in range(7)]
         t0[:, 0:512] = spread(zero[0:4], sp0[0])
@@ -153,7 +155,7 @@
             t2[1, :, 640 * h : 640 * (h + 1)] = spread(q + p, sp2[h])
 
 
-def forward(counts, sources, picked, x, table, sp, after):
+def forward(counts, sources, picked, parts, table, sp, after):
     sets = len(counts)
     one = (
         jax.ShapeDtypeStruct((EDGES, 64 * ROWS0), BF16),
@@ -161,15 +163,19 @@
         jax.ShapeDtypeStruct((2, EDGES, 64 * ROWS2), BF16),
     )
     outs = pl.pallas_call(
-        functools.partial(forward_kernel, sets),
+        functools.partial(forward_kernel, sets, len(parts)),
         out_shape=one * sets,
-        in_specs=[SMEM] * (3 * sets) + [VMEM] * 2 + [HBM] * 3 + [ANY],
+        in_specs=[SMEM] * (3 * sets) + [HBM] * (len(parts) + 4) + [ANY],
         out_specs=(VMEM,) * (3 * sets),
-        scratch_shapes=[pltpu.VMEM((sets, KP * PITCH, LANES), F32)]
+        scratch_shapes=[
+            pltpu.VMEM((sets, KP * PITCH, LANES), F32),
+            pltpu.VMEM((len(parts) * parts[0].shape[0], JP, LANES), BF16),
+            pltpu.VMEM((ROTS, KP, JP), BF16),
+        ]
         + [pltpu.VMEM(m.shape, BF16) for m in sp]
-        + [pltpu.SemaphoreType.DMA((3,))],
+        + [pltpu.SemaphoreType.DMA((len(parts) + 4,))],
         compiler_params=WIDE,
-    )(*counts, *sources, *picked, x, table, *sp, after)
+    )(*counts, *sources, *picked, *parts, table, *sp, after)
     return [outs[3 * i : 3 * i + 3] for i in range(sets)]
 
 
@@ -244,10 +250,10 @@
     finish(acc, *outs)
 
 
-def store_returned(acc, low, middle, high):
-    low[...] = acc[0:36].astype(BF16)
+def store_returned(acc, first, middle, last):
+    first[...] = acc[0:36].astype(BF16)
     middle[...] = acc[36:72]
-    high[...] = acc[72:108].astype(BF16)
+    last[...] = acc[72:108].astype(BF16)
 
 
 def store_gathered(acc, out):
@@ -277,9 +283,9 @@
     )(*counts, *picked, *targets, *[t for one in turned for t in one], table, gathered, after)
 
 
-def final_kernel(border_atoms, feats, gathered_in, gathered_x, returned, out, acc):
+def final_kernel(border_atoms, feats, gathered, returned, out, acc):
     for a in range(ATOMS):
-        acc[pl.ds(a * 57, JP), :] = gathered_in[a] + gathered_x[a]
+        acc[pl.ds(a * 57, JP), :] = gathered[a]
     for t in range(BOUND):
         acc[pl.ds(border_atoms[t] * 57, JP), :] += returned[t]
     for j in range(HARM):
@@ -287,9 +293,32 @@
         out[j] = (feats[j].astype(F32) + 0.25 * total).astype(BF16)
 
 
-def ring(axis, block, shift):
+def swap(axis, block, odd):
     count = lax.axis_size(axis)
-    return lax.ppermute(block, axis, [(i, (i + shift) % count) for i in range(count)])
+    return lax.ppermute(block, axis, [(i, (i + (1 if (i + odd) % 2 == 0 else -1)) % count) for i in range(count)])
+
+
+def exchange(axis, first, last):
+    last = swap(axis, last, 1)
+    if axis == GY:
+        both = lax.all_gather(first, "core", axis=0, tiled=False)
+        return jnp.where(lax.axis_index("core") == 0, both[1], both[0]), last
+    return swap(axis, first, 0), last
+
+
+def widen(axis, block):
+    first, last = exchange(axis, block, block)
+    return jnp.concatenate([first, block, last], axis=0)
+
+
+def fold(axis, first, middle, last):
+    first, last = exchange(axis, first, last)
+    return middle + first.astype(F32) + last.astype(F32)
+
+
+def thirds(block):
+    third = block.shape[0] // 3
+    return block[:third].astype(BF16), block[third : 2 * third], block[2 * third :].astype(BF16)
 
 
 GX, GY, GZ = "gx", ("zh", "core"), ("x", "zl")
@@ -352,56 +381,46 @@
     source_in, target_in, rot_in = inner_source[0, 0, 0], inner_target[0, 0, 0], inner_rotation[0, 0, 0]
     far_rows, target_x = cross_source[0, 0, 0], cross_target[0, 0, 0]
     rot_inward, rot_outward = cross_rotation[0, 0, 0, 0], cross_rotation[0, 0, 0, 1]
-
-    def widen(axis, block):
-        return jnp.concatenate([ring(axis, block, 1), block, ring(axis, block, -1)], axis=0)
+    def place(axis, offset):
+        return jnp.where(lax.axis_index(axis) % 2 == 1, offset, 2 - offset)
+
+    slot, atom = far_rows // BOUND, far_rows % BOUND
+    far_rows = (place(GX, slot // 9) * 3 + place(GY, slot // 3 % 3)) * 3 + place(GZ, slot % 3)
+    far_rows = far_rows * BOUND + atom
 
     near = widen(GZ, border)
-    turned_out, turned_in = forward(
-        [count_x, count_in], [target_x, source_in], [rot_outward, rot_in], x, table, sp, near
+    [turned_out] = forward([count_x], [target_x], [rot_outward], [x], table, sp, near)
+    near = widen(GY, near)
+    near, turned_out = lax.optimization_barrier((near, turned_out))
+    near_first, near_last = exchange(GX, near, near)
+    [turned_in] = forward([count_in], [source_in], [rot_in], [x], table, sp, near)
+    [turned_x] = forward(
+        [count_x], [far_rows], [rot_inward], [near_first, near, near_last], table, sp, turned_in[0]
     )
-    near = widen(GY, near)
-    near, turned_in = lax.optimization_barrier((near, turned_in))
-    near = widen(GX, near)
 
     face = (36, JP, LANES)
-    inside = (ATOMS, JP, LANES)
-    low, middle, high = back(
-        [count_x], [rot_outward], [far_rows], [turned_out], table, gathered_weights, near, 112, AROUND,
+    first, middle, last = back(
+        [count_x], [rot_outward], [far_rows], [turned_out], table, gathered_weights, turned_x[0], 112, AROUND,
         store_returned,
         (jax.ShapeDtypeStruct(face, BF16), jax.ShapeDtypeStruct(face, F32), jax.ShapeDtypeStruct(face, BF16)),
     )
-
-    def fold(axis, low, middle, high):
-        return middle + ring(axis, low, -1).astype(F32) + ring(axis, high, 1).astype(F32)
-
-    def thirds(block):
-        third = block.shape[0] // 3
-        return block[:third].astype(BF16), block[third : 2 * third], block[2 * third :].astype(BF16)
-
-    gathered_in = back(
-        [count_in], [rot_in], [target_in], [turned_in], table, gathered_weights, low, 40, ATOMS, store_gathered,
-        jax.ShapeDtypeStruct(inside, F32),
+    gathered = back(
+        [count_in, count_x], [rot_in, rot_inward], [target_in, target_x], [turned_in, turned_x], table,
+        gathered_weights, first, 40, ATOMS, store_gathered, jax.ShapeDtypeStruct((ATOMS, JP, LANES), F32),
     )
-    [turned_x] = forward([count_x], [far_rows], [rot_inward], near, table, sp, gathered_in)
-    returned = fold(GX, low, middle, high)
-    returned, turned_x = lax.optimization_barrier((returned, turned_x))
-    gathered_x = back(
-        [count_x], [rot_inward], [target_x], [turned_x], table, gathered_weights, returned, 40, ATOMS,
-        store_gathered, jax.ShapeDtypeStruct(inside, F32),
-    )
+    returned = fold(GX, first, middle, last)
+    returned, gathered = lax.optimization_barrier((returned, gathered))
     returned = fold(GY, *thirds(returned))
-    returned, gathered_x = lax.optimization_barrier((returned, gathered_x))
     returned = fold(GZ, *thirds(returned))
 
     updated = pl.pallas_call(
         final_kernel,
         out_shape=jax.ShapeDtypeStruct((HARM, ATOMS, LANES), BF16),
-        in_specs=[SMEM] + [VMEM] * 4,
+        in_specs=[SMEM] + [VMEM] * 3,
         out_specs=VMEM,
         scratch_shapes=[pltpu.VMEM((ATOMS * 57, LANES), F32)],
         compiler_params=PARAMS,
-    )(border_rows, feats, gathered_in, gathered_x, returned)
+    )(border_rows, feats, gathered, returned)
     return updated.transpose(1, 0, 2).reshape(features.shape)
 
 

time: 144 us -> 139 us (0.965)
  the two profiles are of different devices: /device:TPU:70 before, /device:TPU:24 now
where the time goes in v3:
time: 139 us; the launch traced here: 138 us
  Pallas kernels  40.2 us (29%)
  starting transfers between devices  36.5 us (26%)
  waiting for transfers between devices  19.2 us (14%)
  blocking collectives  18.9 us (14%)
  between operations  15.2 us (11%)
  local copies, waits for them, and re-layouts  6.35 us (5%)
  other arithmetic  1.74 us (1%)
    ppermute x10, starting transfers between devices, swap(): lax.ppermute(block, axis, [(i, (i + (1 if (i + odd) % 2 == 0 else -1)) %...  36.5 us
    ppermute x10, waiting for transfers between devices, swap(): lax.ppermute(block, axis, [(i, (i + (1 if (i + odd) % 2 == 0 else -1)) %...  19.2 us
    pallas_call x3, Pallas kernels, forward(): pl.pallas_call(functools.partial(forward_kernel, sets, len(parts)), out_s...  19 us
    pallas_call x2, Pallas kernels, back(): pl.pallas_call(functools.partial(back_kernel, sets, trash, finish), out_s...  18.3 us
    all_gather x1, blocking collectives, shards(): four = lax.all_gather(share, 'x', axis=0, tiled=False)  13 us
    all_gather x2, blocking collectives, exchange(): both = lax.all_gather(first, 'core', axis=0, tiled=False)  5.91 us
    unnamed x32, local copies, waits for them, and re-layouts  3.07 us
  transfers between devices with their start and end apart: 11, of which 7 were waited for; matrix products, arithmetic and copies ran while one was open for 1% of the time, Pallas kernels for 22%

profile of v3, /device:TPU:24, one launch (start us, length us, event | category | flops | bytes accessed | tf_op | source)
XLA Modules:
  0.0 138.1 jit_solution(1058145147460796748)
XLA Ops:
  6.5 0.8 reshape.46
  7.4 0.8 reshape.49
  8.2 0.8 reshape.48
  9.1 13.0 %all-gather.4 = bf16[4,356,128]{2,1,0:T(8,128)(2,1)S(1)} all-gather(bf16[1,356,128]{2,1,0:T(8,128)(2,1)S(1)} %maximum_bitcast_fusion), channel_id=3, replica_groups=mesh['gx'=8,'zh'=4,'core'=2,'x'=4,'zl'=2] {'x'}, dimensions={0}, use_global_device_ids=true | all-gather | bytes 455680 | tf_op jit(solution)/shard_map/all_gather | solution.py:347
  22.3 0.8 pad_maximum_fusion
  23.8 0.8 copy-done.2
  24.6 6.4 %collective-permute-start.1 = (bf16[4,56,128]{2,1,0:T(8,128)(2,1)S(1)}, bf16[4,56,128]{2,1,0:T(8,128)(2,1)S(1)}, u32[]{:S(2)}, u32[]{:S(2)}) collective-permute-start(bf16[4,56,128]{2,1,0:T(8,128)(2,1)S(1)} %get-tuple-element.25), channel_id=1, source_target_pairs={{0,7},{1,2},{2,1},{3,4},{4,3},{5,6},{6,5},{7,0},{8,15},{9,10},{10,... | collective-permute-start | bytes 172040 | tf_op jit(solution)/shard_map/ppermute | solution.py:298
  31.0 1.9 %collective-permute-start = (bf16[4,56,128]{2,1,0:T(8,128)(2,1)S(1)}, bf16[4,56,128]{2,1,0:T(8,128)(2,1)S(1)}, u32[]{:S(2)}, u32[]{:S(2)}) collective-permute-start(bf16[4,56,128]{2,1,0:T(8,128)(2,1)S(1)} %get-tuple-element.25), channel_id=1, source_target_pairs={{0,1},{1,0},{2,3},{3,2},{4,5},{5,4},{6,7},{7,6},{8,9},{9,8},{10,11... | collective-permute-start | bytes 172040 | tf_op jit(solution)/shard_map/ppermute | solution.py:298
  34.2 0.8 shard_map.164.refs_4_.refs_6_.refs_12_
  35.0 1.3 copy-done
  37.1 5.8 %collective-permute-start.2 = (bf16[12,56,128]{2,1,0:T(8,128)(2,1)S(1)}, bf16[12,56,128]{2,1,0:T(8,128)(2,1)S(1)}, u32[]{:S(2)}, u32[]{:S(2)}) collective-permute-start(bf16[12,56,128]{2,1,0:T(8,128)(2,1)S(1)} %constant_dynamic-update-slice_fusion.refs_8_), channel_id=1, source_target_pairs={{0,56},{8,16},{16,8},{24,32},{32,24},{40,48},{48,40},{56,0},{1,57}... | collective-permute-start | bytes 516104 | tf_op jit(solution)/shard_map/ppermute | solution.py:298
  42.9 6.2 %shard_map.165 = (bf16[128,1024]{1,0:T(8,128)(2,1)}, bf16[2,128,1536]{2,1,0:T(8,128)(2,1)}, bf16[2,128,1280]{2,1,0:T(8,128)(2,1)}) custom-call(s32[1]{0:T(128)} %bitcast.54.refs_0_, s32[128]{0:T(128)} %bitcast.75, s32[128]{0:T(128)} %get-tuple-element.52.refs_2_.refs_1_, bf16[32,56,128]{2,1,0:T(8,128)(2,1)} %copy-done.2, bf16[256,32,56]{2,1,0:T(8,128)(2,1)} %copy-done, ...), custom_call_target="tpu_custom_call" | custom-call | tf_op jit(solution)/shard_map/pallas_call | solution.py:165
  49.2 2.3 %all-gather = bf16[24,56,128]{2,1,0:T(8,128)(2,1)S(1)} all-gather(bf16[12,56,128]{2,1,0:T(8,128)(2,1)} %copy-done.8), channel_id=2, replica_groups=mesh['gx'=8,'zh'=4,'core'=2,'x'=4,'zl'=2] {'core'}, dimensions={0}, use_global_device_ids=true | all-gather | bytes 516096 | tf_op jit(solution)/shard_map/all_gather | solution.py:304
  51.7 4.7 %collective-permute-start.4 = (bf16[36,56,128]{2,1,0:T(8,128)(2,1)S(1)}, bf16[36,56,128]{2,1,0:T(8,128)(2,1)S(1)}, u32[]{:S(2)}, u32[]{:S(2)}) collective-permute-start(bf16[36,56,128]{2,1,0:T(8,128)(2,1)S(1)} %constant_dynamic-update-slice_fusion.3.refs_8_.refs_4_), channel_id=1, source_target_pairs={{0,448},{64,128},{128,64},{192,256},{256,192},{320,384},{384,320},... | collective-permute-start | bytes 1548296 | tf_op jit(solution)/shard_map/ppermute | solution.py:298
  56.4 1.9 %collective-permute-start.3 = (bf16[36,56,128]{2,1,0:T(8,128)(2,1)S(1)}, bf16[36,56,128]{2,1,0:T(8,128)(2,1)S(1)}, u32[]{:S(2)}, u32[]{:S(2)}) collective-permute-start(bf16[36,56,128]{2,1,0:T(8,128)(2,1)S(1)} %constant_dynamic-update-slice_fusion.3.refs_8_.refs_4_), channel_id=1, source_target_pairs={{0,64},{64,0},{128,192},{192,128},{256,320},{320,256},{384,448},{4... | collective-permute-start | bytes 1548296 | tf_op jit(solution)/shard_map/ppermute | solution.py:298
  59.6 6.2 %shard_map.166 = (bf16[128,1024]{1,0:T(8,128)(2,1)}, bf16[2,128,1536]{2,1,0:T(8,128)(2,1)}, bf16[2,128,1280]{2,1,0:T(8,128)(2,1)}) custom-call(s32[1]{0:T(128)} %bitcast.52.refs_0_, s32[128]{0:T(128)} %bitcast.77, s32[128]{0:T(128)} %bitcast.73, bf16[32,56,128]{2,1,0:T(8,128)(2,1)} %copy-done.2, bf16[256,32,56]{2,1,0:T(8,128)(2,1)} %copy-done, ...), custom_call_target="tpu_custom_call" | custom-call | tf_op jit(solution)/shard_map/pallas_call | solution.py:165
  65.8 3.2 %collective-permute-done.4.refs_5_ = bf16[36,56,128]{2,1,0:T(8,128)(2,1)S(1)} collective-permute-done((bf16[36,56,128]{2,1,0:T(8,128)(2,1)S(1)}, bf16[36,56,128]{2,1,0:T(8,128)(2,1)S(1)}, u32[]{:S(2)}, u32[]{:S(2)}) %collective-permute-start.4) | collective-permute-done | bytes 516128 | tf_op jit(solution)/shard_map/ppermute | solution.py:298
  68.9 3.2 %collective-permute-done.3.refs_3_ = bf16[36,56,128]{2,1,0:T(8,128)(2,1)S(1)} collective-permute-done((bf16[36,56,128]{2,1,0:T(8,128)(2,1)S(1)}, bf16[36,56,128]{2,1,0:T(8,128)(2,1)S(1)}, u32[]{:S(2)}, u32[]{:S(2)}) %collective-permute-start.3) | collective-permute-done | bytes 516128 | tf_op jit(solution)/shard_map/ppermute | solution.py:298
  72.1 0.8 copy-done.10
  72.9 6.6 %shard_map.167 = (bf16[128,1024]{1,0:T(8,128)(2,1)}, bf16[2,128,1536]{2,1,0:T(8,128)(2,1)}, bf16[2,128,1280]{2,1,0:T(8,128)(2,1)}) custom-call(s32[1]{0:T(128)} %bitcast.55.refs_0_, s32[128]{0:T(128)} %fusion.3.refs_1_.refs_2_, s32[128]{0:T(128)} %get-tuple-element.51.refs_2_.refs_3_, bf16[36,56,128]{2,1,0:T(8,128)(2,1)} %copy-done.10, ...), custom_call_target="tpu_custom_call" | custom-call | tf_op jit(solution)/shard_map/pallas_call | solution.py:165
  79.5 7.7 %shard_map.168 = (bf16[36,56,128]{2,1,0:T(8,128)(2,1)}, f32[36,56,128]{2,1,0:T(8,128)}, bf16[36,56,128]{2,1,0:T(8,128)(2,1)}) custom-call(s32[1]{0:T(128)} %bitcast.56.refs_0_, s32[128]{0:T(128)} %get-tuple-element.52.refs_2_.refs_1_, s32[128]{0:T(128)} %fusion.3.refs_1_.refs_2_, bf16[128,1024]{1,0:T(8,128)(2,1)} %get-tuple-element.30.refs_3_, ...), custom_call_target="tpu_custom_call" | custom-call | tf_op jit(solution)/shard_map/pallas_call | solution.py:265
  87.3 4.0 %collective-permute-start.6 = (bf16[36,56,128]{2,1,0:T(8,128)(2,1)}, bf16[36,56,128]{2,1,0:T(8,128)(2,1)S(1)}, u32[]{:S(2)}, u32[]{:S(2)}) collective-permute-start(bf16[36,56,128]{2,1,0:T(8,128)(2,1)} %get-tuple-element.38), channel_id=1, source_target_pairs={{0,448},{64,128},{128,64},{192,256},{256,192},{320,384},{384,320},... | collective-permute-start | bytes 1548296 | tf_op jit(solution)/shard_map/ppermute | solution.py:298
  91.2 2.1 %collective-permute-start.5 = (bf16[36,56,128]{2,1,0:T(8,128)(2,1)}, bf16[36,56,128]{2,1,0:T(8,128)(2,1)S(1)}, u32[]{:S(2)}, u32[]{:S(2)}) collective-permute-start(bf16[36,56,128]{2,1,0:T(8,128)(2,1)} %get-tuple-element.37.refs_14_), channel_id=1, source_target_pairs={{0,64},{64,0},{128,192},{192,128},{256,320},{320,256},{384,448},{4... | collective-permute-start | bytes 1548296 | tf_op jit(solution)/shard_map/ppermute | solution.py:298
  93.4 10.5 %shard_map.169.gathered = f32[32,56,128]{2,1,0:T(8,128)} custom-call(s32[1]{0:T(128)} %bitcast.53.refs_0_, s32[1]{0:T(128)} %bitcast.57.refs_1_, s32[128]{0:T(128)} %bitcast.74, s32[128]{0:T(128)} %get-tuple-element.51.refs_2_.refs_3_, s32[128]{0:T(128)} %bitcast.78, s32[128]{0:T(128)} %bitcast.76, bf16[128,1024]{1,0:T(8,128)(2,1)} %get-tuple-element.34.refs_10_.refs_6_, ...), custom_call_target="tpu_custom_call" | custom-call | tf_op jit(solution)/shard_map/pallas_call | solution.py:265
  104.2 2.7 %collective-permute-done.5 = bf16[36,56,128]{2,1,0:T(8,128)(2,1)S(1)} collective-permute-done((bf16[36,56,128]{2,1,0:T(8,128)(2,1)}, bf16[36,56,128]{2,1,0:T(8,128)(2,1)S(1)}, u32[]{:S(2)}, u32[]{:S(2)}) %collective-permute-start.5) | collective-permute-done | bytes 516128 | tf_op jit(solution)/shard_map/ppermute | solution.py:298
  107.3 2.2 %collective-permute-start.7 = (bf16[12,56,128]{2,1,0:T(8,128)(2,1)S(1)}, bf16[12,56,128]{2,1,0:T(8,128)(2,1)S(1)}, u32[]{:S(2)}, u32[]{:S(2)}) collective-permute-start(bf16[12,56,128]{2,1,0:T(8,128)(2,1)S(1)} %get-tuple-element.48), channel_id=1, source_target_pairs={{0,56},{8,16},{16,8},{24,32},{32,24},{40,48},{48,40},{56,0},{1,57}... | collective-permute-start | bytes 516104 | tf_op jit(solution)/shard_map/ppermute | solution.py:298
  109.5 3.6 %all-gather.3 = bf16[24,56,128]{2,1,0:T(8,128)(2,1)S(1)} all-gather(bf16[12,56,128]{2,1,0:T(8,128)(2,1)S(1)} %get-tuple-element.47), channel_id=5, replica_groups=mesh['gx'=8,'zh'=4,'core'=2,'x'=4,'zl'=2] {'core'}, dimensions={0}, use_global_device_ids=true | all-gather | bytes 516096 | tf_op jit(solution)/shard_map/all_gather | solution.py:304
  113.1 4.7 %collective-permute-done.7 = bf16[12,56,128]{2,1,0:T(8,128)(2,1)S(1)} collective-permute-done((bf16[12,56,128]{2,1,0:T(8,128)(2,1)S(1)}, bf16[12,56,128]{2,1,0:T(8,128)(2,1)S(1)}, u32[]{:S(2)}, u32[]{:S(2)}) %collective-permute-start.7) | collective-permute-done | bytes 172064 | tf_op jit(solution)/shard_map/ppermute | solution.py:298
  117.9 3.6 %collective-permute-start.8 = (bf16[4,56,128]{2,1,0:T(8,128)(2,1)S(1)}, bf16[4,56,128]{2,1,0:T(8,128)(2,1)S(1)}, u32[]{:S(2)}, u32[]{:S(2)}) collective-permute-start(bf16[4,56,128]{2,1,0:T(8,128)(2,1)S(1)} %get-tuple-element.49), channel_id=1, source_target_pairs={{0,1},{1,0},{2,3},{3,2},{4,5},{5,4},{6,7},{7,6},{8,9},{9,8},{10,11... | collective-permute-start | bytes 172040 | tf_op jit(solution)/shard_map/ppermute | solution.py:298
  121.5 3.8 %collective-permute-start.9 = (bf16[4,56,128]{2,1,0:T(8,128)(2,1)S(1)}, bf16[4,56,128]{2,1,0:T(8,128)(2,1)S(1)}, u32[]{:S(2)}, u32[]{:S(2)}) collective-permute-start(bf16[4,56,128]{2,1,0:T(8,128)(2,1)S(1)} %get-tuple-element.50), channel_id=1, source_target_pairs={{0,7},{1,2},{2,1},{3,4},{4,3},{5,6},{6,5},{7,0},{8,15},{9,10},{10,... | collective-permute-start | bytes 172040 | tf_op jit(solution)/shard_map/ppermute | solution.py:298
  125.3 4.4 %collective-permute-done.9 = bf16[4,56,128]{2,1,0:T(8,128)(2,1)S(1)} collective-permute-done((bf16[4,56,128]{2,1,0:T(8,128)(2,1)S(1)}, bf16[4,56,128]{2,1,0:T(8,128)(2,1)S(1)}, u32[]{:S(2)}, u32[]{:S(2)}) %collective-permute-start.9) | collective-permute-done | bytes 57376 | tf_op jit(solution)/shard_map/ppermute | solution.py:298
  129.7 1.5 %shard_map.170 = bf16[49,32,128]{2,1,0:T(8,128)(2,1)} custom-call(s32[4]{0:T(128)S(1)} %bitcast.61, bf16[49,32,128]{2,1,0:T(8,128)(2,1)S(1)} %bitcast.59, f32[32,56,128]{2,1,0:T(8,128)S(1)} %copy-done.1, f32[4,56,128]{2,1,0:T(8,128)S(1)} %fusion.2.returned), custom_call_target="tpu_custom_call" | custom-call | tf_op jit(solution)/shard_map/pallas_call | solution.py:416
  (63 shorter events, 3.7 us)
Async XLA Ops:
  6.5 73.0 %all-gather.7.cloned.1.call-start = ((), (), s32[]{:S(2)}) async-start(), calls=%async_computation | async-start | bytes 6197248 | tf_op jit(solution)/shard_map/all_gather | solution.py:354
  9.0 14.1 %copy-start.3 = (bf16[1,1,1,32,49,128]{5,3,4,2,1,0:T(8,128)(2,1)S(1)}, bf16[1,1,1,32,49,128]{5,3,4,2,1,0:T(8,128)(2,1)}, u32[]{:S(2)}) copy-start(bf16[1,1,1,32,49,128]{5,3,4,2,1,0:T(8,128)(2,1)} %param.17) | copy-start | bytes 1204228
  9.0 14.1 %copy-start.5 = (s32[1,1,1,4]{3,2,1,0:T(1,128)S(1)}, s32[1,1,1,4]{3,2,1,0:T(1,128)}, u32[]{:S(2)}) copy-start(s32[1,1,1,4]{3,2,1,0:T(1,128)} %param.18) | copy-start | bytes 52
  9.1 23.8 %copy-start.11 = (s32[1,1,1,2,128]{4,3,2,1,0:T(2,128)S(1)}, s32[1,1,1,2,128]{4,3,2,1,0:T(2,128)}, u32[]{:S(2)}) copy-start(s32[1,1,1,2,128]{4,3,2,1,0:T(2,128)} %param.25) | copy-start | bytes 3076
  9.1 25.1 %copy-start.4 = (bf16[49,49,256]{2,1,0:T(8,128)(2,1)S(1)}, bf16[49,49,256]{2,1,0:T(8,128)(2,1)}, u32[]{:S(2)}) copy-start(bf16[49,49,256]{2,1,0:T(8,128)(2,1)} %rotations.1) | copy-start | bytes 3687940
  23.8 0.8 copy-start.2
  24.6 12.5 %collective-permute-start.1 = (bf16[4,56,128]{2,1,0:T(8,128)(2,1)S(1)}, bf16[4,56,128]{2,1,0:T(8,128)(2,1)S(1)}, u32[]{:S(2)}, u32[]{:S(2)}) collective-permute-start(bf16[4,56,128]{2,1,0:T(8,128)(2,1)S(1)} %get-tuple-element.25), channel_id=1, source_target_pairs={{0,7},{1,2},{2,1},{3,4},{4,3},{5,6},{6,5},{7,0},{8,15},{9,10},{10,... | collective-permute-start | bytes 172040 | tf_op jit(solution)/shard_map/ppermute | solution.py:298
  31.0 6.1 %collective-permute-start = (bf16[4,56,128]{2,1,0:T(8,128)(2,1)S(1)}, bf16[4,56,128]{2,1,0:T(8,128)(2,1)S(1)}, u32[]{:S(2)}, u32[]{:S(2)}) collective-permute-start(bf16[4,56,128]{2,1,0:T(8,128)(2,1)S(1)} %get-tuple-element.25), channel_id=1, source_target_pairs={{0,1},{1,0},{2,3},{3,2},{4,5},{5,4},{6,7},{7,6},{8,9},{9,8},{10,11... | collective-permute-start | bytes 172040 | tf_op jit(solution)/shard_map/ppermute | solution.py:298
  35.0 1.3 copy-start
  37.1 5.8 %copy-start.8 = (bf16[12,56,128]{2,1,0:T(8,128)(2,1)}, bf16[12,56,128]{2,1,0:T(8,128)(2,1)S(1)}, u32[]{:S(2)}) copy-start(bf16[12,56,128]{2,1,0:T(8,128)(2,1)S(1)} %constant_dynamic-update-slice_fusion.refs_8_) | copy-start | bytes 516100
  37.1 14.5 %collective-permute-start.2 = (bf16[12,56,128]{2,1,0:T(8,128)(2,1)S(1)}, bf16[12,56,128]{2,1,0:T(8,128)(2,1)S(1)}, u32[]{:S(2)}, u32[]{:S(2)}) collective-permute-start(bf16[12,56,128]{2,1,0:T(8,128)(2,1)S(1)} %constant_dynamic-update-slice_fusion.refs_8_), channel_id=1, source_target_pairs={{0,56},{8,16},{16,8},{24,32},{32,24},{40,48},{48,40},{56,0},{1,57}... | collective-permute-start | bytes 516104 | tf_op jit(solution)/shard_map/ppermute | solution.py:298
  42.9 16.1 %copy-start.12 = (s32[1,1,1,128]{3,2,1,0:T(1,128)S(1)}, s32[1,1,1,128]{3,2,1,0:T(1,128)}, u32[]{:S(2)}) copy-start(s32[1,1,1,128]{3,2,1,0:T(1,128)} %param.23) | copy-start | bytes 1540
  51.7 7.9 %copy-start.6 = (bf16[36,56,128]{2,1,0:T(8,128)(2,1)}, bf16[36,56,128]{2,1,0:T(8,128)(2,1)S(1)}, u32[]{:S(2)}) copy-start(bf16[36,56,128]{2,1,0:T(8,128)(2,1)S(1)} %constant_dynamic-update-slice_fusion.3.refs_8_.refs_4_) | copy-start | bytes 1548292
  51.7 17.3 %collective-permute-start.4 = (bf16[36,56,128]{2,1,0:T(8,128)(2,1)S(1)}, bf16[36,56,128]{2,1,0:T(8,128)(2,1)S(1)}, u32[]{:S(2)}, u32[]{:S(2)}) collective-permute-start(bf16[36,56,128]{2,1,0:T(8,128)(2,1)S(1)} %constant_dynamic-update-slice_fusion.3.refs_8_.refs_4_), channel_id=1, source_target_pairs={{0,448},{64,128},{128,64},{192,256},{256,192},{320,384},{384,320},... | collective-permute-start | bytes 1548296 | tf_op jit(solution)/shard_map/ppermute | solution.py:298
  56.4 15.7 %collective-permute-start.3 = (bf16[36,56,128]{2,1,0:T(8,128)(2,1)S(1)}, bf16[36,56,128]{2,1,0:T(8,128)(2,1)S(1)}, u32[]{:S(2)}, u32[]{:S(2)}) collective-permute-start(bf16[36,56,128]{2,1,0:T(8,128)(2,1)S(1)} %constant_dynamic-update-slice_fusion.3.refs_8_.refs_4_), channel_id=1, source_target_pairs={{0,64},{64,0},{128,192},{192,128},{256,320},{320,256},{384,448},{4... | collective-permute-start | bytes 1548296 | tf_op jit(solution)/shard_map/ppermute | solution.py:298
  68.9 3.2 %copy-start.9 = (bf16[36,56,128]{2,1,0:T(8,128)(2,1)}, bf16[36,56,128]{2,1,0:T(8,128)(2,1)S(1)}, u32[]{:S(2)}) copy-start(bf16[36,56,128]{2,1,0:T(8,128)(2,1)S(1)} %collective-permute-done.4.refs_5_) | copy-start | bytes 1548292
  72.1 0.8 copy-start.10
  87.3 17.0 %collective-permute-start.6 = (bf16[36,56,128]{2,1,0:T(8,128)(2,1)}, bf16[36,56,128]{2,1,0:T(8,128)(2,1)S(1)}, u32[]{:S(2)}, u32[]{:S(2)}) collective-permute-start(bf16[36,56,128]{2,1,0:T(8,128)(2,1)} %get-tuple-element.38), channel_id=1, source_target_pairs={{0,448},{64,128},{128,64},{192,256},{256,192},{320,384},{384,320},... | collective-permute-start | bytes 1548296 | tf_op jit(solution)/shard_map/ppermute | solution.py:298
  91.2 15.7 %collective-permute-start.5 = (bf16[36,56,128]{2,1,0:T(8,128)(2,1)}, bf16[36,56,128]{2,1,0:T(8,128)(2,1)S(1)}, u32[]{:S(2)}, u32[]{:S(2)}) collective-permute-start(bf16[36,56,128]{2,1,0:T(8,128)(2,1)} %get-tuple-element.37.refs_14_), channel_id=1, source_target_pairs={{0,64},{64,0},{128,192},{192,128},{256,320},{320,256},{384,448},{4... | collective-permute-start | bytes 1548296 | tf_op jit(solution)/shard_map/ppermute | solution.py:298
  93.4 13.6 %copy-start.7 = (f32[36,56,128]{2,1,0:T(8,128)S(1)}, f32[36,56,128]{2,1,0:T(8,128)}, u32[]{:S(2)}) copy-start(f32[36,56,128]{2,1,0:T(8,128)} %get-tuple-element.36) | copy-start | bytes 3096580
  107.2 22.5 %copy-start.1 = (f32[32,56,128]{2,1,0:T(8,128)S(1)}, f32[32,56,128]{2,1,0:T(8,128)}, u32[]{:S(2)}) copy-start(f32[32,56,128]{2,1,0:T(8,128)} %shard_map.169.gathered) | copy-start | bytes 2752516
  107.3 10.5 %collective-permute-start.7 = (bf16[12,56,128]{2,1,0:T(8,128)(2,1)S(1)}, bf16[12,56,128]{2,1,0:T(8,128)(2,1)S(1)}, u32[]{:S(2)}, u32[]{:S(2)}) collective-permute-start(bf16[12,56,128]{2,1,0:T(8,128)(2,1)S(1)} %get-tuple-element.48), channel_id=1, source_target_pairs={{0,56},{8,16},{16,8},{24,32},{32,24},{40,48},{48,40},{56,0},{1,57}... | collective-permute-start | bytes 516104 | tf_op jit(solution)/shard_map/ppermute | solution.py:298
  117.9 7.4 %collective-permute-start.8 = (bf16[4,56,128]{2,1,0:T(8,128)(2,1)S(1)}, bf16[4,56,128]{2,1,0:T(8,128)(2,1)S(1)}, u32[]{:S(2)}, u32[]{:S(2)}) collective-permute-start(bf16[4,56,128]{2,1,0:T(8,128)(2,1)S(1)} %get-tuple-element.49), channel_id=1, source_target_pairs={{0,1},{1,0},{2,3},{3,2},{4,5},{5,4},{6,7},{7,6},{8,9},{9,8},{10,11... | collective-permute-start | bytes 172040 | tf_op jit(solution)/shard_map/ppermute | solution.py:298
  121.5 8.2 %collective-permute-start.9 = (bf16[4,56,128]{2,1,0:T(8,128)(2,1)S(1)}, bf16[4,56,128]{2,1,0:T(8,128)(2,1)S(1)}, u32[]{:S(2)}, u32[]{:S(2)}) collective-permute-start(bf16[4,56,128]{2,1,0:T(8,128)(2,1)S(1)} %get-tuple-element.50), channel_id=1, source_target_pairs={{0,7},{1,2},{2,1},{3,4},{4,3},{5,6},{6,5},{7,0},{8,15},{9,10},{10,... | collective-permute-start | bytes 172040 | tf_op jit(solution)/shard_map/ppermute | solution.py:298
Sparse Core Ops, SparseCore 0:
  23.2 55.6 all-gather.6

commit v4 on v3

--- a/solution.py
+++ b/solution.py
@@ -86,6 +86,25 @@
         x_out[a] = jnp.concatenate([rows, tail], axis=0).astype(BF16)
     for t in range(BOUND):
         border_out[t] = x_out[border_atoms[t]]
+
+
+def share_kernel(zero, one, two, out):
+    def columns(ref, b):
+        return ref[..., b * LANES : (b + 1) * LANES].astype(F32)
+
+    blank = jnp.zeros((2, LANES), F32)
+    for b in range(BLK0):
+        rows = jnp.concatenate([columns(zero, b), blank], axis=0)
+        out[b * ROWS0 : (b + 1) * ROWS0, :] = rows.astype(BF16)
+    start = ROWS0 * BLK0
+    for b in range(BLK1):
+        parts = columns(one, b)
+        rows = jnp.concatenate([parts[:, 0, :], parts[:, 1, :]], axis=0)
+        out[start + b * ROWS1 : start + (b + 1) * ROWS1, :] = rows.astype(BF16)
+    start += ROWS1 * BLK1
+    parts = [columns(two, b) for b in range(BLK2)]
+    rows = jnp.concatenate([p[:, sign, :] for p in parts for sign in range(2)], axis=0)
+    out[start:, :] = rows.astype(BF16)
 
 
 def rotations_kernel(rotations, out, tmp):
@@ -340,10 +359,13 @@
     order_one,
     order_two,
 ):
-    share0 = jnp.pad(order_zero.reshape(14, BLK0, LANES).transpose(1, 0, 2), ((0, 0), (0, 2), (0, 0)))
-    share1 = order_one.reshape(2, 12, BLK1, LANES).transpose(2, 0, 1, 3).reshape(BLK1, ROWS1, LANES)
-    share2 = order_two.reshape(2, 10, BLK2, LANES).transpose(2, 0, 1, 3).reshape(BLK2, 20, LANES)
-    share = jnp.concatenate([s.reshape(-1, LANES) for s in (share0, share1, share2)], axis=0)
+    share = pl.pallas_call(
+        share_kernel,
+        out_shape=jax.ShapeDtypeStruct((ROWS0 * BLK0 + ROWS1 * BLK1 + ROWS2 * BLK2, LANES), BF16),
+        in_specs=[VMEM] * 3,
+        out_specs=VMEM,
+        compiler_params=WIDE,
+    )(order_zero, order_one.transpose(1, 0, 2), order_two.transpose(1, 0, 2))
     four = lax.all_gather(share, "x", axis=0, tiled=False)
     pieces = []
     start = 0
@@ -388,12 +410,11 @@
     far_rows = (place(GX, slot // 9) * 3 + place(GY, slot // 3 % 3)) * 3 + place(GZ, slot % 3)
     far_rows = far_rows * BOUND + atom
 
-    near = widen(GZ, border)
-    [turned_out] = forward([count_x], [target_x], [rot_outward], [x], table, sp, near)
-    near = widen(GY, near)
-    near, turned_out = lax.optimization_barrier((near, turned_out))
+    near = widen(GY, widen(GZ, border))
     near_first, near_last = exchange(GX, near, near)
-    [turned_in] = forward([count_in], [source_in], [rot_in], [x], table, sp, near)
+    turned_out, turned_in = forward(
+        [count_x, count_in], [target_x, source_in], [rot_outward, rot_in], [x], table, sp, near
+    )
     [turned_x] = forward(
         [count_x], [far_rows], [rot_inward], [near_first, near, near_last], table, sp, turned_in[0]
     )

time: 139 us -> 137 us (0.986)
  the two profiles are of different devices: /device:TPU:24 before, /device:TPU:2 now
where the time goes in v4:
time: 137 us; the launch traced here: 136 us
  Pallas kernels  38.8 us (28%)
  starting transfers between devices  35.5 us (26%)
  blocking collectives  22.1 us (16%)
  waiting for transfers between devices  19.1 us (14%)
  between operations  15.1 us (11%)
  local copies, waits for them, and re-layouts  3.8 us (3%)
  other arithmetic  1.72 us (1%)
    ppermute x10, starting transfers between devices, swap(): lax.ppermute(block, axis, [(i, (i + (1 if (i + odd) % 2 == 0 else -1)) %...  35.5 us
    pallas_call x2, Pallas kernels, back(): pl.pallas_call(functools.partial(back_kernel, sets, trash, finish), out_s...  19.1 us
    ppermute x10, waiting for transfers between devices, swap(): lax.ppermute(block, axis, [(i, (i + (1 if (i + odd) % 2 == 0 else -1)) %...  17.6 us
    all_gather x1, blocking collectives, shards(): four = lax.all_gather(share, 'x', axis=0, tiled=False)  15.4 us
    pallas_call x2, Pallas kernels, forward(): pl.pallas_call(functools.partial(forward_kernel, sets, len(parts)), out_s...  15.2 us
    all_gather x2, blocking collectives, exchange(): both = lax.all_gather(first, 'core', axis=0, tiled=False)  6.62 us
    unnamed x29, local copies, waits for them, and re-layouts  3 us
  transfers between devices with their start and end apart: 11, of which 7 were waited for; matrix products, arithmetic and copies ran while one was open for 1% of the time, Pallas kernels for 20%

profile of v4, /device:TPU:2, one launch (start us, length us, event | category | flops | bytes accessed | tf_op | source)
XLA Modules:
  0.0 136.0 jit_solution(4680211693022854468)
XLA Ops:
  6.5 1.6 %shard_map.166 = bf16[356,128]{1,0:T(8,128)(2,1)} custom-call(bf16[14,896]{1,0:T(8,128)(2,1)} %zero.1, bf16[12,2,768]{2,1,0:T(2,128)(2,1)} %bitcast.63, bf16[10,2,640]{2,1,0:T(2,128)(2,1)} %bitcast.64), custom_call_target="tpu_custom_call" | custom-call | tf_op jit(solution)/shard_map/pallas_call | solution.py:362
  8.1 15.4 %all-gather.4 = bf16[4,356,128]{2,1,0:T(8,128)(2,1)S(1)} all-gather(bf16[1,356,128]{2,1,0:T(8,128)(2,1)} %bitcast.62), channel_id=3, replica_groups=mesh['gx'=8,'zh'=4,'core'=2,'x'=4,'zl'=2] {'x'}, dimensions={0}, use_global_device_ids=true | all-gather | bytes 455680 | tf_op jit(solution)/shard_map/all_gather | solution.py:369
  23.8 0.8 pad_maximum_fusion
  24.6 0.7 shard_map.163
  25.3 0.8 copy-done.4
  26.0 1.9 %collective-permute-start = (bf16[4,56,128]{2,1,0:T(8,128)(2,1)S(1)}, bf16[4,56,128]{2,1,0:T(8,128)(2,1)S(1)}, u32[]{:S(2)}, u32[]{:S(2)}) collective-permute-start(bf16[4,56,128]{2,1,0:T(8,128)(2,1)S(1)} %get-tuple-element.22), channel_id=1, source_target_pairs={{0,1},{1,0},{2,3},{3,2},{4,5},{5,4},{6,7},{7,6},{8,9},{9,8},{10,11... | collective-permute-start | bytes 172040 | tf_op jit(solution)/shard_map/ppermute | solution.py:317
  28.0 6.5 %collective-permute-start.1 = (bf16[4,56,128]{2,1,0:T(8,128)(2,1)S(1)}, bf16[4,56,128]{2,1,0:T(8,128)(2,1)S(1)}, u32[]{:S(2)}, u32[]{:S(2)}) collective-permute-start(bf16[4,56,128]{2,1,0:T(8,128)(2,1)S(1)} %get-tuple-element.22), channel_id=1, source_target_pairs={{0,7},{1,2},{2,1},{3,4},{4,3},{5,6},{6,5},{7,0},{8,15},{9,10},{10,... | collective-permute-start | bytes 172040 | tf_op jit(solution)/shard_map/ppermute | solution.py:317
  34.5 2.1 %collective-permute-done.1 = bf16[4,56,128]{2,1,0:T(8,128)(2,1)S(1)} collective-permute-done((bf16[4,56,128]{2,1,0:T(8,128)(2,1)S(1)}, bf16[4,56,128]{2,1,0:T(8,128)(2,1)S(1)}, u32[]{:S(2)}, u32[]{:S(2)}) %collective-permute-start.1) | collective-permute-done | bytes 57376 | tf_op jit(solution)/shard_map/ppermute | solution.py:317
  36.6 3.5 %collective-permute-start.2 = (bf16[12,56,128]{2,1,0:T(8,128)(2,1)S(1)}, bf16[12,56,128]{2,1,0:T(8,128)(2,1)S(1)}, u32[]{:S(2)}, u32[]{:S(2)}) collective-permute-start(bf16[12,56,128]{2,1,0:T(8,128)(2,1)S(1)} %constant_dynamic-update-slice_fusion), channel_id=1, source_target_pairs={{0,56},{8,16},{16,8},{24,32},{32,24},{40,48},{48,40},{56,0},{1,57}... | collective-permute-start | bytes 516104 | tf_op jit(solution)/shard_map/ppermute | solution.py:317
  40.1 2.7 %all-gather = bf16[24,56,128]{2,1,0:T(8,128)(2,1)S(1)} all-gather(bf16[12,56,128]{2,1,0:T(8,128)(2,1)S(1)} %constant_dynamic-update-slice_fusion), channel_id=2, replica_groups=mesh['gx'=8,'zh'=4,'core'=2,'x'=4,'zl'=2] {'core'}, dimensions={0}, use_global_device_ids=true | all-gather | bytes 516096 | tf_op jit(solution)/shard_map/all_gather | solution.py:323
  42.9 5.1 %collective-permute-done.2 = bf16[12,56,128]{2,1,0:T(8,128)(2,1)S(1)} collective-permute-done((bf16[12,56,128]{2,1,0:T(8,128)(2,1)S(1)}, bf16[12,56,128]{2,1,0:T(8,128)(2,1)S(1)}, u32[]{:S(2)}, u32[]{:S(2)}) %collective-permute-start.2) | collective-permute-done | bytes 172064 | tf_op jit(solution)/shard_map/ppermute | solution.py:317
  48.1 5.0 %collective-permute-start.4 = (bf16[36,56,128]{2,1,0:T(8,128)(2,1)S(1)}, bf16[36,56,128]{2,1,0:T(8,128)(2,1)S(1)}, u32[]{:S(2)}, u32[]{:S(2)}) collective-permute-start(bf16[36,56,128]{2,1,0:T(8,128)(2,1)S(1)} %constant_dynamic-update-slice_fusion.3.refs_11_.refs_4_), channel_id=1, source_target_pairs={{0,448},{64,128},{128,64},{192,256},{256,192},{320,384},{384,320},... | collective-permute-start | bytes 1548296 | tf_op jit(solution)/shard_map/ppermute | solution.py:317
  53.1 1.9 %collective-permute-start.3 = (bf16[36,56,128]{2,1,0:T(8,128)(2,1)S(1)}, bf16[36,56,128]{2,1,0:T(8,128)(2,1)S(1)}, u32[]{:S(2)}, u32[]{:S(2)}) collective-permute-start(bf16[36,56,128]{2,1,0:T(8,128)(2,1)S(1)} %constant_dynamic-update-slice_fusion.3.refs_11_.refs_4_), channel_id=1, source_target_pairs={{0,64},{64,0},{128,192},{192,128},{256,320},{320,256},{384,448},{4... | collective-permute-start | bytes 1548296 | tf_op jit(solution)/shard_map/ppermute | solution.py:317
  56.4 0.8 shard_map.164.refs_7_.refs_6_.refs_12_
  57.2 1.3 copy-done
  59.7 8.6 %shard_map.165 = (bf16[128,1024]{1,0:T(8,128)(2,1)}, bf16[2,128,1536]{2,1,0:T(8,128)(2,1)}, bf16[2,128,1280]{2,1,0:T(8,128)(2,1)}, bf16[128,1024]{1,0:T(8,128)(2...) custom-call(s32[1]{0:T(128)} %bitcast.47.refs_0_, s32[1]{0:T(128)} %bitcast.45.refs_1_, s32[128]{0:T(128)} %bitcast.67, ...), custom_call_target="tpu_custom_call" | custom-call | tf_op jit(solution)/shard_map/pallas_call | solution.py:184
  68.3 0.9 collective-permute-done.3.refs_3_
  69.2 0.8 copy-done.9
  70.0 6.6 %shard_map.167 = (bf16[128,1024]{1,0:T(8,128)(2,1)}, bf16[2,128,1536]{2,1,0:T(8,128)(2,1)}, bf16[2,128,1280]{2,1,0:T(8,128)(2,1)}) custom-call(s32[1]{0:T(128)} %bitcast.48.refs_0_, s32[128]{0:T(128)} %fusion.3.refs_1_.refs_2_, s32[128]{0:T(128)} %get-tuple-element.43.refs_2_.refs_3_, bf16[36,56,128]{2,1,0:T(8,128)(2,1)} %copy-done.9, ...), custom_call_target="tpu_custom_call" | custom-call | tf_op jit(solution)/shard_map/pallas_call | solution.py:184
  76.6 1.5 %all-gather.7.cloned.1.call-done = bf16[22784,128]{1,0:T(8,128)(2,1)} async-done(((bf16[1424,128]{1,0:T(8,128)(2,1)}), bf16[22784,128]{1,0:T(8,128)(2,1)}) %all-gather.7.cloned.1.call-update) | async-done | bytes 5832720 | tf_op jit(solution)/shard_map/all_gather | solution.py:376
  78.0 8.1 %shard_map.168 = (bf16[36,56,128]{2,1,0:T(8,128)(2,1)}, f32[36,56,128]{2,1,0:T(8,128)}, bf16[36,56,128]{2,1,0:T(8,128)(2,1)}) custom-call(s32[1]{0:T(128)} %bitcast.49.refs_0_, s32[128]{0:T(128)} %get-tuple-element.44.refs_4_.refs_1_, s32[128]{0:T(128)} %fusion.3.refs_1_.refs_2_, bf16[128,1024]{1,0:T(8,128)(2,1)} %get-tuple-element.23.refs_3_, ...), custom_call_target="tpu_custom_call" | custom-call | tf_op jit(solution)/shard_map/pallas_call | solution.py:284
  86.2 4.3 %collective-permute-start.6 = (bf16[36,56,128]{2,1,0:T(8,128)(2,1)}, bf16[36,56,128]{2,1,0:T(8,128)(2,1)S(1)}, u32[]{:S(2)}, u32[]{:S(2)}) collective-permute-start(bf16[36,56,128]{2,1,0:T(8,128)(2,1)} %get-tuple-element.30), channel_id=1, source_target_pairs={{0,448},{64,128},{128,64},{192,256},{256,192},{320,384},{384,320},... | collective-permute-start | bytes 1548296 | tf_op jit(solution)/shard_map/ppermute | solution.py:317
  90.5 2.3 %collective-permute-start.5 = (bf16[36,56,128]{2,1,0:T(8,128)(2,1)}, bf16[36,56,128]{2,1,0:T(8,128)(2,1)S(1)}, u32[]{:S(2)}, u32[]{:S(2)}) collective-permute-start(bf16[36,56,128]{2,1,0:T(8,128)(2,1)} %get-tuple-element.29.refs_14_), channel_id=1, source_target_pairs={{0,64},{64,0},{128,192},{192,128},{256,320},{320,256},{384,448},{4... | collective-permute-start | bytes 1548296 | tf_op jit(solution)/shard_map/ppermute | solution.py:317
  92.8 10.9 %shard_map.169.gathered = f32[32,56,128]{2,1,0:T(8,128)} custom-call(s32[1]{0:T(128)} %bitcast.46.refs_0_, s32[1]{0:T(128)} %bitcast.50.refs_1_, s32[128]{0:T(128)} %bitcast.66, s32[128]{0:T(128)} %get-tuple-element.43.refs_2_.refs_3_, s32[128]{0:T(128)} %bitcast.70, s32[128]{0:T(128)} %bitcast.68, bf16[128,1024]{1,0:T(8,128)(2,1)} %get-tuple-element.26.refs_10_.refs_6_, ...), custom_call_target="tpu_custom_call" | custom-call | tf_op jit(solution)/shard_map/pallas_call | solution.py:284
  103.8 2.5 %collective-permute-done.5 = bf16[36,56,128]{2,1,0:T(8,128)(2,1)S(1)} collective-permute-done((bf16[36,56,128]{2,1,0:T(8,128)(2,1)}, bf16[36,56,128]{2,1,0:T(8,128)(2,1)S(1)}, u32[]{:S(2)}, u32[]{:S(2)}) %collective-permute-start.5) | collective-permute-done | bytes 516128 | tf_op jit(solution)/shard_map/ppermute | solution.py:317
  106.6 2.1 %collective-permute-start.7 = (bf16[12,56,128]{2,1,0:T(8,128)(2,1)S(1)}, bf16[12,56,128]{2,1,0:T(8,128)(2,1)S(1)}, u32[]{:S(2)}, u32[]{:S(2)}) collective-permute-start(bf16[12,56,128]{2,1,0:T(8,128)(2,1)S(1)} %get-tuple-element.40), channel_id=1, source_target_pairs={{0,56},{8,16},{16,8},{24,32},{32,24},{40,48},{48,40},{56,0},{1,57}... | collective-permute-start | bytes 516104 | tf_op jit(solution)/shard_map/ppermute | solution.py:317
  108.6 3.9 %all-gather.3 = bf16[24,56,128]{2,1,0:T(8,128)(2,1)S(1)} all-gather(bf16[12,56,128]{2,1,0:T(8,128)(2,1)S(1)} %get-tuple-element.39), channel_id=5, replica_groups=mesh['gx'=8,'zh'=4,'core'=2,'x'=4,'zl'=2] {'core'}, dimensions={0}, use_global_device_ids=true | all-gather | bytes 516096 | tf_op jit(solution)/shard_map/all_gather | solution.py:323
  112.6 3.1 %collective-permute-done.7 = bf16[12,56,128]{2,1,0:T(8,128)(2,1)S(1)} collective-permute-done((bf16[12,56,128]{2,1,0:T(8,128)(2,1)S(1)}, bf16[12,56,128]{2,1,0:T(8,128)(2,1)S(1)}, u32[]{:S(2)}, u32[]{:S(2)}) %collective-permute-start.7) | collective-permute-done | bytes 172064 | tf_op jit(solution)/shard_map/ppermute | solution.py:317
  115.8 4.9 %collective-permute-start.8 = (bf16[4,56,128]{2,1,0:T(8,128)(2,1)S(1)}, bf16[4,56,128]{2,1,0:T(8,128)(2,1)S(1)}, u32[]{:S(2)}, u32[]{:S(2)}) collective-permute-start(bf16[4,56,128]{2,1,0:T(8,128)(2,1)S(1)} %get-tuple-element.41), channel_id=1, source_target_pairs={{0,1},{1,0},{2,3},{3,2},{4,5},{5,4},{6,7},{7,6},{8,9},{9,8},{10,11... | collective-permute-start | bytes 172040 | tf_op jit(solution)/shard_map/ppermute | solution.py:317
  120.7 3.1 %collective-permute-start.9 = (bf16[4,56,128]{2,1,0:T(8,128)(2,1)S(1)}, bf16[4,56,128]{2,1,0:T(8,128)(2,1)S(1)}, u32[]{:S(2)}, u32[]{:S(2)}) collective-permute-start(bf16[4,56,128]{2,1,0:T(8,128)(2,1)S(1)} %get-tuple-element.42), channel_id=1, source_target_pairs={{0,7},{1,2},{2,1},{3,4},{4,3},{5,6},{6,5},{7,0},{8,15},{9,10},{10,... | collective-permute-start | bytes 172040 | tf_op jit(solution)/shard_map/ppermute | solution.py:317
  123.8 3.9 %collective-permute-done.9 = bf16[4,56,128]{2,1,0:T(8,128)(2,1)S(1)} collective-permute-done((bf16[4,56,128]{2,1,0:T(8,128)(2,1)S(1)}, bf16[4,56,128]{2,1,0:T(8,128)(2,1)S(1)}, u32[]{:S(2)}, u32[]{:S(2)}) %collective-permute-start.9) | collective-permute-done | bytes 57376 | tf_op jit(solution)/shard_map/ppermute | solution.py:317
  127.7 1.5 %shard_map.170 = bf16[49,32,128]{2,1,0:T(8,128)(2,1)} custom-call(s32[4]{0:T(128)S(1)} %bitcast.54, bf16[49,32,128]{2,1,0:T(8,128)(2,1)S(1)} %bitcast.52, f32[32,56,128]{2,1,0:T(8,128)S(1)} %copy-done.1, f32[4,56,128]{2,1,0:T(8,128)S(1)} %fusion.2.returned), custom_call_target="tpu_custom_call" | custom-call | tf_op jit(solution)/shard_map/pallas_call | solution.py:437
  (51 shorter events, 1.9 us)
Async XLA Ops:
  6.5 18.0 %copy-start.5 = (s32[1,1,1,4]{3,2,1,0:T(1,128)S(1)}, s32[1,1,1,4]{3,2,1,0:T(1,128)}, u32[]{:S(2)}) copy-start(s32[1,1,1,4]{3,2,1,0:T(1,128)} %param.18) | copy-start | bytes 52
  6.5 18.0 %copy-start.2 = (bf16[1,1,1,32,49,128]{5,3,4,2,1,0:T(8,128)(2,1)S(1)}, bf16[1,1,1,32,49,128]{5,3,4,2,1,0:T(8,128)(2,1)}, u32[]{:S(2)}) copy-start(bf16[1,1,1,32,49,128]{5,3,4,2,1,0:T(8,128)(2,1)} %param.17) | copy-start | bytes 1204228
  6.5 71.5 %all-gather.7.cloned.1.call-start = ((), (), s32[]{:S(2)}) async-start(), calls=%async_computation | async-start | bytes 6197248 | tf_op jit(solution)/shard_map/all_gather | solution.py:376
  23.8 32.6 %copy-start.3 = (bf16[49,49,256]{2,1,0:T(8,128)(2,1)S(1)}, bf16[49,49,256]{2,1,0:T(8,128)(2,1)}, u32[]{:S(2)}) copy-start(bf16[49,49,256]{2,1,0:T(8,128)(2,1)} %rotations.1) | copy-start | bytes 3687940
  25.3 0.8 copy-start.4
  26.0 8.5 %collective-permute-start = (bf16[4,56,128]{2,1,0:T(8,128)(2,1)S(1)}, bf16[4,56,128]{2,1,0:T(8,128)(2,1)S(1)}, u32[]{:S(2)}, u32[]{:S(2)}) collective-permute-start(bf16[4,56,128]{2,1,0:T(8,128)(2,1)S(1)} %get-tuple-element.22), channel_id=1, source_target_pairs={{0,1},{1,0},{2,3},{3,2},{4,5},{5,4},{6,7},{7,6},{8,9},{9,8},{10,11... | collective-permute-start | bytes 172040 | tf_op jit(solution)/shard_map/ppermute | solution.py:317
  28.0 8.7 %collective-permute-start.1 = (bf16[4,56,128]{2,1,0:T(8,128)(2,1)S(1)}, bf16[4,56,128]{2,1,0:T(8,128)(2,1)S(1)}, u32[]{:S(2)}, u32[]{:S(2)}) collective-permute-start(bf16[4,56,128]{2,1,0:T(8,128)(2,1)S(1)} %get-tuple-element.22), channel_id=1, source_target_pairs={{0,7},{1,2},{2,1},{3,4},{4,3},{5,6},{6,5},{7,0},{8,15},{9,10},{10,... | collective-permute-start | bytes 172040 | tf_op jit(solution)/shard_map/ppermute | solution.py:317
  36.6 11.4 %collective-permute-start.2 = (bf16[12,56,128]{2,1,0:T(8,128)(2,1)S(1)}, bf16[12,56,128]{2,1,0:T(8,128)(2,1)S(1)}, u32[]{:S(2)}, u32[]{:S(2)}) collective-permute-start(bf16[12,56,128]{2,1,0:T(8,128)(2,1)S(1)} %constant_dynamic-update-slice_fusion), channel_id=1, source_target_pairs={{0,56},{8,16},{16,8},{24,32},{32,24},{40,48},{48,40},{56,0},{1,57}... | collective-permute-start | bytes 516104 | tf_op jit(solution)/shard_map/ppermute | solution.py:317
  42.9 15.6 %copy-start.11 = (s32[1,1,1,128]{3,2,1,0:T(1,128)S(1)}, s32[1,1,1,128]{3,2,1,0:T(1,128)}, u32[]{:S(2)}) copy-start(s32[1,1,1,128]{3,2,1,0:T(1,128)} %param.23) | copy-start | bytes 1540
  42.9 16.2 %copy-start.10 = (s32[1,1,1,2,128]{4,3,2,1,0:T(2,128)S(1)}, s32[1,1,1,2,128]{4,3,2,1,0:T(2,128)}, u32[]{:S(2)}) copy-start(s32[1,1,1,2,128]{4,3,2,1,0:T(2,128)} %param.25) | copy-start | bytes 3076
  48.0 11.6 %copy-start.6 = (bf16[36,56,128]{2,1,0:T(8,128)(2,1)}, bf16[36,56,128]{2,1,0:T(8,128)(2,1)S(1)}, u32[]{:S(2)}) copy-start(bf16[36,56,128]{2,1,0:T(8,128)(2,1)S(1)} %constant_dynamic-update-slice_fusion.3.refs_11_.refs_4_) | copy-start | bytes 1548292
  48.1 20.2 %collective-permute-start.4 = (bf16[36,56,128]{2,1,0:T(8,128)(2,1)S(1)}, bf16[36,56,128]{2,1,0:T(8,128)(2,1)S(1)}, u32[]{:S(2)}, u32[]{:S(2)}) collective-permute-start(bf16[36,56,128]{2,1,0:T(8,128)(2,1)S(1)} %constant_dynamic-update-slice_fusion.3.refs_11_.refs_4_), channel_id=1, source_target_pairs={{0,448},{64,128},{128,64},{192,256},{256,192},{320,384},{384,320},... | collective-permute-start | bytes 1548296 | tf_op jit(solution)/shard_map/ppermute | solution.py:317
  53.1 16.1 %collective-permute-start.3 = (bf16[36,56,128]{2,1,0:T(8,128)(2,1)S(1)}, bf16[36,56,128]{2,1,0:T(8,128)(2,1)S(1)}, u32[]{:S(2)}, u32[]{:S(2)}) collective-permute-start(bf16[36,56,128]{2,1,0:T(8,128)(2,1)S(1)} %constant_dynamic-update-slice_fusion.3.refs_11_.refs_4_), channel_id=1, source_target_pairs={{0,64},{64,0},{128,192},{192,128},{256,320},{320,256},{384,448},{4... | collective-permute-start | bytes 1548296 | tf_op jit(solution)/shard_map/ppermute | solution.py:317
  57.2 1.3 copy-start
  68.3 0.9 copy-start.8
  69.2 0.8 copy-start.9
  86.2 17.6 %collective-permute-start.6 = (bf16[36,56,128]{2,1,0:T(8,128)(2,1)}, bf16[36,56,128]{2,1,0:T(8,128)(2,1)S(1)}, u32[]{:S(2)}, u32[]{:S(2)}) collective-permute-start(bf16[36,56,128]{2,1,0:T(8,128)(2,1)} %get-tuple-element.30), channel_id=1, source_target_pairs={{0,448},{64,128},{128,64},{192,256},{256,192},{320,384},{384,320},... | collective-permute-start | bytes 1548296 | tf_op jit(solution)/shard_map/ppermute | solution.py:317
  90.5 15.8 %collective-permute-start.5 = (bf16[36,56,128]{2,1,0:T(8,128)(2,1)}, bf16[36,56,128]{2,1,0:T(8,128)(2,1)S(1)}, u32[]{:S(2)}, u32[]{:S(2)}) collective-permute-start(bf16[36,56,128]{2,1,0:T(8,128)(2,1)} %get-tuple-element.29.refs_14_), channel_id=1, source_target_pairs={{0,64},{64,0},{128,192},{192,128},{256,320},{320,256},{384,448},{4... | collective-permute-start | bytes 1548296 | tf_op jit(solution)/shard_map/ppermute | solution.py:317
  92.8 13.5 %copy-start.7 = (f32[36,56,128]{2,1,0:T(8,128)S(1)}, f32[36,56,128]{2,1,0:T(8,128)}, u32[]{:S(2)}) copy-start(f32[36,56,128]{2,1,0:T(8,128)} %get-tuple-element.28) | copy-start | bytes 3096580
  106.5 21.2 %copy-start.1 = (f32[32,56,128]{2,1,0:T(8,128)S(1)}, f32[32,56,128]{2,1,0:T(8,128)}, u32[]{:S(2)}) copy-start(f32[32,56,128]{2,1,0:T(8,128)} %shard_map.169.gathered) | copy-start | bytes 2752516
  106.6 9.1 %collective-permute-start.7 = (bf16[12,56,128]{2,1,0:T(8,128)(2,1)S(1)}, bf16[12,56,128]{2,1,0:T(8,128)(2,1)S(1)}, u32[]{:S(2)}, u32[]{:S(2)}) collective-permute-start(bf16[12,56,128]{2,1,0:T(8,128)(2,1)S(1)} %get-tuple-element.40), channel_id=1, source_target_pairs={{0,56},{8,16},{16,8},{24,32},{32,24},{40,48},{48,40},{56,0},{1,57}... | collective-permute-start | bytes 516104 | tf_op jit(solution)/shard_map/ppermute | solution.py:317
  115.8 8.0 %collective-permute-start.8 = (bf16[4,56,128]{2,1,0:T(8,128)(2,1)S(1)}, bf16[4,56,128]{2,1,0:T(8,128)(2,1)S(1)}, u32[]{:S(2)}, u32[]{:S(2)}) collective-permute-start(bf16[4,56,128]{2,1,0:T(8,128)(2,1)S(1)} %get-tuple-element.41), channel_id=1, source_target_pairs={{0,1},{1,0},{2,3},{3,2},{4,5},{5,4},{6,7},{7,6},{8,9},{9,8},{10,11... | collective-permute-start | bytes 172040 | tf_op jit(solution)/shard_map/ppermute | solution.py:317
  120.7 7.0 %collective-permute-start.9 = (bf16[4,56,128]{2,1,0:T(8,128)(2,1)S(1)}, bf16[4,56,128]{2,1,0:T(8,128)(2,1)S(1)}, u32[]{:S(2)}, u32[]{:S(2)}) collective-permute-start(bf16[4,56,128]{2,1,0:T(8,128)(2,1)S(1)} %get-tuple-element.42), channel_id=1, source_target_pairs={{0,7},{1,2},{2,1},{3,4},{4,3},{5,6},{6,5},{7,0},{8,15},{9,10},{10,... | collective-permute-start | bytes 172040 | tf_op jit(solution)/shard_map/ppermute | solution.py:317
Sparse Core Ops, SparseCore 0:
  24.7 53.3 all-gather.6

commit v5 on v4

--- a/solution.py
+++ b/solution.py
@@ -19,7 +19,7 @@
 ATOMS = 32
 BOUND = 4
 AROUND = 27 * BOUND
-STEP = 32
+STEP = 64
 PITCH = EDGES + 1
 LANES = 128
 BF16 = jnp.bfloat16
@@ -411,6 +411,7 @@
     far_rows = far_rows * BOUND + atom
 
     near = widen(GY, widen(GZ, border))
+    near, table = lax.optimization_barrier((near, table))
     near_first, near_last = exchange(GX, near, near)
     turned_out, turned_in = forward(
         [count_x, count_in], [target_x, source_in], [rot_outward, rot_in], [x], table, sp, near

time: 137 us -> 137 us (level)
  the two profiles are of different devices: /device:TPU:2 before, /device:TPU:24 now
where the time goes in v5:
time: 137 us
  Pallas kernels  38.3 us (28%)
  starting transfers between devices  37.6 us (27%)
  waiting for transfers between devices  21.9 us (16%)
  blocking collectives  18.3 us (13%)
  between operations  15.1 us (11%)
  local copies, waits for them, and re-layouts  3.8 us (3%)
  other arithmetic  1.72 us (1%)
    ppermute x10, starting transfers between devices, swap(): lax.ppermute(block, axis, [(i, (i + (1 if (i + odd) % 2 == 0 else -1)) %...  37.6 us
    ppermute x10, waiting for transfers between devices, swap(): lax.ppermute(block, axis, [(i, (i + (1 if (i + odd) % 2 == 0 else -1)) %...  19.2 us
    pallas_call x2, Pallas kernels, back(): pl.pallas_call(functools.partial(back_kernel, sets, trash, finish), out_s...  18.6 us
    pallas_call x2, Pallas kernels, forward(): pl.pallas_call(functools.partial(forward_kernel, sets, len(parts)), out_s...  15.2 us
    all_gather x1, blocking collectives, shards(): four = lax.all_gather(share, 'x', axis=0, tiled=False)  13.2 us
    all_gather x2, blocking collectives, exchange(): both = lax.all_gather(first, 'core', axis=0, tiled=False)  5.16 us
    unnamed x29, local copies, waits for them, and re-layouts  2.99 us
    all_gather x1, waiting for transfers between devices, shards(): lax.all_gather(jnp.concatenate(pieces, axis=0), ('zh', 'zl', 'core'), axi...  2.77 us
  transfers between devices with their start and end apart: 11, of which 7 were waited for; matrix products, arithmetic and copies ran while one was open for 1% of the time, Pallas kernels for 20%

profile of v5, /device:TPU:24, one launch (start us, length us, event | category | flops | bytes accessed | tf_op | source)
XLA Modules:
  0.0 136.7 jit_solution(177907067041328292)
XLA Ops:
  6.5 1.6 %shard_map.166 = bf16[356,128]{1,0:T(8,128)(2,1)} custom-call(bf16[14,896]{1,0:T(8,128)(2,1)} %zero.1, bf16[12,2,768]{2,1,0:T(2,128)(2,1)} %bitcast.63, bf16[10,2,640]{2,1,0:T(2,128)(2,1)} %bitcast.64), custom_call_target="tpu_custom_call" | custom-call | tf_op jit(solution)/shard_map/pallas_call | solution.py:362
  8.1 13.2 %all-gather.4 = bf16[4,356,128]{2,1,0:T(8,128)(2,1)S(1)} all-gather(bf16[1,356,128]{2,1,0:T(8,128)(2,1)} %bitcast.62), channel_id=3, replica_groups=mesh['gx'=8,'zh'=4,'core'=2,'x'=4,'zl'=2] {'x'}, dimensions={0}, use_global_device_ids=true | all-gather | bytes 455680 | tf_op jit(solution)/shard_map/all_gather | solution.py:369
  21.5 0.8 pad_maximum_fusion
  22.3 0.7 shard_map.163
  23.0 0.8 copy-done.4
  23.8 4.3 %collective-permute-start = (bf16[4,56,128]{2,1,0:T(8,128)(2,1)S(1)}, bf16[4,56,128]{2,1,0:T(8,128)(2,1)S(1)}, u32[]{:S(2)}, u32[]{:S(2)}) collective-permute-start(bf16[4,56,128]{2,1,0:T(8,128)(2,1)S(1)} %get-tuple-element.24), channel_id=1, source_target_pairs={{0,1},{1,0},{2,3},{3,2},{4,5},{5,4},{6,7},{7,6},{8,9},{9,8},{10,11... | collective-permute-start | bytes 172040 | tf_op jit(solution)/shard_map/ppermute | solution.py:317
  28.0 4.0 %collective-permute-start.1 = (bf16[4,56,128]{2,1,0:T(8,128)(2,1)S(1)}, bf16[4,56,128]{2,1,0:T(8,128)(2,1)S(1)}, u32[]{:S(2)}, u32[]{:S(2)}) collective-permute-start(bf16[4,56,128]{2,1,0:T(8,128)(2,1)S(1)} %get-tuple-element.24), channel_id=1, source_target_pairs={{0,7},{1,2},{2,1},{3,4},{4,3},{5,6},{6,5},{7,0},{8,15},{9,10},{10,... | collective-permute-start | bytes 172040 | tf_op jit(solution)/shard_map/ppermute | solution.py:317
  32.1 0.8 shard_map.164.refs_7_.refs_6_.refs_12_
  33.0 1.3 copy-done
  34.3 1.9 %collective-permute-done.1 = bf16[4,56,128]{2,1,0:T(8,128)(2,1)S(1)} collective-permute-done((bf16[4,56,128]{2,1,0:T(8,128)(2,1)S(1)}, bf16[4,56,128]{2,1,0:T(8,128)(2,1)S(1)}, u32[]{:S(2)}, u32[]{:S(2)}) %collective-permute-start.1) | collective-permute-done | bytes 57376 | tf_op jit(solution)/shard_map/ppermute | solution.py:317
  36.2 6.3 %collective-permute-start.2 = (bf16[12,56,128]{2,1,0:T(8,128)(2,1)S(1)}, bf16[12,56,128]{2,1,0:T(8,128)(2,1)S(1)}, u32[]{:S(2)}, u32[]{:S(2)}) collective-permute-start(bf16[12,56,128]{2,1,0:T(8,128)(2,1)S(1)} %constant_dynamic-update-slice_fusion), channel_id=1, source_target_pairs={{0,56},{8,16},{16,8},{24,32},{32,24},{40,48},{48,40},{56,0},{1,57}... | collective-permute-start | bytes 516104 | tf_op jit(solution)/shard_map/ppermute | solution.py:317
  42.6 2.1 %all-gather = bf16[24,56,128]{2,1,0:T(8,128)(2,1)S(1)} all-gather(bf16[12,56,128]{2,1,0:T(8,128)(2,1)S(1)} %constant_dynamic-update-slice_fusion), channel_id=2, replica_groups=mesh['gx'=8,'zh'=4,'core'=2,'x'=4,'zl'=2] {'core'}, dimensions={0}, use_global_device_ids=true | all-gather | bytes 516096 | tf_op jit(solution)/shard_map/all_gather | solution.py:323
  44.7 2.9 %collective-permute-done.2 = bf16[12,56,128]{2,1,0:T(8,128)(2,1)S(1)} collective-permute-done((bf16[12,56,128]{2,1,0:T(8,128)(2,1)S(1)}, bf16[12,56,128]{2,1,0:T(8,128)(2,1)S(1)}, u32[]{:S(2)}, u32[]{:S(2)}) %collective-permute-start.2) | collective-permute-done | bytes 172064 | tf_op jit(solution)/shard_map/ppermute | solution.py:317
  47.6 4.6 %collective-permute-start.4 = (bf16[36,56,128]{2,1,0:T(8,128)(2,1)S(1)}, bf16[36,56,128]{2,1,0:T(8,128)(2,1)S(1)}, u32[]{:S(2)}, u32[]{:S(2)}) collective-permute-start(bf16[36,56,128]{2,1,0:T(8,128)(2,1)S(1)} %constant_dynamic-update-slice_fusion.3.refs_11_.refs_4_), channel_id=1, source_target_pairs={{0,448},{64,128},{128,64},{192,256},{256,192},{320,384},{384,320},... | collective-permute-start | bytes 1548296 | tf_op jit(solution)/shard_map/ppermute | solution.py:317
  52.3 1.9 %collective-permute-start.3 = (bf16[36,56,128]{2,1,0:T(8,128)(2,1)S(1)}, bf16[36,56,128]{2,1,0:T(8,128)(2,1)S(1)}, u32[]{:S(2)}, u32[]{:S(2)}) collective-permute-start(bf16[36,56,128]{2,1,0:T(8,128)(2,1)S(1)} %constant_dynamic-update-slice_fusion.3.refs_11_.refs_4_), channel_id=1, source_target_pairs={{0,64},{64,0},{128,192},{192,128},{256,320},{320,256},{384,448},{4... | collective-permute-start | bytes 1548296 | tf_op jit(solution)/shard_map/ppermute | solution.py:317
  56.7 8.5 %shard_map.165 = (bf16[128,1024]{1,0:T(8,128)(2,1)}, bf16[2,128,1536]{2,1,0:T(8,128)(2,1)}, bf16[2,128,1280]{2,1,0:T(8,128)(2,1)}, bf16[128,1024]{1,0:T(8,128)(2...) custom-call(s32[1]{0:T(128)} %bitcast.47.refs_0_, s32[1]{0:T(128)} %bitcast.45.refs_1_, s32[128]{0:T(128)} %bitcast.67, ...), custom_call_target="tpu_custom_call" | custom-call | tf_op jit(solution)/shard_map/pallas_call | solution.py:184
  65.2 2.5 %collective-permute-done.3.refs_3_ = bf16[36,56,128]{2,1,0:T(8,128)(2,1)S(1)} collective-permute-done((bf16[36,56,128]{2,1,0:T(8,128)(2,1)S(1)}, bf16[36,56,128]{2,1,0:T(8,128)(2,1)S(1)}, u32[]{:S(2)}, u32[]{:S(2)}) %collective-permute-start.3) | collective-permute-done | bytes 516128 | tf_op jit(solution)/shard_map/ppermute | solution.py:317
  67.7 0.8 copy-done.9
  68.5 6.6 %shard_map.167 = (bf16[128,1024]{1,0:T(8,128)(2,1)}, bf16[2,128,1536]{2,1,0:T(8,128)(2,1)}, bf16[2,128,1280]{2,1,0:T(8,128)(2,1)}) custom-call(s32[1]{0:T(128)} %bitcast.48.refs_0_, s32[128]{0:T(128)} %fusion.3.refs_1_.refs_2_, s32[128]{0:T(128)} %get-tuple-element.47.refs_2_.refs_3_, bf16[36,56,128]{2,1,0:T(8,128)(2,1)} %copy-done.9, ...), custom_call_target="tpu_custom_call" | custom-call | tf_op jit(solution)/shard_map/pallas_call | solution.py:184
  75.2 2.8 %all-gather.7.cloned.1.call-done = bf16[22784,128]{1,0:T(8,128)(2,1)} async-done(((bf16[1424,128]{1,0:T(8,128)(2,1)}), bf16[22784,128]{1,0:T(8,128)(2,1)}) %all-gather.7.cloned.1.call-update) | async-done | bytes 5832720 | tf_op jit(solution)/shard_map/all_gather | solution.py:376
  77.9 7.8 %shard_map.168 = (bf16[36,56,128]{2,1,0:T(8,128)(2,1)}, f32[36,56,128]{2,1,0:T(8,128)}, bf16[36,56,128]{2,1,0:T(8,128)(2,1)}) custom-call(s32[1]{0:T(128)} %bitcast.49.refs_0_, s32[128]{0:T(128)} %get-tuple-element.48.refs_4_.refs_1_, s32[128]{0:T(128)} %fusion.3.refs_1_.refs_2_, bf16[128,1024]{1,0:T(8,128)(2,1)} %get-tuple-element.27.refs_3_, ...), custom_call_target="tpu_custom_call" | custom-call | tf_op jit(solution)/shard_map/pallas_call | solution.py:284
  85.8 4.6 %collective-permute-start.6 = (bf16[36,56,128]{2,1,0:T(8,128)(2,1)}, bf16[36,56,128]{2,1,0:T(8,128)(2,1)S(1)}, u32[]{:S(2)}, u32[]{:S(2)}) collective-permute-start(bf16[36,56,128]{2,1,0:T(8,128)(2,1)} %get-tuple-element.34), channel_id=1, source_target_pairs={{0,448},{64,128},{128,64},{192,256},{256,192},{320,384},{384,320},... | collective-permute-start | bytes 1548296 | tf_op jit(solution)/shard_map/ppermute | solution.py:317
  90.4 2.1 %collective-permute-start.5 = (bf16[36,56,128]{2,1,0:T(8,128)(2,1)}, bf16[36,56,128]{2,1,0:T(8,128)(2,1)S(1)}, u32[]{:S(2)}, u32[]{:S(2)}) collective-permute-start(bf16[36,56,128]{2,1,0:T(8,128)(2,1)} %get-tuple-element.33.refs_14_), channel_id=1, source_target_pairs={{0,64},{64,0},{128,192},{192,128},{256,320},{320,256},{384,448},{4... | collective-permute-start | bytes 1548296 | tf_op jit(solution)/shard_map/ppermute | solution.py:317
  92.5 10.7 %shard_map.169.gathered = f32[32,56,128]{2,1,0:T(8,128)} custom-call(s32[1]{0:T(128)} %bitcast.46.refs_0_, s32[1]{0:T(128)} %bitcast.50.refs_1_, s32[128]{0:T(128)} %bitcast.66, s32[128]{0:T(128)} %get-tuple-element.47.refs_2_.refs_3_, s32[128]{0:T(128)} %bitcast.70, s32[128]{0:T(128)} %bitcast.68, bf16[128,1024]{1,0:T(8,128)(2,1)} %get-tuple-element.30.refs_10_.refs_6_, ...), custom_call_target="tpu_custom_call" | custom-call | tf_op jit(solution)/shard_map/pallas_call | solution.py:284
  103.2 2.8 %collective-permute-done.5 = bf16[36,56,128]{2,1,0:T(8,128)(2,1)S(1)} collective-permute-done((bf16[36,56,128]{2,1,0:T(8,128)(2,1)}, bf16[36,56,128]{2,1,0:T(8,128)(2,1)S(1)}, u32[]{:S(2)}, u32[]{:S(2)}) %collective-permute-start.5) | collective-permute-done | bytes 516128 | tf_op jit(solution)/shard_map/ppermute | solution.py:317
  106.3 2.2 %collective-permute-start.7 = (bf16[12,56,128]{2,1,0:T(8,128)(2,1)S(1)}, bf16[12,56,128]{2,1,0:T(8,128)(2,1)S(1)}, u32[]{:S(2)}, u32[]{:S(2)}) collective-permute-start(bf16[12,56,128]{2,1,0:T(8,128)(2,1)S(1)} %get-tuple-element.44), channel_id=1, source_target_pairs={{0,56},{8,16},{16,8},{24,32},{32,24},{40,48},{48,40},{56,0},{1,57}... | collective-permute-start | bytes 516104 | tf_op jit(solution)/shard_map/ppermute | solution.py:317
  108.5 3.1 %all-gather.3 = bf16[24,56,128]{2,1,0:T(8,128)(2,1)S(1)} all-gather(bf16[12,56,128]{2,1,0:T(8,128)(2,1)S(1)} %get-tuple-element.43), channel_id=5, replica_groups=mesh['gx'=8,'zh'=4,'core'=2,'x'=4,'zl'=2] {'core'}, dimensions={0}, use_global_device_ids=true | all-gather | bytes 516096 | tf_op jit(solution)/shard_map/all_gather | solution.py:323
  111.6 5.0 %collective-permute-done.7 = bf16[12,56,128]{2,1,0:T(8,128)(2,1)S(1)} collective-permute-done((bf16[12,56,128]{2,1,0:T(8,128)(2,1)S(1)}, bf16[12,56,128]{2,1,0:T(8,128)(2,1)S(1)}, u32[]{:S(2)}, u32[]{:S(2)}) %collective-permute-start.7) | collective-permute-done | bytes 172064 | tf_op jit(solution)/shard_map/ppermute | solution.py:317
  116.7 3.5 %collective-permute-start.8 = (bf16[4,56,128]{2,1,0:T(8,128)(2,1)S(1)}, bf16[4,56,128]{2,1,0:T(8,128)(2,1)S(1)}, u32[]{:S(2)}, u32[]{:S(2)}) collective-permute-start(bf16[4,56,128]{2,1,0:T(8,128)(2,1)S(1)} %get-tuple-element.45), channel_id=1, source_target_pairs={{0,1},{1,0},{2,3},{3,2},{4,5},{5,4},{6,7},{7,6},{8,9},{9,8},{10,11... | collective-permute-start | bytes 172040 | tf_op jit(solution)/shard_map/ppermute | solution.py:317
  120.2 4.0 %collective-permute-start.9 = (bf16[4,56,128]{2,1,0:T(8,128)(2,1)S(1)}, bf16[4,56,128]{2,1,0:T(8,128)(2,1)S(1)}, u32[]{:S(2)}, u32[]{:S(2)}) collective-permute-start(bf16[4,56,128]{2,1,0:T(8,128)(2,1)S(1)} %get-tuple-element.46), channel_id=1, source_target_pairs={{0,7},{1,2},{2,1},{3,4},{4,3},{5,6},{6,5},{7,0},{8,15},{9,10},{10,... | collective-permute-start | bytes 172040 | tf_op jit(solution)/shard_map/ppermute | solution.py:317
  124.2 4.2 %collective-permute-done.9 = bf16[4,56,128]{2,1,0:T(8,128)(2,1)S(1)} collective-permute-done((bf16[4,56,128]{2,1,0:T(8,128)(2,1)S(1)}, bf16[4,56,128]{2,1,0:T(8,128)(2,1)S(1)}, u32[]{:S(2)}, u32[]{:S(2)}) %collective-permute-start.9) | collective-permute-done | bytes 57376 | tf_op jit(solution)/shard_map/ppermute | solution.py:317
  128.4 1.5 %shard_map.170 = bf16[49,32,128]{2,1,0:T(8,128)(2,1)} custom-call(s32[4]{0:T(128)S(1)} %bitcast.54, bf16[49,32,128]{2,1,0:T(8,128)(2,1)S(1)} %bitcast.52, f32[32,56,128]{2,1,0:T(8,128)S(1)} %copy-done.1, f32[4,56,128]{2,1,0:T(8,128)S(1)} %fusion.2.returned), custom_call_target="tpu_custom_call" | custom-call | tf_op jit(solution)/shard_map/pallas_call | solution.py:438
  (51 shorter events, 1.9 us)
Async XLA Ops:
  6.5 15.8 %copy-start.5 = (s32[1,1,1,4]{3,2,1,0:T(1,128)S(1)}, s32[1,1,1,4]{3,2,1,0:T(1,128)}, u32[]{:S(2)}) copy-start(s32[1,1,1,4]{3,2,1,0:T(1,128)} %param.18) | copy-start | bytes 52
  6.5 15.8 %copy-start.2 = (bf16[1,1,1,32,49,128]{5,3,4,2,1,0:T(8,128)(2,1)S(1)}, bf16[1,1,1,32,49,128]{5,3,4,2,1,0:T(8,128)(2,1)}, u32[]{:S(2)}) copy-start(bf16[1,1,1,32,49,128]{5,3,4,2,1,0:T(8,128)(2,1)} %param.17) | copy-start | bytes 1204228
  6.5 71.4 %all-gather.7.cloned.1.call-start = ((), (), s32[]{:S(2)}) async-start(), calls=%async_computation | async-start | bytes 6197248 | tf_op jit(solution)/shard_map/all_gather | solution.py:376
  8.1 24.0 %copy-start.3 = (bf16[49,49,256]{2,1,0:T(8,128)(2,1)S(1)}, bf16[49,49,256]{2,1,0:T(8,128)(2,1)}, u32[]{:S(2)}) copy-start(bf16[49,49,256]{2,1,0:T(8,128)(2,1)} %rotations.1) | copy-start | bytes 3687940
  23.0 0.8 copy-start.4
  23.8 10.5 %collective-permute-start = (bf16[4,56,128]{2,1,0:T(8,128)(2,1)S(1)}, bf16[4,56,128]{2,1,0:T(8,128)(2,1)S(1)}, u32[]{:S(2)}, u32[]{:S(2)}) collective-permute-start(bf16[4,56,128]{2,1,0:T(8,128)(2,1)S(1)} %get-tuple-element.24), channel_id=1, source_target_pairs={{0,1},{1,0},{2,3},{3,2},{4,5},{5,4},{6,7},{7,6},{8,9},{9,8},{10,11... | collective-permute-start | bytes 172040 | tf_op jit(solution)/shard_map/ppermute | solution.py:317
  28.0 8.2 %collective-permute-start.1 = (bf16[4,56,128]{2,1,0:T(8,128)(2,1)S(1)}, bf16[4,56,128]{2,1,0:T(8,128)(2,1)S(1)}, u32[]{:S(2)}, u32[]{:S(2)}) collective-permute-start(bf16[4,56,128]{2,1,0:T(8,128)(2,1)S(1)} %get-tuple-element.24), channel_id=1, source_target_pairs={{0,7},{1,2},{2,1},{3,4},{4,3},{5,6},{6,5},{7,0},{8,15},{9,10},{10,... | collective-permute-start | bytes 172040 | tf_op jit(solution)/shard_map/ppermute | solution.py:317
  32.1 23.4 %copy-start.11 = (s32[1,1,1,128]{3,2,1,0:T(1,128)S(1)}, s32[1,1,1,128]{3,2,1,0:T(1,128)}, u32[]{:S(2)}) copy-start(s32[1,1,1,128]{3,2,1,0:T(1,128)} %param.23) | copy-start | bytes 1540
  32.1 24.0 %copy-start.10 = (s32[1,1,1,2,128]{4,3,2,1,0:T(2,128)S(1)}, s32[1,1,1,2,128]{4,3,2,1,0:T(2,128)}, u32[]{:S(2)}) copy-start(s32[1,1,1,2,128]{4,3,2,1,0:T(2,128)} %param.25) | copy-start | bytes 3076
  33.0 1.3 copy-start
  36.2 11.4 %collective-permute-start.2 = (bf16[12,56,128]{2,1,0:T(8,128)(2,1)S(1)}, bf16[12,56,128]{2,1,0:T(8,128)(2,1)S(1)}, u32[]{:S(2)}, u32[]{:S(2)}) collective-permute-start(bf16[12,56,128]{2,1,0:T(8,128)(2,1)S(1)} %constant_dynamic-update-slice_fusion), channel_id=1, source_target_pairs={{0,56},{8,16},{16,8},{24,32},{32,24},{40,48},{48,40},{56,0},{1,57}... | collective-permute-start | bytes 516104 | tf_op jit(solution)/shard_map/ppermute | solution.py:317
  47.6 9.0 %copy-start.6 = (bf16[36,56,128]{2,1,0:T(8,128)(2,1)}, bf16[36,56,128]{2,1,0:T(8,128)(2,1)S(1)}, u32[]{:S(2)}) copy-start(bf16[36,56,128]{2,1,0:T(8,128)(2,1)S(1)} %constant_dynamic-update-slice_fusion.3.refs_11_.refs_4_) | copy-start | bytes 1548292
  47.6 17.6 %collective-permute-start.4 = (bf16[36,56,128]{2,1,0:T(8,128)(2,1)S(1)}, bf16[36,56,128]{2,1,0:T(8,128)(2,1)S(1)}, u32[]{:S(2)}, u32[]{:S(2)}) collective-permute-start(bf16[36,56,128]{2,1,0:T(8,128)(2,1)S(1)} %constant_dynamic-update-slice_fusion.3.refs_11_.refs_4_), channel_id=1, source_target_pairs={{0,448},{64,128},{128,64},{192,256},{256,192},{320,384},{384,320},... | collective-permute-start | bytes 1548296 | tf_op jit(solution)/shard_map/ppermute | solution.py:317
  52.3 15.5 %collective-permute-start.3 = (bf16[36,56,128]{2,1,0:T(8,128)(2,1)S(1)}, bf16[36,56,128]{2,1,0:T(8,128)(2,1)S(1)}, u32[]{:S(2)}, u32[]{:S(2)}) collective-permute-start(bf16[36,56,128]{2,1,0:T(8,128)(2,1)S(1)} %constant_dynamic-update-slice_fusion.3.refs_11_.refs_4_), channel_id=1, source_target_pairs={{0,64},{64,0},{128,192},{192,128},{256,320},{320,256},{384,448},{4... | collective-permute-start | bytes 1548296 | tf_op jit(solution)/shard_map/ppermute | solution.py:317
  65.2 2.5 %copy-start.8 = (bf16[36,56,128]{2,1,0:T(8,128)(2,1)}, bf16[36,56,128]{2,1,0:T(8,128)(2,1)S(1)}, u32[]{:S(2)}) copy-start(bf16[36,56,128]{2,1,0:T(8,128)(2,1)S(1)} %collective-permute-done.4.refs_5_) | copy-start | bytes 1548292
  67.7 0.8 copy-start.9
  85.8 17.4 %collective-permute-start.6 = (bf16[36,56,128]{2,1,0:T(8,128)(2,1)}, bf16[36,56,128]{2,1,0:T(8,128)(2,1)S(1)}, u32[]{:S(2)}, u32[]{:S(2)}) collective-permute-start(bf16[36,56,128]{2,1,0:T(8,128)(2,1)} %get-tuple-element.34), channel_id=1, source_target_pairs={{0,448},{64,128},{128,64},{192,256},{256,192},{320,384},{384,320},... | collective-permute-start | bytes 1548296 | tf_op jit(solution)/shard_map/ppermute | solution.py:317
  90.4 15.7 %collective-permute-start.5 = (bf16[36,56,128]{2,1,0:T(8,128)(2,1)}, bf16[36,56,128]{2,1,0:T(8,128)(2,1)S(1)}, u32[]{:S(2)}, u32[]{:S(2)}) collective-permute-start(bf16[36,56,128]{2,1,0:T(8,128)(2,1)} %get-tuple-element.33.refs_14_), channel_id=1, source_target_pairs={{0,64},{64,0},{128,192},{192,128},{256,320},{320,256},{384,448},{4... | collective-permute-start | bytes 1548296 | tf_op jit(solution)/shard_map/ppermute | solution.py:317
  92.5 13.6 %copy-start.7 = (f32[36,56,128]{2,1,0:T(8,128)S(1)}, f32[36,56,128]{2,1,0:T(8,128)}, u32[]{:S(2)}) copy-start(f32[36,56,128]{2,1,0:T(8,128)} %get-tuple-element.32) | copy-start | bytes 3096580
  106.3 22.2 %copy-start.1 = (f32[32,56,128]{2,1,0:T(8,128)S(1)}, f32[32,56,128]{2,1,0:T(8,128)}, u32[]{:S(2)}) copy-start(f32[32,56,128]{2,1,0:T(8,128)} %shard_map.169.gathered) | copy-start | bytes 2752516
  106.3 10.3 %collective-permute-start.7 = (bf16[12,56,128]{2,1,0:T(8,128)(2,1)S(1)}, bf16[12,56,128]{2,1,0:T(8,128)(2,1)S(1)}, u32[]{:S(2)}, u32[]{:S(2)}) collective-permute-start(bf16[12,56,128]{2,1,0:T(8,128)(2,1)S(1)} %get-tuple-element.44), channel_id=1, source_target_pairs={{0,56},{8,16},{16,8},{24,32},{32,24},{40,48},{48,40},{56,0},{1,57}... | collective-permute-start | bytes 516104 | tf_op jit(solution)/shard_map/ppermute | solution.py:317
  116.7 7.5 %collective-permute-start.8 = (bf16[4,56,128]{2,1,0:T(8,128)(2,1)S(1)}, bf16[4,56,128]{2,1,0:T(8,128)(2,1)S(1)}, u32[]{:S(2)}, u32[]{:S(2)}) collective-permute-start(bf16[4,56,128]{2,1,0:T(8,128)(2,1)S(1)} %get-tuple-element.45), channel_id=1, source_target_pairs={{0,1},{1,0},{2,3},{3,2},{4,5},{5,4},{6,7},{7,6},{8,9},{9,8},{10,11... | collective-permute-start | bytes 172040 | tf_op jit(solution)/shard_map/ppermute | solution.py:317
  120.2 8.2 %collective-permute-start.9 = (bf16[4,56,128]{2,1,0:T(8,128)(2,1)S(1)}, bf16[4,56,128]{2,1,0:T(8,128)(2,1)S(1)}, u32[]{:S(2)}, u32[]{:S(2)}) collective-permute-start(bf16[4,56,128]{2,1,0:T(8,128)(2,1)S(1)} %get-tuple-element.46), channel_id=1, source_target_pairs={{0,7},{1,2},{2,1},{3,4},{4,3},{5,6},{6,5},{7,0},{8,15},{9,10},{10,... | collective-permute-start | bytes 172040 | tf_op jit(solution)/shard_map/ppermute | solution.py:317
Sparse Core Ops, SparseCore 0:
  22.4 55.4 all-gather.6

commit v6 on v5

--- a/solution.py
+++ b/solution.py
@@ -407,8 +407,9 @@
         return jnp.where(lax.axis_index(axis) % 2 == 1, offset, 2 - offset)
 
     slot, atom = far_rows // BOUND, far_rows % BOUND
-    far_rows = (place(GX, slot // 9) * 3 + place(GY, slot // 3 % 3)) * 3 + place(GZ, slot % 3)
-    far_rows = far_rows * BOUND + atom
+    on_x, on_y, on_z = place(GX, slot // 9), place(GY, slot // 3 % 3), place(GZ, slot % 3)
+    far_rows = ((on_x * 3 + on_y) * 3 + on_z) * BOUND + atom
+    fold_rows = ((on_x * 3 + on_z) * 3 + on_y) * BOUND + atom
 
     near = widen(GY, widen(GZ, border))
     near, table = lax.optimization_barrier((near, table))
@@ -422,7 +423,7 @@
 
     face = (36, JP, LANES)
     first, middle, last = back(
-        [count_x], [rot_outward], [far_rows], [turned_out], table, gathered_weights, turned_x[0], 112, AROUND,
+        [count_x], [rot_outward], [fold_rows], [turned_out], table, gathered_weights, turned_x[0], 112, AROUND,
         store_returned,
         (jax.ShapeDtypeStruct(face, BF16), jax.ShapeDtypeStruct(face, F32), jax.ShapeDtypeStruct(face, BF16)),
     )
@@ -432,8 +433,8 @@
     )
     returned = fold(GX, first, middle, last)
     returned, gathered = lax.optimization_barrier((returned, gathered))
+    returned = fold(GZ, *thirds(returned))
     returned = fold(GY, *thirds(returned))
-    returned = fold(GZ, *thirds(returned))
 
     updated = pl.pallas_call(
         final_kernel,

time: 137 us -> 136 us (level)
  the two profiles are of different devices: /device:TPU:24 before, /device:TPU:16 now
where the time goes in v6:
time: 136 us
  starting transfers between devices  41.3 us (30%)
  Pallas kernels  38.2 us (28%)
  blocking collectives  18.3 us (13%)
  waiting for transfers between devices  16.6 us (12%)
  between operations  15.1 us (11%)
  local copies, waits for them, and re-layouts  3.98 us (3%)
  other arithmetic  2.27 us (2%)
    ppermute x10, starting transfers between devices, swap(): lax.ppermute(block, axis, [(i, (i + (1 if (i + odd) % 2 == 0 else -1)) %...  41.3 us
    pallas_call x2, Pallas kernels, back(): pl.pallas_call(functools.partial(back_kernel, sets, trash, finish), out_s...  18.4 us
    pallas_call x2, Pallas kernels, forward(): pl.pallas_call(functools.partial(forward_kernel, sets, len(parts)), out_s...  15.2 us
    ppermute x10, waiting for transfers between devices, swap(): lax.ppermute(block, axis, [(i, (i + (1 if (i + odd) % 2 == 0 else -1)) %...  13.6 us
    all_gather x1, blocking collectives, shards(): four = lax.all_gather(share, 'x', axis=0, tiled=False)  13.2 us
    all_gather x2, blocking collectives, exchange(): both = lax.all_gather(first, 'core', axis=0, tiled=False)  5.09 us
    unnamed x29, local copies, waits for them, and re-layouts  3.18 us
    all_gather x1, waiting for transfers between devices, shards(): lax.all_gather(jnp.concatenate(pieces, axis=0), ('zh', 'zl', 'core'), axi...  3 us
  transfers between devices with their start and end apart: 11, of which 6 were waited for; matrix products, arithmetic and copies ran while one was open for 1% of the time, Pallas kernels for 20%

profile of v6, /device:TPU:16, one launch (start us, length us, event | category | flops | bytes accessed | tf_op | source)
XLA Modules:
  0.0 135.7 jit_solution(724211330360875490)
XLA Ops:
  6.5 1.6 %shard_map.166 = bf16[356,128]{1,0:T(8,128)(2,1)} custom-call(bf16[14,896]{1,0:T(8,128)(2,1)} %zero.1, bf16[12,2,768]{2,1,0:T(2,128)(2,1)} %bitcast.68, bf16[10,2,640]{2,1,0:T(2,128)(2,1)} %bitcast.69), custom_call_target="tpu_custom_call" | custom-call | tf_op jit(solution)/shard_map/pallas_call | solution.py:362
  8.1 13.2 %all-gather.4 = bf16[4,356,128]{2,1,0:T(8,128)(2,1)S(1)} all-gather(bf16[1,356,128]{2,1,0:T(8,128)(2,1)} %bitcast.67), channel_id=3, replica_groups=mesh['gx'=8,'zh'=4,'core'=2,'x'=4,'zl'=2] {'x'}, dimensions={0}, use_global_device_ids=true | all-gather | bytes 455680 | tf_op jit(solution)/shard_map/all_gather | solution.py:369
  21.5 0.8 pad_maximum_fusion
  22.3 0.7 shard_map.163
  23.0 0.8 copy-done.4
  23.8 4.3 %collective-permute-start = (bf16[4,56,128]{2,1,0:T(8,128)(2,1)S(1)}, bf16[4,56,128]{2,1,0:T(8,128)(2,1)S(1)}, u32[]{:S(2)}, u32[]{:S(2)}) collective-permute-start(bf16[4,56,128]{2,1,0:T(8,128)(2,1)S(1)} %get-tuple-element.24), channel_id=1, source_target_pairs={{0,1},{1,0},{2,3},{3,2},{4,5},{5,4},{6,7},{7,6},{8,9},{9,8},{10,11... | collective-permute-start | bytes 172040 | tf_op jit(solution)/shard_map/ppermute | solution.py:317
  28.0 4.0 %collective-permute-start.1 = (bf16[4,56,128]{2,1,0:T(8,128)(2,1)S(1)}, bf16[4,56,128]{2,1,0:T(8,128)(2,1)S(1)}, u32[]{:S(2)}, u32[]{:S(2)}) collective-permute-start(bf16[4,56,128]{2,1,0:T(8,128)(2,1)S(1)} %get-tuple-element.24), channel_id=1, source_target_pairs={{0,7},{1,2},{2,1},{3,4},{4,3},{5,6},{6,5},{7,0},{8,15},{9,10},{10,... | collective-permute-start | bytes 172040 | tf_op jit(solution)/shard_map/ppermute | solution.py:317
  32.1 0.8 shard_map.164.refs_7_.refs_6_.refs_12_
  33.0 1.3 copy-done
  34.3 1.9 %collective-permute-done.1 = bf16[4,56,128]{2,1,0:T(8,128)(2,1)S(1)} collective-permute-done((bf16[4,56,128]{2,1,0:T(8,128)(2,1)S(1)}, bf16[4,56,128]{2,1,0:T(8,128)(2,1)S(1)}, u32[]{:S(2)}, u32[]{:S(2)}) %collective-permute-start.1) | collective-permute-done | bytes 57376 | tf_op jit(solution)/shard_map/ppermute | solution.py:317
  36.2 6.3 %collective-permute-start.2 = (bf16[12,56,128]{2,1,0:T(8,128)(2,1)S(1)}, bf16[12,56,128]{2,1,0:T(8,128)(2,1)S(1)}, u32[]{:S(2)}, u32[]{:S(2)}) collective-permute-start(bf16[12,56,128]{2,1,0:T(8,128)(2,1)S(1)} %constant_dynamic-update-slice_fusion), channel_id=1, source_target_pairs={{0,56},{8,16},{16,8},{24,32},{32,24},{40,48},{48,40},{56,0},{1,57}... | collective-permute-start | bytes 516104 | tf_op jit(solution)/shard_map/ppermute | solution.py:317
  42.6 2.1 %all-gather = bf16[24,56,128]{2,1,0:T(8,128)(2,1)S(1)} all-gather(bf16[12,56,128]{2,1,0:T(8,128)(2,1)S(1)} %constant_dynamic-update-slice_fusion), channel_id=2, replica_groups=mesh['gx'=8,'zh'=4,'core'=2,'x'=4,'zl'=2] {'core'}, dimensions={0}, use_global_device_ids=true | all-gather | bytes 516096 | tf_op jit(solution)/shard_map/all_gather | solution.py:323
  44.7 2.9 %collective-permute-done.2 = bf16[12,56,128]{2,1,0:T(8,128)(2,1)S(1)} collective-permute-done((bf16[12,56,128]{2,1,0:T(8,128)(2,1)S(1)}, bf16[12,56,128]{2,1,0:T(8,128)(2,1)S(1)}, u32[]{:S(2)}, u32[]{:S(2)}) %collective-permute-start.2) | collective-permute-done | bytes 172064 | tf_op jit(solution)/shard_map/ppermute | solution.py:317
  47.7 2.5 %collective-permute-start.4 = (bf16[36,56,128]{2,1,0:T(8,128)(2,1)S(1)}, bf16[36,56,128]{2,1,0:T(8,128)(2,1)S(1)}, u32[]{:S(2)}, u32[]{:S(2)}) collective-permute-start(bf16[36,56,128]{2,1,0:T(8,128)(2,1)S(1)} %constant_dynamic-update-slice_fusion.3.refs_11_.refs_4_), channel_id=1, source_target_pairs={{0,448},{64,128},{128,64},{192,256},{256,192},{320,384},{384,320},... | collective-permute-start | bytes 1548296 | tf_op jit(solution)/shard_map/ppermute | solution.py:317
  50.2 5.5 %collective-permute-start.3 = (bf16[36,56,128]{2,1,0:T(8,128)(2,1)S(1)}, bf16[36,56,128]{2,1,0:T(8,128)(2,1)S(1)}, u32[]{:S(2)}, u32[]{:S(2)}) collective-permute-start(bf16[36,56,128]{2,1,0:T(8,128)(2,1)S(1)} %constant_dynamic-update-slice_fusion.3.refs_11_.refs_4_), channel_id=1, source_target_pairs={{0,64},{64,0},{128,192},{192,128},{256,320},{320,256},{384,448},{4... | collective-permute-start | bytes 1548296 | tf_op jit(solution)/shard_map/ppermute | solution.py:317
  57.7 0.6 multiply_add_fusion
  58.8 8.6 %shard_map.165 = (bf16[128,1024]{1,0:T(8,128)(2,1)}, bf16[2,128,1536]{2,1,0:T(8,128)(2,1)}, bf16[2,128,1280]{2,1,0:T(8,128)(2,1)}, bf16[128,1024]{1,0:T(8,128)(2...) custom-call(s32[1]{0:T(128)} %bitcast.52.refs_0_, s32[1]{0:T(128)} %bitcast.50.refs_1_, s32[128]{0:T(128)} %bitcast.72, ...), custom_call_target="tpu_custom_call" | custom-call | tf_op jit(solution)/shard_map/pallas_call | solution.py:184
  67.4 0.8 copy-done.8
  68.4 6.6 %shard_map.167 = (bf16[128,1024]{1,0:T(8,128)(2,1)}, bf16[2,128,1536]{2,1,0:T(8,128)(2,1)}, bf16[2,128,1280]{2,1,0:T(8,128)(2,1)}) custom-call(s32[1]{0:T(128)} %bitcast.53.refs_0_, s32[128]{0:T(128)} %get-tuple-element.43.refs_1_, s32[128]{0:T(128)} %get-tuple-element.51.refs_2_.refs_3_, bf16[36,56,128]{2,1,0:T(8,128)(2,1)} %copy-done.9, ...), custom_call_target="tpu_custom_call" | custom-call | tf_op jit(solution)/shard_map/pallas_call | solution.py:184
  75.0 3.0 %all-gather.7.cloned.1.call-done = bf16[22784,128]{1,0:T(8,128)(2,1)} async-done(((bf16[1424,128]{1,0:T(8,128)(2,1)}), bf16[22784,128]{1,0:T(8,128)(2,1)}) %all-gather.7.cloned.1.call-update) | async-done | bytes 5832720 | tf_op jit(solution)/shard_map/all_gather | solution.py:376
  78.0 7.8 %shard_map.168 = (bf16[36,56,128]{2,1,0:T(8,128)(2,1)}, f32[36,56,128]{2,1,0:T(8,128)}, bf16[36,56,128]{2,1,0:T(8,128)(2,1)}) custom-call(s32[1]{0:T(128)} %bitcast.54.refs_0_, s32[128]{0:T(128)} %get-tuple-element.52.refs_4_.refs_1_, s32[128]{0:T(128)} %multiply_add_fusion.1.refs_2_, bf16[128,1024]{1,0:T(8,128)(2,1)} %get-tuple-element.27.refs_3_, ...), custom_call_target="tpu_custom_call" | custom-call | tf_op jit(solution)/shard_map/pallas_call | solution.py:284
  85.8 2.4 %collective-permute-start.6 = (bf16[36,56,128]{2,1,0:T(8,128)(2,1)}, bf16[36,56,128]{2,1,0:T(8,128)(2,1)S(1)}, u32[]{:S(2)}, u32[]{:S(2)}) collective-permute-start(bf16[36,56,128]{2,1,0:T(8,128)(2,1)} %get-tuple-element.34), channel_id=1, source_target_pairs={{0,448},{64,128},{128,64},{192,256},{256,192},{320,384},{384,320},... | collective-permute-start | bytes 1548296 | tf_op jit(solution)/shard_map/ppermute | solution.py:317
  88.2 5.8 %collective-permute-start.5 = (bf16[36,56,128]{2,1,0:T(8,128)(2,1)}, bf16[36,56,128]{2,1,0:T(8,128)(2,1)S(1)}, u32[]{:S(2)}, u32[]{:S(2)}) collective-permute-start(bf16[36,56,128]{2,1,0:T(8,128)(2,1)} %get-tuple-element.33.refs_14_), channel_id=1, source_target_pairs={{0,64},{64,0},{128,192},{192,128},{256,320},{320,256},{384,448},{4... | collective-permute-start | bytes 1548296 | tf_op jit(solution)/shard_map/ppermute | solution.py:317
  94.0 10.7 %shard_map.169.gathered = f32[32,56,128]{2,1,0:T(8,128)} custom-call(s32[1]{0:T(128)} %bitcast.51.refs_0_, s32[1]{0:T(128)} %bitcast.55.refs_1_, s32[128]{0:T(128)} %bitcast.71, s32[128]{0:T(128)} %get-tuple-element.51.refs_2_.refs_3_, s32[128]{0:T(128)} %bitcast.75, s32[128]{0:T(128)} %bitcast.73, bf16[128,1024]{1,0:T(8,128)(2,1)} %get-tuple-element.30.refs_10_.refs_6_, ...), custom_call_target="tpu_custom_call" | custom-call | tf_op jit(solution)/shard_map/pallas_call | solution.py:284
  104.7 1.2 collective-permute-done.5
  106.2 3.0 %collective-permute-start.7 = (bf16[12,56,128]{2,1,0:T(8,128)(2,1)S(1)}, bf16[12,56,128]{2,1,0:T(8,128)(2,1)S(1)}, u32[]{:S(2)}, u32[]{:S(2)}) collective-permute-start(bf16[12,56,128]{2,1,0:T(8,128)(2,1)S(1)} %get-tuple-element.47), channel_id=1, source_target_pairs={{0,1},{1,0},{2,3},{3,2},{4,5},{5,4},{6,7},{7,6},{8,9},{9,8},{10,11... | collective-permute-start | bytes 516104 | tf_op jit(solution)/shard_map/ppermute | solution.py:317
  109.2 5.1 %collective-permute-start.8 = (bf16[12,56,128]{2,1,0:T(8,128)(2,1)S(1)}, bf16[12,56,128]{2,1,0:T(8,128)(2,1)S(1)}, u32[]{:S(2)}, u32[]{:S(2)}) collective-permute-start(bf16[12,56,128]{2,1,0:T(8,128)(2,1)S(1)} %get-tuple-element.48), channel_id=1, source_target_pairs={{0,7},{1,2},{2,1},{3,4},{4,3},{5,6},{6,5},{7,0},{8,15},{9,10},{10,... | collective-permute-start | bytes 516104 | tf_op jit(solution)/shard_map/ppermute | solution.py:317
  114.3 5.4 %collective-permute-done.8 = bf16[12,56,128]{2,1,0:T(8,128)(2,1)S(1)} collective-permute-done((bf16[12,56,128]{2,1,0:T(8,128)(2,1)S(1)}, bf16[12,56,128]{2,1,0:T(8,128)(2,1)S(1)}, u32[]{:S(2)}, u32[]{:S(2)}) %collective-permute-start.8) | collective-permute-done | bytes 172064 | tf_op jit(solution)/shard_map/ppermute | solution.py:317
  119.8 2.4 %collective-permute-start.9 = (bf16[4,56,128]{2,1,0:T(8,128)(2,1)S(1)}, bf16[4,56,128]{2,1,0:T(8,128)(2,1)S(1)}, u32[]{:S(2)}, u32[]{:S(2)}) collective-permute-start(bf16[4,56,128]{2,1,0:T(8,128)(2,1)S(1)} %get-tuple-element.50), channel_id=1, source_target_pairs={{0,56},{8,16},{16,8},{24,32},{32,24},{40,48},{48,40},{56,0},{1,57}... | collective-permute-start | bytes 172040 | tf_op jit(solution)/shard_map/ppermute | solution.py:317
  122.1 3.0 %all-gather.3 = bf16[8,56,128]{2,1,0:T(8,128)(2,1)S(1)} all-gather(bf16[4,56,128]{2,1,0:T(8,128)(2,1)S(1)} %get-tuple-element.49), channel_id=5, replica_groups=mesh['gx'=8,'zh'=4,'core'=2,'x'=4,'zl'=2] {'core'}, dimensions={0}, use_global_device_ids=true | all-gather | bytes 172032 | tf_op jit(solution)/shard_map/all_gather | solution.py:323
  125.2 2.2 %collective-permute-done.9 = bf16[4,56,128]{2,1,0:T(8,128)(2,1)S(1)} collective-permute-done((bf16[4,56,128]{2,1,0:T(8,128)(2,1)S(1)}, bf16[4,56,128]{2,1,0:T(8,128)(2,1)S(1)}, u32[]{:S(2)}, u32[]{:S(2)}) %collective-permute-start.9) | collective-permute-done | bytes 57376 | tf_op jit(solution)/shard_map/ppermute | solution.py:317
  127.4 1.5 %shard_map.170 = bf16[49,32,128]{2,1,0:T(8,128)(2,1)} custom-call(s32[4]{0:T(128)S(1)} %bitcast.59, bf16[49,32,128]{2,1,0:T(8,128)(2,1)S(1)} %bitcast.57, f32[32,56,128]{2,1,0:T(8,128)S(1)} %copy-done.1, f32[4,56,128]{2,1,0:T(8,128)S(1)} %fusion.1.returned), custom_call_target="tpu_custom_call" | custom-call | tf_op jit(solution)/shard_map/pallas_call | solution.py:439
  (52 shorter events, 2.0 us)
Async XLA Ops:
  6.5 15.8 %copy-start.5 = (s32[1,1,1,4]{3,2,1,0:T(1,128)S(1)}, s32[1,1,1,4]{3,2,1,0:T(1,128)}, u32[]{:S(2)}) copy-start(s32[1,1,1,4]{3,2,1,0:T(1,128)} %param.18) | copy-start | bytes 52
  6.5 15.8 %copy-start.2 = (bf16[1,1,1,32,49,128]{5,3,4,2,1,0:T(8,128)(2,1)S(1)}, bf16[1,1,1,32,49,128]{5,3,4,2,1,0:T(8,128)(2,1)}, u32[]{:S(2)}) copy-start(bf16[1,1,1,32,49,128]{5,3,4,2,1,0:T(8,128)(2,1)} %param.17) | copy-start | bytes 1204228
  6.5 71.5 %all-gather.7.cloned.1.call-start = ((), (), s32[]{:S(2)}) async-start(), calls=%async_computation | async-start | bytes 6197248 | tf_op jit(solution)/shard_map/all_gather | solution.py:376
  8.1 24.0 %copy-start.3 = (bf16[49,49,256]{2,1,0:T(8,128)(2,1)S(1)}, bf16[49,49,256]{2,1,0:T(8,128)(2,1)}, u32[]{:S(2)}) copy-start(bf16[49,49,256]{2,1,0:T(8,128)(2,1)} %rotations.1) | copy-start | bytes 3687940
  23.0 0.8 copy-start.4
  23.8 10.6 %collective-permute-start = (bf16[4,56,128]{2,1,0:T(8,128)(2,1)S(1)}, bf16[4,56,128]{2,1,0:T(8,128)(2,1)S(1)}, u32[]{:S(2)}, u32[]{:S(2)}) collective-permute-start(bf16[4,56,128]{2,1,0:T(8,128)(2,1)S(1)} %get-tuple-element.24), channel_id=1, source_target_pairs={{0,1},{1,0},{2,3},{3,2},{4,5},{5,4},{6,7},{7,6},{8,9},{9,8},{10,11... | collective-permute-start | bytes 172040 | tf_op jit(solution)/shard_map/ppermute | solution.py:317
  28.0 8.2 %collective-permute-start.1 = (bf16[4,56,128]{2,1,0:T(8,128)(2,1)S(1)}, bf16[4,56,128]{2,1,0:T(8,128)(2,1)S(1)}, u32[]{:S(2)}, u32[]{:S(2)}) collective-permute-start(bf16[4,56,128]{2,1,0:T(8,128)(2,1)S(1)} %get-tuple-element.24), channel_id=1, source_target_pairs={{0,7},{1,2},{2,1},{3,4},{4,3},{5,6},{6,5},{7,0},{8,15},{9,10},{10,... | collective-permute-start | bytes 172040 | tf_op jit(solution)/shard_map/ppermute | solution.py:317
  32.1 23.7 %copy-start.11 = (s32[1,1,1,2,128]{4,3,2,1,0:T(2,128)S(1)}, s32[1,1,1,2,128]{4,3,2,1,0:T(2,128)}, u32[]{:S(2)}) copy-start(s32[1,1,1,2,128]{4,3,2,1,0:T(2,128)} %param.25) | copy-start | bytes 3076
  32.1 25.5 %copy-start.10 = (s32[1,1,1,128]{3,2,1,0:T(1,128)S(1)}, s32[1,1,1,128]{3,2,1,0:T(1,128)}, u32[]{:S(2)}) copy-start(s32[1,1,1,128]{3,2,1,0:T(1,128)} %param.23) | copy-start | bytes 1540
  33.0 1.4 copy-start
  36.2 11.4 %collective-permute-start.2 = (bf16[12,56,128]{2,1,0:T(8,128)(2,1)S(1)}, bf16[12,56,128]{2,1,0:T(8,128)(2,1)S(1)}, u32[]{:S(2)}, u32[]{:S(2)}) collective-permute-start(bf16[12,56,128]{2,1,0:T(8,128)(2,1)S(1)} %constant_dynamic-update-slice_fusion), channel_id=1, source_target_pairs={{0,56},{8,16},{16,8},{24,32},{32,24},{40,48},{48,40},{56,0},{1,57}... | collective-permute-start | bytes 516104 | tf_op jit(solution)/shard_map/ppermute | solution.py:317
  47.7 11.1 %copy-start.6 = (bf16[36,56,128]{2,1,0:T(8,128)(2,1)}, bf16[36,56,128]{2,1,0:T(8,128)(2,1)S(1)}, u32[]{:S(2)}) copy-start(bf16[36,56,128]{2,1,0:T(8,128)(2,1)S(1)} %constant_dynamic-update-slice_fusion.3.refs_11_.refs_4_) | copy-start | bytes 1548292
  47.7 19.7 %collective-permute-start.4 = (bf16[36,56,128]{2,1,0:T(8,128)(2,1)S(1)}, bf16[36,56,128]{2,1,0:T(8,128)(2,1)S(1)}, u32[]{:S(2)}, u32[]{:S(2)}) collective-permute-start(bf16[36,56,128]{2,1,0:T(8,128)(2,1)S(1)} %constant_dynamic-update-slice_fusion.3.refs_11_.refs_4_), channel_id=1, source_target_pairs={{0,448},{64,128},{128,64},{192,256},{256,192},{320,384},{384,320},... | collective-permute-start | bytes 1548296 | tf_op jit(solution)/shard_map/ppermute | solution.py:317
  50.2 17.2 %collective-permute-start.3 = (bf16[36,56,128]{2,1,0:T(8,128)(2,1)S(1)}, bf16[36,56,128]{2,1,0:T(8,128)(2,1)S(1)}, u32[]{:S(2)}, u32[]{:S(2)}) collective-permute-start(bf16[36,56,128]{2,1,0:T(8,128)(2,1)S(1)} %constant_dynamic-update-slice_fusion.3.refs_11_.refs_4_), channel_id=1, source_target_pairs={{0,64},{64,0},{128,192},{192,128},{256,320},{320,256},{384,448},{4... | collective-permute-start | bytes 1548296 | tf_op jit(solution)/shard_map/ppermute | solution.py:317
  67.4 0.8 copy-start.8
  67.4 1.0 copy-start.9
  85.8 18.9 %collective-permute-start.6 = (bf16[36,56,128]{2,1,0:T(8,128)(2,1)}, bf16[36,56,128]{2,1,0:T(8,128)(2,1)S(1)}, u32[]{:S(2)}, u32[]{:S(2)}) collective-permute-start(bf16[36,56,128]{2,1,0:T(8,128)(2,1)} %get-tuple-element.34), channel_id=1, source_target_pairs={{0,448},{64,128},{128,64},{192,256},{256,192},{320,384},{384,320},... | collective-permute-start | bytes 1548296 | tf_op jit(solution)/shard_map/ppermute | solution.py:317
  88.2 17.7 %collective-permute-start.5 = (bf16[36,56,128]{2,1,0:T(8,128)(2,1)}, bf16[36,56,128]{2,1,0:T(8,128)(2,1)S(1)}, u32[]{:S(2)}, u32[]{:S(2)}) collective-permute-start(bf16[36,56,128]{2,1,0:T(8,128)(2,1)} %get-tuple-element.33.refs_14_), channel_id=1, source_target_pairs={{0,64},{64,0},{128,192},{192,128},{256,320},{320,256},{384,448},{4... | collective-permute-start | bytes 1548296 | tf_op jit(solution)/shard_map/ppermute | solution.py:317
  94.0 11.9 %copy-start.7 = (f32[36,56,128]{2,1,0:T(8,128)S(1)}, f32[36,56,128]{2,1,0:T(8,128)}, u32[]{:S(2)}) copy-start(f32[36,56,128]{2,1,0:T(8,128)} %get-tuple-element.32) | copy-start | bytes 3096580
  106.0 21.4 %copy-start.1 = (f32[32,56,128]{2,1,0:T(8,128)S(1)}, f32[32,56,128]{2,1,0:T(8,128)}, u32[]{:S(2)}) copy-start(f32[32,56,128]{2,1,0:T(8,128)} %shard_map.169.gathered) | copy-start | bytes 2752516
  106.2 8.1 %collective-permute-start.7 = (bf16[12,56,128]{2,1,0:T(8,128)(2,1)S(1)}, bf16[12,56,128]{2,1,0:T(8,128)(2,1)S(1)}, u32[]{:S(2)}, u32[]{:S(2)}) collective-permute-start(bf16[12,56,128]{2,1,0:T(8,128)(2,1)S(1)} %get-tuple-element.47), channel_id=1, source_target_pairs={{0,1},{1,0},{2,3},{3,2},{4,5},{5,4},{6,7},{7,6},{8,9},{9,8},{10,11... | collective-permute-start | bytes 516104 | tf_op jit(solution)/shard_map/ppermute | solution.py:317
  109.2 10.5 %collective-permute-start.8 = (bf16[12,56,128]{2,1,0:T(8,128)(2,1)S(1)}, bf16[12,56,128]{2,1,0:T(8,128)(2,1)S(1)}, u32[]{:S(2)}, u32[]{:S(2)}) collective-permute-start(bf16[12,56,128]{2,1,0:T(8,128)(2,1)S(1)} %get-tuple-element.48), channel_id=1, source_target_pairs={{0,7},{1,2},{2,1},{3,4},{4,3},{5,6},{6,5},{7,0},{8,15},{9,10},{10,... | collective-permute-start | bytes 516104 | tf_op jit(solution)/shard_map/ppermute | solution.py:317
  119.8 7.6 %collective-permute-start.9 = (bf16[4,56,128]{2,1,0:T(8,128)(2,1)S(1)}, bf16[4,56,128]{2,1,0:T(8,128)(2,1)S(1)}, u32[]{:S(2)}, u32[]{:S(2)}) collective-permute-start(bf16[4,56,128]{2,1,0:T(8,128)(2,1)S(1)} %get-tuple-element.50), channel_id=1, source_target_pairs={{0,56},{8,16},{16,8},{24,32},{32,24},{40,48},{48,40},{56,0},{1,57}... | collective-permute-start | bytes 172040 | tf_op jit(solution)/shard_map/ppermute | solution.py:317
Sparse Core Ops, SparseCore 0:
  22.4 55.5 all-gather.6
